TPU v7x, 128 devices: a whole 4x4x4 slice. The times are simulated.
128 devices in a mesh: tm: 8 (over z, core), space: 16 (over x, y).
Axes of the slice: x: 4, y: 4, z: 4, core: 2. Of those that a mesh axis runs over, the one named last changes fastest.
Arguments:
- video_tokens: bfloat16 [128, 256, 1408], P(('tm', 'space')), may hold values from -8 to 8
- grad_rows: bfloat16 [8, 16, 8, 64, 1408], P('tm', 'space'), may hold values from -6 to 6
- targets: int32 [8, 16, 8, 64], P('tm', 'space'), may hold values from 0 to 255, as said below
- counts: int32 [8, 16, 8], P('tm', 'space'), may hold values from 0 to 64, as said below
- attend_space: bfloat16 [1408, 2112], replicated, may hold values from -1 to 1
- output_space: bfloat16 [1408, 704], replicated, may hold values from -0.21875 to 0.21875
- attend_time: bfloat16 [1408, 2112], replicated, may hold values from -1 to 1
- output_time: bfloat16 [1408, 704], replicated, may hold values from -0.21875 to 0.21875
Outputs:
- token_grad: bfloat16 [128, 256, 1408], P(('tm', 'space'))
- space_grad: float32 [1408, 704], P(('tm', 'space'))
- time_grad: float32 [1408, 704], P(('tm', 'space'))
Inputs may be any that keep to these rules, and one draw needn't show every extreme that they name: For every receiver (r, s) the counts counts[o, s, r] over the owners o add up to 256, and exactly one owner sends 64 rows to it. Over the slots j < counts[o, s, r] of all owners o, targets[o, s, r, j] names each of receiver (r, s)'s 256 tokens exactly once; other slots hold arbitrary indices and are ignored.
All inputs are finite; a program needn't handle non-finite values.
Results may differ from a plain program's by a relative error of at most 0.018.
The roundings to bfloat16 on the way count: a program that leaves them out, or rounds other values in their place, can miss the bound.
Values may be sent and summed in bfloat16 or wider, within the bound.
No kernel may reach another device: no remote copies, remote signals or barrier semaphores. Data moves between devices by JAX's collectives and lax.ppermute only.
A program may use at most 128 MiB of HBM per device.

v0:
```python
import jax
import jax.numpy as jnp
from jax import lax
from jax.sharding import PartitionSpec as P

HEADS = 8
HEAD = 88
FRAMES = 32


def as_sent(array):

    def short(part):
        return part.astype(jnp.bfloat16) if part.dtype == jnp.float32 else part

    return jax.tree.map(short, array)


def sublayer(stream, attend, output):
    widened = stream.astype(jnp.float32)
    center = jnp.mean(widened, axis=-1, keepdims=True)
    centered = widened - center
    variance = jnp.mean(centered * centered, axis=-1, keepdims=True)
    normed = (centered * lax.rsqrt(variance + 1e-05)).astype(jnp.bfloat16)
    projected = jnp.dot(normed, attend, preferred_element_type=jnp.float32).astype(jnp.bfloat16)
    projected = projected.reshape(stream.shape[:-1] + (3, HEADS, HEAD))
    query_rows = projected[..., 0, :, :]
    key_rows = projected[..., 1, :, :]
    value_rows = projected[..., 2, :, :]
    scores = jnp.einsum(
        "blmhe,bkmhe->bmhlk", query_rows, key_rows, preferred_element_type=jnp.float32
    ) * HEAD ** (-0.5)
    row_max = jnp.max(scores, axis=-1, keepdims=True)
    weights = jnp.exp(scores - row_max)
    attn_probs = (weights / jnp.sum(weights, axis=-1, keepdims=True)).astype(jnp.bfloat16)
    mixed = jnp.einsum(
        "bmhlk,bkmhe->blmhe", attn_probs, value_rows, preferred_element_type=jnp.float32
    )
    mixed = mixed.astype(jnp.bfloat16).reshape(stream.shape[:-1] + (HEADS * HEAD,))
    branch = lax.dot_general(
        mixed, output, (((mixed.ndim - 1,), (1,)), ((), ())), preferred_element_type=jnp.float32
    )
    return ((widened + branch).astype(jnp.bfloat16), mixed)


def weight_term(cotangent, mixed, count):
    sliced = lax.slice_in_dim(cotangent, 0, count, axis=1)
    return lax.dot_general(
        sliced, mixed, (((0,), (0,)), ((), ())), preferred_element_type=jnp.float32
    )


def body(
    video_tokens, grad_rows, targets, counts, attend_space, output_space, attend_time, output_time
):
    time_devices = lax.axis_size("tm")
    space_devices = lax.axis_size("space")
    frames_dev, patches, model_width = video_tokens.shape
    token_count = frames_dev * patches
    capacity = grad_rows.shape[3]
    dest_rows = grad_rows.reshape(time_devices, capacity, model_width)
    dest_targets = targets.reshape(time_devices, capacity)
    dest_counts = counts.reshape(time_devices)
    slot_index = lax.broadcasted_iota(jnp.int32, (time_devices, token_count, capacity), 2)
    token_index = lax.broadcasted_iota(jnp.int32, (time_devices, token_count, capacity), 1)
    matches = (dest_targets[:, None, :] == token_index) & (slot_index < dest_counts[:, None, None])
    scattered = jnp.einsum(
        "ntc,ncd->ntd", matches.astype(jnp.bfloat16), dest_rows, preferred_element_type=jnp.float32
    )
    summed = lax.psum_scatter(scattered.astype(jnp.bfloat16), "tm", scatter_dimension=0, tiled=True)

    def space_layer(stream):
        return sublayer(stream, attend_space, output_space)

    def time_layer(stream):
        return sublayer(stream, attend_time, output_time)

    hidden_four, space_pull, space_mixed = jax.vjp(
        space_layer, video_tokens[:, :, None, :], has_aux=True
    )
    hidden = hidden_four[:, :, 0, :]
    patch_hidden, patch_grad = (
        lax.all_to_all(
            as_sent(hidden), ("tm", "space"), split_axis=1, concat_axis=0, tiled=True
        ).astype(hidden.dtype),
        lax.all_to_all(summed, ("tm", "space"), split_axis=1, concat_axis=0, tiled=True),
    )
    clip_count = patch_hidden.shape[0] // FRAMES
    narrow = patch_hidden.shape[1]
    time_input = patch_hidden.reshape(clip_count, FRAMES, narrow, model_width)
    time_cotangent = patch_grad.reshape(clip_count, FRAMES, narrow, model_width)
    layer_out, time_pull, time_mixed = jax.vjp(time_layer, time_input, has_aux=True)
    grad_time_input = time_pull(time_cotangent)[0].reshape(clip_count * FRAMES, narrow, model_width)
    share_rows = model_width // (time_devices * space_devices)
    time_grad = lax.psum_scatter(
        weight_term(
            time_cotangent.reshape(-1, model_width),
            time_mixed.reshape(-1, HEADS * HEAD),
            lax.axis_size(("tm", "space")) * share_rows,
        ),
        ("tm", "space"),
        scatter_dimension=0,
        tiled=True,
    )
    grad_hidden = lax.all_to_all(
        as_sent(grad_time_input), ("tm", "space"), split_axis=0, concat_axis=1, tiled=True
    ).astype(grad_time_input.dtype)
    token_grad = space_pull(grad_hidden[:, :, None, :])[0][:, :, 0, :]
    space_grad = lax.psum_scatter(
        weight_term(
            grad_hidden.reshape(-1, model_width),
            space_mixed.reshape(-1, HEADS * HEAD),
            lax.axis_size(("tm", "space")) * share_rows,
        ),
        ("tm", "space"),
        scatter_dimension=0,
        tiled=True,
    )
    return (token_grad, space_grad, time_grad)


def solution(mesh):
    in_specs = (
        P(("tm", "space"), None, None),
        P("tm", "space", None, None, None),
        P("tm", "space", None, None),
        P("tm", "space", None),
        P(),
        P(),
        P(),
        P(),
    )
    out_specs = (P(("tm", "space"), None, None), P(("tm", "space"), None), P(("tm", "space"), None))
    return jax.shard_map(body, mesh=mesh, in_specs=in_specs, out_specs=out_specs, check_vma=False)
```

profile of v0, /device:TPU:0, one launch (start us, length us, event | category | flops | bytes accessed | tf_op | source)
XLA Modules:
  0.0 971.3 jit_solution(13971785510638857648)
XLA Ops:
  7.2 5.7 convolution_convert_fusion
  15.2 4.7 convolution_convert_fusion.1
  28.6 6.0 reduce.25
  35.8 26.8 %all_to_all.12 = bf16[128,2,1408]{2,1,0:T(2,128)(2,1)S(1)} all-to-all(bf16[128,2,1408]{2,1,0:T(2,128)(2,1)} %reshape.401), channel_id=1, replica_groups=mesh['tm'=8,'space'=16] {'tm','space'}, dimensions={0} | all-to-all | bytes 1441792 | tf_op jit(solution)/shard_map/all_to_all | solution.py:83
  67.8 7.8 fusion.37
  78.9 6.2 fusion.6
  85.2 16.4 %reshape.387 = bf16[4,32,2,3,8,88]{5,4,3,1,2,0:T(8,128)(2,1)} reshape(bf16[4,32,2,2112]{3,1,2,0:T(8,128)(2,1)} %fusion.6) | data formatting | bytes 2162688 | tf_op jit(solution)/shard_map/jvp()/reshape | solution.py:26
  105.0 6.0 reduce.26
  120.8 11.6 %all-to-all-done = bf16[128,2,1408]{2,1,0:T(2,128)(2,1)S(1)} async-done(((bf16[128,2,1408]{2,1,0:T(2,128)(2,1)}), bf16[128,2,1408]{2,1,0:T(2,128)(2,1)S(1)}, u32[]{:S(2)}, u32[]{:S(2)}) %all-to-all-start) | async-done | bytes 720928 | tf_op jit(solution)/shard_map/all_to_all | solution.py:86
  134.3 5.6 bitcast_reduce_fusion
  157.3 5.6 multiply_reduce_fusion.1
  166.3 5.7 all-to-all-start.2
  179.2 8.0 all-to-all-done.2
  193.3 371.3 %fusion.103 = (f32[16,704]{1,0:T(8,128)S(1)}, f32[16,704]{1,0:T(8,128)S(1)}) fusion(f32[1408,704]{1,0:T(8,128)} %fusion.108, f32[1408,704]{1,0:T(8,128)} %fusion.63), kind=kCustom, calls=%all-reduce-scatter.2 | all-reduce-scatter fusion | flops 2883585 | bytes 8019968
  568.5 9.6 collective-permute-start.39
  578.2 10.2 %collective-permute-start.79 = (f32[11,704]{1,0:T(8,128)S(1)}, f32[11,704]{1,0:T(8,128)S(1)}, u32[]{:S(2)}, u32[]{:S(2)}) collective-permute-start(f32[11,704]{1,0:T(8,128)S(1)} %slice.31), channel_id=1, source_target_pairs={{0,40},{1,41},{2,42},{3,43},{4,44},{5,45},{6,46},{7,47},{8,48},{9,... | collective-permute-start | bytes 92936
  593.1 6.6 collective-permute-start.34
  609.4 5.6 collective-permute-start.30
  646.9 5.7 collective-permute-start.14
  683.2 6.2 collective-permute-start.2
  689.4 10.2 %collective-permute-start.1 = (f32[16,704]{1,0:T(8,128)S(1)}, f32[16,704]{1,0:T(8,128)S(1)}, u32[]{:S(2)}, u32[]{:S(2)}) collective-permute-start(f32[16,704]{1,0:T(8,128)S(1)} %get-tuple-element.7), channel_id=1, source_target_pairs={{0,2},{1,3},{2,4},{3,5},{4,6},{5,7},{6,8},{7,9},{8,10},{9,11},{10,... | collective-permute-start | bytes 135176
  700.2 10.2 %collective-permute-start = (f32[16,704]{1,0:T(8,128)S(1)}, f32[16,704]{1,0:T(8,128)S(1)}, u32[]{:S(2)}, u32[]{:S(2)}) collective-permute-start(f32[16,704]{1,0:T(8,128)S(1)} %get-tuple-element.7), channel_id=1, source_target_pairs={{0,1},{1,2},{2,3},{3,4},{4,5},{5,6},{6,7},{7,8},{8,9},{9,10},{10,1... | collective-permute-start | bytes 135176
  710.5 6.3 collective-permute-start.78
  716.8 5.3 collective-permute-start.77
  735.9 5.7 collective-permute-start.70
  775.7 5.1 collective-permute-start.54
  789.9 5.7 collective-permute-start.49
  809.3 60.6 %concatenate = f32[651,704]{1,0:T(8,128)} concatenate(f32[11,704]{1,0:T(8,128)} %copy-done.24, f32[16,704]{1,0:T(8,128)} %copy-done.21, f32[16,704]{1,0:T(8,128)} %copy-done.22, f32[16,704]{1,0:T(8,128)} %copy-done.23, f32[16,704]{1,0:T(8,128)} %collective-permute-done.35, f32[16,704]{1,0:T(8,128)} %collective-permute-done.34, f32[16,704]{1,0:T(8,128)} %collective-permute-done.33, ...), dimensions={0} | concatenate | bytes 3666432
  873.4 6.8 collective-permute-start.42
  880.2 10.2 %collective-permute-start.41 = (f32[16,704]{1,0:T(8,128)S(1)}, f32[16,704]{1,0:T(8,128)S(1)}, u32[]{:S(2)}, u32[]{:S(2)}) collective-permute-start(f32[16,704]{1,0:T(8,128)S(1)} %get-tuple-element.8), channel_id=1, source_target_pairs={{0,2},{1,3},{2,4},{3,5},{4,6},{5,7},{6,8},{7,9},{8,10},{9,11},{10,... | collective-permute-start | bytes 135176
  890.4 10.8 %collective-permute-start.40 = (f32[16,704]{1,0:T(8,128)S(1)}, f32[16,704]{1,0:T(8,128)}, u32[]{:S(2)}, u32[]{:S(2)}) collective-permute-start(f32[16,704]{1,0:T(8,128)S(1)} %get-tuple-element.8), channel_id=1, source_target_pairs={{0,1},{1,2},{2,3},{3,4},{4,5},{5,6},{6,7},{7,8},{8,9},{9,10},{10,1... | collective-permute-start | bytes 135176
  904.2 58.5 %concatenate.1 = f32[651,704]{1,0:T(8,128)} concatenate(f32[11,704]{1,0:T(8,128)S(1)} %copy-done.20, f32[16,704]{1,0:T(8,128)S(1)} %copy-done.50, f32[16,704]{1,0:T(8,128)S(1)} %copy-done.53, f32[16,704]{1,0:T(8,128)S(1)} %copy-done.55, f32[16,704]{1,0:T(8,128)S(1)} %copy-done.58, f32[16,704]{1,0:T(8,128)S(1)} %copy-done.62, f32[16,704]{1,0:T(8,128)S(1)} %copy-done.65, ...), dimensions={0} | concatenate | bytes 3666432
  (469 shorter events, 227.3 us)
Async XLA Ops:
  7.2 94.4 %reduce-scatter.6.cloned.1.call-start = ((), (), s32[]{:S(2)}) async-start(), calls=%async_computation.4 | async-start | bytes 6488064 | tf_op jit(solution)/shard_map/reduce_scatter | solution.py:70
  112.1 20.3 %all-to-all-start = ((bf16[128,2,1408]{2,1,0:T(2,128)(2,1)}), bf16[128,2,1408]{2,1,0:T(2,128)(2,1)S(1)}, u32[]{:S(2)}, u32[]{:S(2)}) async-start(bf16[128,2,1408]{2,1,0:T(2,128)(2,1)} %reshape.403), calls=%async_computation.1 | async-start | bytes 1441792 | tf_op jit(solution)/shard_map/all_to_all | solution.py:86
  166.3 21.0 %all-to-all-start.2 = ((bf16[128,2,1408]{2,1,0:T(2,128)(2,1)}), bf16[128,2,1408]{2,1,0:T(2,128)(2,1)}, u32[]{:S(2)}, u32[]{:S(2)}) async-start(bf16[128,2,1408]{2,1,0:T(2,128)(2,1)} %copy.107), calls=%async_computation.3 | async-start | bytes 1441792 | tf_op jit(solution)/shard_map/all_to_all | solution.py:105
  564.6 35.0 %collective-permute-start.38 = (f32[16,704]{1,0:T(8,128)S(1)}, f32[16,704]{1,0:T(8,128)S(1)}, u32[]{:S(2)}, u32[]{:S(2)}) collective-permute-start(f32[16,704]{1,0:T(8,128)S(1)} %get-tuple-element.7), channel_id=1, source_target_pairs={{0,39},{1,40},{2,41},{3,42},{4,43},{5,44},{6,45},{7,46},{8,47},{9,... | collective-permute-start | bytes 135176
  565.9 37.5 %collective-permute-start.37 = (f32[16,704]{1,0:T(8,128)S(1)}, f32[16,704]{1,0:T(8,128)S(1)}, u32[]{:S(2)}, u32[]{:S(2)}) collective-permute-start(f32[16,704]{1,0:T(8,128)S(1)} %get-tuple-element.7), channel_id=1, source_target_pairs={{0,38},{1,39},{2,40},{3,41},{4,42},{5,43},{6,44},{7,45},{8,46},{9,... | collective-permute-start | bytes 135176
  567.2 40.2 %collective-permute-start.36 = (f32[16,704]{1,0:T(8,128)S(1)}, f32[16,704]{1,0:T(8,128)S(1)}, u32[]{:S(2)}, u32[]{:S(2)}) collective-permute-start(f32[16,704]{1,0:T(8,128)S(1)} %get-tuple-element.7), channel_id=1, source_target_pairs={{0,37},{1,38},{2,39},{3,40},{4,41},{5,42},{6,43},{7,44},{8,45},{9,... | collective-permute-start | bytes 135176
  568.5 19.9 %collective-permute-start.39 = (f32[11,704]{1,0:T(8,128)S(1)}, f32[11,704]{1,0:T(8,128)S(1)}, u32[]{:S(2)}, u32[]{:S(2)}) collective-permute-start(f32[11,704]{1,0:T(8,128)S(1)} %slice.30), channel_id=1, source_target_pairs={{0,40},{1,41},{2,42},{3,43},{4,44},{5,45},{6,46},{7,47},{8,48},{9,... | collective-permute-start | bytes 92936
  588.4 21.0 %collective-permute-start.35 = (f32[16,704]{1,0:T(8,128)S(1)}, f32[16,704]{1,0:T(8,128)}, u32[]{:S(2)}, u32[]{:S(2)}) collective-permute-start(f32[16,704]{1,0:T(8,128)S(1)} %get-tuple-element.7), channel_id=1, source_target_pairs={{0,36},{1,37},{2,38},{3,39},{4,40},{5,41},{6,42},{7,43},{8,44},{9,... | collective-permute-start | bytes 135176
  593.1 22.0 %collective-permute-start.34 = (f32[16,704]{1,0:T(8,128)S(1)}, f32[16,704]{1,0:T(8,128)}, u32[]{:S(2)}, u32[]{:S(2)}) collective-permute-start(f32[16,704]{1,0:T(8,128)S(1)} %get-tuple-element.7), channel_id=1, source_target_pairs={{0,35},{1,36},{2,37},{3,38},{4,39},{5,40},{6,41},{7,42},{8,43},{9,... | collective-permute-start | bytes 135176
  599.6 17.0 %collective-permute-start.33 = (f32[16,704]{1,0:T(8,128)S(1)}, f32[16,704]{1,0:T(8,128)}, u32[]{:S(2)}, u32[]{:S(2)}) collective-permute-start(f32[16,704]{1,0:T(8,128)S(1)} %get-tuple-element.7), channel_id=1, source_target_pairs={{0,34},{1,35},{2,36},{3,37},{4,38},{5,39},{6,40},{7,41},{8,42},{9,... | collective-permute-start | bytes 135176
  657.8 16.8 %collective-permute-start.10 = (f32[16,704]{1,0:T(8,128)S(1)}, f32[16,704]{1,0:T(8,128)S(1)}, u32[]{:S(2)}, u32[]{:S(2)}) collective-permute-start(f32[16,704]{1,0:T(8,128)S(1)} %get-tuple-element.7), channel_id=1, source_target_pairs={{0,11},{1,12},{2,13},{3,14},{4,15},{5,16},{6,17},{7,18},{8,19},{9,... | collective-permute-start | bytes 135176
  661.8 17.3 %collective-permute-start.9 = (f32[16,704]{1,0:T(8,128)S(1)}, f32[16,704]{1,0:T(8,128)S(1)}, u32[]{:S(2)}, u32[]{:S(2)}) collective-permute-start(f32[16,704]{1,0:T(8,128)S(1)} %get-tuple-element.7), channel_id=1, source_target_pairs={{0,10},{1,11},{2,12},{3,13},{4,14},{5,15},{6,16},{7,17},{8,18},{9,... | collective-permute-start | bytes 135176
  670.7 18.7 %collective-permute-start.6 = (f32[16,704]{1,0:T(8,128)S(1)}, f32[16,704]{1,0:T(8,128)S(1)}, u32[]{:S(2)}, u32[]{:S(2)}) collective-permute-start(f32[16,704]{1,0:T(8,128)S(1)} %get-tuple-element.7), channel_id=1, source_target_pairs={{0,7},{1,8},{2,9},{3,10},{4,11},{5,12},{6,13},{7,14},{8,15},{9,16}... | collective-permute-start | bytes 135176
  674.6 25.6 %collective-permute-start.5 = (f32[16,704]{1,0:T(8,128)S(1)}, f32[16,704]{1,0:T(8,128)S(1)}, u32[]{:S(2)}, u32[]{:S(2)}) collective-permute-start(f32[16,704]{1,0:T(8,128)S(1)} %get-tuple-element.7), channel_id=1, source_target_pairs={{0,6},{1,7},{2,8},{3,9},{4,10},{5,11},{6,12},{7,13},{8,14},{9,15},... | collective-permute-start | bytes 135176
  679.1 31.3 %collective-permute-start.4 = (f32[16,704]{1,0:T(8,128)S(1)}, f32[16,704]{1,0:T(8,128)S(1)}, u32[]{:S(2)}, u32[]{:S(2)}) collective-permute-start(f32[16,704]{1,0:T(8,128)S(1)} %get-tuple-element.7), channel_id=1, source_target_pairs={{0,5},{1,6},{2,7},{3,8},{4,9},{5,10},{6,11},{7,12},{8,13},{9,14},{... | collective-permute-start | bytes 135176
  680.4 36.4 %collective-permute-start.3 = (f32[16,704]{1,0:T(8,128)S(1)}, f32[16,704]{1,0:T(8,128)S(1)}, u32[]{:S(2)}, u32[]{:S(2)}) collective-permute-start(f32[16,704]{1,0:T(8,128)S(1)} %get-tuple-element.7), channel_id=1, source_target_pairs={{0,4},{1,5},{2,6},{3,7},{4,8},{5,9},{6,10},{7,11},{8,12},{9,13},{1... | collective-permute-start | bytes 135176
  683.2 39.0 %collective-permute-start.2 = (f32[16,704]{1,0:T(8,128)S(1)}, f32[16,704]{1,0:T(8,128)S(1)}, u32[]{:S(2)}, u32[]{:S(2)}) collective-permute-start(f32[16,704]{1,0:T(8,128)S(1)} %get-tuple-element.7), channel_id=1, source_target_pairs={{0,3},{1,4},{2,5},{3,6},{4,7},{5,8},{6,9},{7,10},{8,11},{9,12},{10... | collective-permute-start | bytes 135176
  689.4 35.6 %collective-permute-start.1 = (f32[16,704]{1,0:T(8,128)S(1)}, f32[16,704]{1,0:T(8,128)S(1)}, u32[]{:S(2)}, u32[]{:S(2)}) collective-permute-start(f32[16,704]{1,0:T(8,128)S(1)} %get-tuple-element.7), channel_id=1, source_target_pairs={{0,2},{1,3},{2,4},{3,5},{4,6},{5,7},{6,8},{7,9},{8,10},{9,11},{10,... | collective-permute-start | bytes 135176
  700.2 27.3 %collective-permute-start = (f32[16,704]{1,0:T(8,128)S(1)}, f32[16,704]{1,0:T(8,128)S(1)}, u32[]{:S(2)}, u32[]{:S(2)}) collective-permute-start(f32[16,704]{1,0:T(8,128)S(1)} %get-tuple-element.7), channel_id=1, source_target_pairs={{0,1},{1,2},{2,3},{3,4},{4,5},{5,6},{6,7},{7,8},{8,9},{9,10},{10,1... | collective-permute-start | bytes 135176
  710.5 21.4 %collective-permute-start.78 = (f32[16,704]{1,0:T(8,128)S(1)}, f32[16,704]{1,0:T(8,128)S(1)}, u32[]{:S(2)}, u32[]{:S(2)}) collective-permute-start(f32[16,704]{1,0:T(8,128)S(1)} %get-tuple-element.8), channel_id=1, source_target_pairs={{0,39},{1,40},{2,41},{3,42},{4,43},{5,44},{6,45},{7,46},{8,47},{9,... | collective-permute-start | bytes 135176
  716.8 16.3 %collective-permute-start.77 = (f32[16,704]{1,0:T(8,128)S(1)}, f32[16,704]{1,0:T(8,128)S(1)}, u32[]{:S(2)}, u32[]{:S(2)}) collective-permute-start(f32[16,704]{1,0:T(8,128)S(1)} %get-tuple-element.8), channel_id=1, source_target_pairs={{0,38},{1,39},{2,40},{3,41},{4,42},{5,43},{6,44},{7,45},{8,46},{9,... | collective-permute-start | bytes 135176
  782.2 16.5 %collective-permute-start.52 = (f32[16,704]{1,0:T(8,128)S(1)}, f32[16,704]{1,0:T(8,128)S(1)}, u32[]{:S(2)}, u32[]{:S(2)}) collective-permute-start(f32[16,704]{1,0:T(8,128)S(1)} %get-tuple-element.8), channel_id=1, source_target_pairs={{0,13},{1,14},{2,15},{3,16},{4,17},{5,18},{6,19},{7,20},{8,21},{9,... | collective-permute-start | bytes 135176
  786.3 17.8 %collective-permute-start.50 = (f32[16,704]{1,0:T(8,128)S(1)}, f32[16,704]{1,0:T(8,128)S(1)}, u32[]{:S(2)}, u32[]{:S(2)}) collective-permute-start(f32[16,704]{1,0:T(8,128)S(1)} %get-tuple-element.8), channel_id=1, source_target_pairs={{0,11},{1,12},{2,13},{3,14},{4,15},{5,16},{6,17},{7,18},{8,19},{9,... | collective-permute-start | bytes 135176
  789.9 80.0 %collective-permute-start.49 = (f32[16,704]{1,0:T(8,128)S(1)}, f32[16,704]{1,0:T(8,128)}, u32[]{:S(2)}, u32[]{:S(2)}) collective-permute-start(f32[16,704]{1,0:T(8,128)S(1)} %get-tuple-element.8), channel_id=1, source_target_pairs={{0,10},{1,11},{2,12},{3,13},{4,14},{5,15},{6,16},{7,17},{8,18},{9,... | collective-permute-start | bytes 135176
  795.5 75.6 %collective-permute-start.48 = (f32[16,704]{1,0:T(8,128)S(1)}, f32[16,704]{1,0:T(8,128)}, u32[]{:S(2)}, u32[]{:S(2)}) collective-permute-start(f32[16,704]{1,0:T(8,128)S(1)} %get-tuple-element.8), channel_id=1, source_target_pairs={{0,9},{1,10},{2,11},{3,12},{4,13},{5,14},{6,15},{7,16},{8,17},{9,1... | collective-permute-start | bytes 135176
  798.7 74.7 %collective-permute-start.47 = (f32[16,704]{1,0:T(8,128)S(1)}, f32[16,704]{1,0:T(8,128)}, u32[]{:S(2)}, u32[]{:S(2)}) collective-permute-start(f32[16,704]{1,0:T(8,128)S(1)} %get-tuple-element.8), channel_id=1, source_target_pairs={{0,8},{1,9},{2,10},{3,11},{4,12},{5,13},{6,14},{7,15},{8,16},{9,17... | collective-permute-start | bytes 135176
  800.6 79.6 %collective-permute-start.46 = (f32[16,704]{1,0:T(8,128)S(1)}, f32[16,704]{1,0:T(8,128)}, u32[]{:S(2)}, u32[]{:S(2)}) collective-permute-start(f32[16,704]{1,0:T(8,128)S(1)} %get-tuple-element.8), channel_id=1, source_target_pairs={{0,7},{1,8},{2,9},{3,10},{4,11},{5,12},{6,13},{7,14},{8,15},{9,16}... | collective-permute-start | bytes 135176
  804.0 86.3 %collective-permute-start.45 = (f32[16,704]{1,0:T(8,128)S(1)}, f32[16,704]{1,0:T(8,128)}, u32[]{:S(2)}, u32[]{:S(2)}) collective-permute-start(f32[16,704]{1,0:T(8,128)S(1)} %get-tuple-element.8), channel_id=1, source_target_pairs={{0,6},{1,7},{2,8},{3,9},{4,10},{5,11},{6,12},{7,13},{8,14},{9,15},... | collective-permute-start | bytes 135176
  869.8 32.8 %collective-permute-start.44 = (f32[16,704]{1,0:T(8,128)S(1)}, f32[16,704]{1,0:T(8,128)S(1)}, u32[]{:S(2)}, u32[]{:S(2)}) collective-permute-start(f32[16,704]{1,0:T(8,128)S(1)} %get-tuple-element.8), channel_id=1, source_target_pairs={{0,5},{1,6},{2,7},{3,8},{4,9},{5,10},{6,11},{7,12},{8,13},{9,14},{... | collective-permute-start | bytes 135176
  871.1 31.5 %collective-permute-start.43 = (f32[16,704]{1,0:T(8,128)S(1)}, f32[16,704]{1,0:T(8,128)S(1)}, u32[]{:S(2)}, u32[]{:S(2)}) collective-permute-start(f32[16,704]{1,0:T(8,128)S(1)} %get-tuple-element.8), channel_id=1, source_target_pairs={{0,4},{1,5},{2,6},{3,7},{4,8},{5,9},{6,10},{7,11},{8,12},{9,13},{1... | collective-permute-start | bytes 135176
  873.4 29.3 %collective-permute-start.42 = (f32[16,704]{1,0:T(8,128)S(1)}, f32[16,704]{1,0:T(8,128)S(1)}, u32[]{:S(2)}, u32[]{:S(2)}) collective-permute-start(f32[16,704]{1,0:T(8,128)S(1)} %get-tuple-element.8), channel_id=1, source_target_pairs={{0,3},{1,4},{2,5},{3,6},{4,7},{5,8},{6,9},{7,10},{8,11},{9,12},{10... | collective-permute-start | bytes 135176
  880.2 22.5 %collective-permute-start.41 = (f32[16,704]{1,0:T(8,128)S(1)}, f32[16,704]{1,0:T(8,128)S(1)}, u32[]{:S(2)}, u32[]{:S(2)}) collective-permute-start(f32[16,704]{1,0:T(8,128)S(1)} %get-tuple-element.8), channel_id=1, source_target_pairs={{0,2},{1,3},{2,4},{3,5},{4,6},{5,7},{6,8},{7,9},{8,10},{9,11},{10,... | collective-permute-start | bytes 135176
  (173 other events, 4928.0 us)
Sparse Core Ops, SparseCore 0:
  13.1 51.3 reduce-scatter.5
where the time goes:
time: 986 us; the launch traced here: 971 us
  blocking collectives  398 us (40%)
  starting transfers between devices  275 us (28%)
  local copies, waits for them, and re-layouts  183 us (19%)
  matrix products  46.1 us (5%)
  other arithmetic  31.2 us (3%)
  waiting for transfers between devices  19.9 us (2%)
  between operations  17.3 us (2%)
    unnamed x1, blocking collectives  371 us
    unnamed x80, starting transfers between devices  265 us
    unnamed x255, local copies, waits for them, and re-layouts  136 us
    all_to_all x1, blocking collectives, body(): lax.all_to_all(as_sent(hidden), ('tm', 'space'), split_axis=1, concat_axi...  26.8 us
    reshape x2, local copies, waits for them, and re-layouts, sublayer(): projected = projected.reshape(stream.shape[:-1] + (3, HEADS, HEAD))  20.5 us
  transfers between devices with their start and end apart: 83, of which 2 were waited for; matrix products, arithmetic and copies ran while one was open for 14% of the time, Pallas kernels for 0%

commit v1 on v0

v1 whole, which is shorter than its diff:
```python
import jax
import jax.numpy as jnp
from jax import lax
from jax.sharding import Mesh
from jax.sharding import PartitionSpec as P

HEADS = 8
HEAD = 88


def sublayer(stream, attend, output):
    widened = stream.astype(jnp.float32)
    center = jnp.mean(widened, axis=-1, keepdims=True)
    centered = widened - center
    variance = jnp.mean(centered * centered, axis=-1, keepdims=True)
    normed = (centered * lax.rsqrt(variance + 1e-05)).astype(jnp.bfloat16)
    projected = jnp.dot(normed, attend, preferred_element_type=jnp.float32).astype(jnp.bfloat16)
    projected = projected.reshape(stream.shape[:-1] + (3, HEADS, HEAD))
    query_rows = projected[..., 0, :, :]
    key_rows = projected[..., 1, :, :]
    value_rows = projected[..., 2, :, :]
    scores = jnp.einsum(
        "blmhe,bkmhe->bmhlk", query_rows, key_rows, preferred_element_type=jnp.float32
    ) * HEAD ** (-0.5)
    row_max = jnp.max(scores, axis=-1, keepdims=True)
    weights = jnp.exp(scores - row_max)
    attn_probs = (weights / jnp.sum(weights, axis=-1, keepdims=True)).astype(jnp.bfloat16)
    mixed = jnp.einsum(
        "bmhlk,bkmhe->blmhe", attn_probs, value_rows, preferred_element_type=jnp.float32
    )
    mixed = mixed.astype(jnp.bfloat16).reshape(stream.shape[:-1] + (HEADS * HEAD,))
    branch = lax.dot_general(
        mixed, output, (((mixed.ndim - 1,), (1,)), ((), ())), preferred_element_type=jnp.float32
    )
    return ((widened + branch).astype(jnp.bfloat16), mixed)


def summed_share(partial):
    rows, columns = partial.shape
    chips, cores, space = lax.axis_size("z"), lax.axis_size("core"), lax.axis_size("space")
    share = rows // (chips * cores * space)
    sent = partial.astype(jnp.bfloat16).reshape(chips, cores, space * share, columns)
    sent = jnp.swapaxes(sent, 0, 1)
    for axis, count in (("core", cores), ("z", chips)):
        sent = sent.reshape(count, -1, columns)
        got = lax.all_to_all(sent, axis, split_axis=0, concat_axis=0, tiled=True)
        sent = jnp.sum(got.astype(jnp.float32), axis=0).astype(jnp.bfloat16)
    sent = jnp.pad(sent.reshape(space, share, columns), ((0, 0), (0, 5), (0, 0)))
    got = lax.all_to_all(sent, "space", split_axis=0, concat_axis=0, tiled=True)
    return jnp.sum(got.astype(jnp.float32), axis=0)[:share]


CLIP = ("core", "space")


def to_patches(frame):
    devices = lax.axis_size(CLIP)
    cut = frame.reshape(devices, frame.shape[1] // devices, frame.shape[2])
    return lax.all_to_all(cut, CLIP, split_axis=0, concat_axis=0, tiled=True)


def body(
    video_tokens, grad_rows, targets, counts, attend_space, output_space, attend_time, output_time
):
    owners = lax.axis_size(("z", "core"))
    frames_dev, patches, model_width = video_tokens.shape
    capacity = grad_rows.shape[3]
    routed = ("z", "core")
    rows = lax.all_to_all(
        grad_rows.reshape(owners, capacity, model_width), routed, split_axis=0, concat_axis=0, tiled=True
    )
    aimed = targets.reshape(owners, capacity)
    slot = lax.broadcasted_iota(jnp.int32, aimed.shape, 1)
    aimed = jnp.where(slot < counts.reshape(owners, 1), aimed, -1)
    aimed = lax.all_to_all(aimed, routed, split_axis=0, concat_axis=0, tiled=True)
    token = lax.broadcasted_iota(jnp.int32, (patches, owners * capacity), 0)
    matches = (aimed.reshape(1, -1) == token).astype(jnp.bfloat16)
    grad_out = jnp.dot(
        matches, rows.reshape(-1, model_width), preferred_element_type=jnp.float32
    ).astype(jnp.bfloat16)

    def space_layer(stream):
        return sublayer(stream, attend_space, output_space)

    def time_layer(stream):
        return sublayer(stream, attend_time, output_time)

    hidden_four, space_pull, space_mixed = jax.vjp(
        space_layer, video_tokens[:, :, None, :], has_aux=True
    )
    patch_hidden = to_patches(hidden_four[:, :, 0, :])
    patch_grad = to_patches(grad_out[None])
    layer_out, time_pull, time_mixed = jax.vjp(time_layer, patch_hidden[None], has_aux=True)
    grad_time_input = time_pull(patch_grad[None])[0][0]
    time_part = lax.dot_general(
        patch_grad.reshape(-1, model_width),
        time_mixed.reshape(-1, HEADS * HEAD),
        (((0,), (0,)), ((), ())),
        preferred_element_type=jnp.float32,
    )
    grad_hidden = lax.all_to_all(grad_time_input, CLIP, split_axis=0, concat_axis=0, tiled=True)
    grad_hidden = grad_hidden.reshape(1, patches, model_width)
    space_part = lax.dot_general(
        grad_hidden.reshape(-1, model_width),
        space_mixed.reshape(-1, HEADS * HEAD),
        (((0,), (0,)), ((), ())),
        preferred_element_type=jnp.float32,
    )
    time_grad = summed_share(time_part)
    space_grad = summed_share(space_part)
    token_grad = space_pull(grad_hidden[:, :, None, :])[0][:, :, 0, :]
    return (token_grad, space_grad, time_grad)


def solution(mesh):
    chips = mesh.shape["tm"] // 2
    fine = Mesh(
        mesh.devices.reshape(chips, 2, mesh.shape["space"]), ("z", "core", "space")
    )
    tm = ("z", "core")
    whole = ("z", "core", "space")
    in_specs = (
        P(whole, None, None),
        P(tm, "space", None, None, None),
        P(tm, "space", None, None),
        P(tm, "space", None),
        P(),
        P(),
        P(),
        P(),
    )
    out_specs = (P(whole, None, None), P(whole, None), P(whole, None))
    return jax.shard_map(body, mesh=fine, in_specs=in_specs, out_specs=out_specs, check_vma=False)
```

time: 986 us -> 246 us (0.25); the launches traced: 971 us -> 243 us
  blocking collectives: 398 us -> 0 us
  starting transfers between devices: 275 us -> 54.5 us
  local copies, waits for them, and re-layouts: 183 us -> 44.6 us
  waiting for transfers between devices: 19.9 us -> 54.6 us
  between operations: 17.3 us -> 1.12 us
    unnamed x1 -> x0, blocking collectives: 371 us -> none
    unnamed x80 -> x0, starting transfers between devices: 265 us -> none
    unnamed x255 -> x58, local copies, waits for them, and re-layouts: 136 us -> 4.71 us
    all_to_all x2 -> x11, starting transfers between devices: 10.3 us -> 54.5 us  [the longest x4 18.4 us: summed_share(): got = lax.all_to_all(sent, axis, split_axis=0, concat_axis=0, tiled=True)]
    all_to_all x2 -> x11, waiting for transfers between devices: 19.6 us -> 54.6 us  [the longest x2 19.6 us: to_patches(): return lax.all_to_all(cut, CLIP, split_axis=0, concat_axis=0, tiled=True)]
    all_to_all x1 -> x0, blocking collectives: 26.8 us -> none  [body(): lax.all_to_all(as_sent(hidden), ('tm', 'space'), split_axis=1, concat_axi...]
    reshape x2 -> x1, local copies, waits for them, and re-layouts: 20.5 us -> 4.18 us  [sublayer(): projected = projected.reshape(stream.shape[:-1] + (3, HEADS, HEAD))]
    reduce_sum x0 -> x6, other arithmetic: none -> 14.3 us  [the longest x4 11 us: summed_share(): sent = jnp.sum(got.astype(jnp.float32), axis=0).astype(jnp.bfloat16)]
  transfers between devices with their start and end apart: 83 -> 11, of which waited for: 2 -> 8; matrix products, arithmetic and copies ran while one was open for 14% -> 32% of each run, Pallas kernels for 0% -> 0%
where the time goes in v1:
time: 246 us; the launch traced here: 243 us
  waiting for transfers between devices  54.6 us (22%)
  starting transfers between devices  54.5 us (22%)
  matrix products  50.9 us (21%)
  local copies, waits for them, and re-layouts  44.6 us (18%)
  other arithmetic  37.5 us (15%)
    dot_general x4, matrix products, sublayer(): jnp.dot(normed, attend, preferred_element_type=jnp.float32)  21.6 us
    all_to_all x2, waiting for transfers between devices, to_patches(): return lax.all_to_all(cut, CLIP, split_axis=0, concat_axis=0, tiled=True)  19.6 us
    all_to_all x4, starting transfers between devices, summed_share(): got = lax.all_to_all(sent, axis, split_axis=0, concat_axis=0, tiled=True)  18.4 us
    all_to_all x2, starting transfers between devices, to_patches(): return lax.all_to_all(cut, CLIP, split_axis=0, concat_axis=0, tiled=True)  12.2 us
    reduce_sum x4, other arithmetic, summed_share(): sent = jnp.sum(got.astype(jnp.float32), axis=0).astype(jnp.bfloat16)  11 us
    all_to_all x1, waiting for transfers between devices, body(): lax.all_to_all(grad_time_input, CLIP, split_axis=0, concat_axis=0, tiled=...  10.7 us
    all_to_all x4, waiting for transfers between devices, summed_share(): got = lax.all_to_all(sent, axis, split_axis=0, concat_axis=0, tiled=True)  10.7 us
    all_to_all x2, starting transfers between devices, summed_share(): got = lax.all_to_all(sent, 'space', split_axis=0, concat_axis=0, tiled=True)  9.86 us
  transfers between devices with their start and end apart: 11, of which 8 were waited for; matrix products, arithmetic and copies ran while one was open for 32% of the time, Pallas kernels for 0%

profile of v1, /device:TPU:0, one launch (start us, length us, event | category | flops | bytes accessed | tf_op | source)
XLA Modules:
  0.0 243.3 jit_solution(4066076997210437913)
XLA Ops:
  2.2 5.4 %all-to-all-start = ((s32[8,1,64]{2,1,0:T(1,128)}), s32[8,1,64]{2,1,0:T(1,128)S(1)}, u32[]{:S(2)}, u32[]{:S(2)}) async-start(s32[8,1,64]{2,1,0:T(1,128)} %compare_select_fusion), calls=%async_computation | async-start | bytes 8192 | tf_op jit(solution)/shard_map/all_to_all | solution.py:75
  10.9 4.7 %convolution_convert_fusion = bf16[256,2112]{0,1:T(8,128)(2,1)S(1)} fusion(bf16[1408,2112]{0,1:T(8,128)(2,1)} %param.12, bf16[1,256,1408]{2,1,0:T(8,128)(2,1)S(1)} %copy-done.3, f32[256]{0:T(256)S(1)} %fusion.89, f32[256]{0:T(256)S(1)} %broadcast_multiply_fusion.1), kind=kOutput, calls=%fused_computation.5 | convolution fusion | flops 1524514816 | bytes 7751680 | tf_op jit(solution)/shard_map/jvp()/dot_general | solution.py:17
  22.3 7.4 %all-to-all-start.3 = ((bf16[32,8,1408]{2,1,0:T(8,128)(2,1)}), bf16[32,8,1408]{2,1,0:T(8,128)(2,1)S(1)}, u32[]{:S(2)}, u32[]{:S(2)}) async-start(bf16[32,8,1408]{2,1,0:T(8,128)(2,1)} %fusion.15), calls=%async_computation.3 | async-start | bytes 1441792 | tf_op jit(solution)/shard_map/all_to_all | solution.py:59
  31.0 12.8 %all-to-all-done.3 = bf16[32,8,1408]{2,1,0:T(8,128)(2,1)S(1)} async-done(((bf16[32,8,1408]{2,1,0:T(8,128)(2,1)}), bf16[32,8,1408]{2,1,0:T(8,128)(2,1)S(1)}, u32[]{:S(2)}, u32[]{:S(2)}) %all-to-all-start.3) | async-done | bytes 720928 | tf_op jit(solution)/shard_map/all_to_all | solution.py:59
  43.8 4.7 %all-to-all-start.1 = ((bf16[8,64,1408]{2,1,0:T(8,128)(2,1)}), bf16[8,64,1408]{2,1,0:T(8,128)(2,1)}, u32[]{:S(2)}, u32[]{:S(2)}) async-start(bf16[8,64,1408]{2,1,0:T(8,128)(2,1)} %bitcast.210), calls=%async_computation.1 | async-start | bytes 2883584 | tf_op jit(solution)/shard_map/all_to_all | solution.py:69
  49.0 5.7 %fusion.4 = bf16[32,8,2112]{2,1,0:T(8,128)(2,1)} fusion(bf16[1408,2112]{0,1:T(8,128)(2,1)} %param.14, bf16[32,8,1408]{2,1,0:T(8,128)(2,1)S(1)} %all-to-all-done.3, f32[32,8]{1,0:T(8,128)S(1)} %fusion.88, f32[32,8]{1,0:T(8,128)S(1)} %broadcast_multiply_fusion), kind=kOutput, calls=%fused_computation.4 | convolution fusion | flops 1524514816 | bytes 7751680 | tf_op jit(solution)/shard_map/jvp()/dot_general | solution.py:17
  54.7 4.2 %reshape.564 = bf16[1,32,8,3,8,88]{5,4,3,2,1,0:T(8,128)(2,1)} reshape(bf16[32,8,2112]{2,1,0:T(8,128)(2,1)} %fusion.4) | data formatting | bytes 2162688 | tf_op jit(solution)/shard_map/jvp()/reshape | solution.py:18
  61.5 7.3 %all-to-all-done.1 = bf16[8,64,1408]{2,1,0:T(8,128)(2,1)} async-done(((bf16[8,64,1408]{2,1,0:T(8,128)(2,1)}), bf16[8,64,1408]{2,1,0:T(8,128)(2,1)}, u32[]{:S(2)}, u32[]{:S(2)}) %all-to-all-start.1) | async-done | bytes 1441824 | tf_op jit(solution)/shard_map/all_to_all | solution.py:69
  71.6 4.8 %all-to-all-start.2 = ((bf16[32,8,1408]{2,1,0:T(8,128)(2,1)}), bf16[32,8,1408]{2,1,0:T(8,128)(2,1)}, u32[]{:S(2)}, u32[]{:S(2)}) async-start(bf16[32,8,1408]{2,1,0:T(8,128)(2,1)} %fusion.16), calls=%async_computation.2 | async-start | bytes 1441792 | tf_op jit(solution)/shard_map/all_to_all | solution.py:59
  83.3 6.9 %all-to-all-done.2 = bf16[32,8,1408]{2,1,0:T(8,128)(2,1)} async-done(((bf16[32,8,1408]{2,1,0:T(8,128)(2,1)}), bf16[32,8,1408]{2,1,0:T(8,128)(2,1)}, u32[]{:S(2)}, u32[]{:S(2)}) %all-to-all-start.2) | async-done | bytes 720928 | tf_op jit(solution)/shard_map/all_to_all | solution.py:59
  90.2 3.4 %fusion.41 = bf16[32,8,704]{2,1,0:T(8,128)(2,1)} fusion(bf16[32,8,1408]{2,1,0:T(8,128)(2,1)} %all-to-all-done.2, bf16[1408,704]{0,1:T(8,128)(2,1)} %param.15), kind=kOutput, calls=%fused_computation.68 | convolution fusion | flops 507691008 | bytes 3063808 | tf_op jit(solution)/shard_map/transpose(jvp())/dot_general | solution.py:32
  104.1 3.7 %reshape.568 = bf16[32,8,2112]{2,1,0:T(8,128)(2,1)} reshape(bf16[1,32,8,3,8,88]{5,4,3,2,1,0:T(8,128)(2,1)} %copy.59) | data formatting | bytes 2162688 | tf_op jit(solution)/shard_map/reshape.82
  107.8 5.1 %fusion.35 = (f32[32,8]{1,0:T(8,128)S(1)}, f32[32,8,1408]{2,1,0:T(8,128)S(1)}) fusion(bf16[32,8,1408]{2,1,0:T(8,128)(2,1)S(1)} %all-to-all-done.3, f32[32,8]{1,0:T(8,128)S(1)} %broadcast_multiply_fusion, bf16[32,8,2112]{2,1,0:T(8,128)(2,1)} %reshape.568, bf16[1408,2112]{0,1:T(8,128)(2,1)} %param.14), kind=kOutput, calls=%fused_computation.52 | convolution fusion | flops 1524694784 | bytes 9193472 | tf_op jit(solution)/shard_map/transpose(jvp())/dot_general | solution.py:17
  114.5 3.2 %convolution_convert_fusion.2 = bf16[1408,704]{0,1:T(8,128)(2,1)} fusion(bf16[256,704]{1,0:T(8,128)(2,1)S(1)} %copy-done.16, bf16[32,8,1408]{2,1,0:T(8,128)(2,1)} %all-to-all-done.2), kind=kOutput, calls=%fused_computation.7 | convolution fusion | flops 508502016 | bytes 3063808 | tf_op jit(solution)/shard_map/dot_general | solution.py:95
  117.6 4.0 %copy.67 = bf16[1408,704]{1,0:T(8,128)(2,1)} copy(bf16[1408,704]{0,1:T(8,128)(2,1)} %convolution_convert_fusion.2) | data formatting | bytes 3964928 | tf_op jit(solution)/shard_map/convert_element_type | solution.py:42
  121.7 3.1 %copy.68 = bf16[2,4,176,704]{3,2,1,0:T(8,128)(2,1)} copy(bf16[2,4,176,704]{3,2,0,1:T(8,128)(2,1)} %bitcast.198) | data formatting | bytes 3964928 | tf_op jit(solution)/shard_map/transpose | solution.py:43
  124.8 4.8 %all-to-all-start.8 = ((bf16[2,704,704]{2,1,0:T(8,128)(2,1)}), bf16[2,704,704]{2,1,0:T(8,128)(2,1)}, u32[]{:S(2)}, u32[]{:S(2)}) async-start(bf16[2,704,704]{2,1,0:T(8,128)(2,1)} %bitcast.197), calls=%async_computation.8 | async-start | bytes 4325376 | tf_op jit(solution)/shard_map/all_to_all | solution.py:46
  132.6 3.9 %all-to-all-start.4 = ((bf16[32,8,1408]{2,1,0:T(8,128)(2,1)}), bf16[32,8,1408]{2,1,0:T(8,128)(2,1)S(1)}, u32[]{:S(2)}, u32[]{:S(2)}) async-start(bf16[32,8,1408]{2,1,0:T(8,128)(2,1)} %add_convert_fusion.1), calls=%async_computation.4 | async-start | bytes 1441792 | tf_op jit(solution)/shard_map/all_to_all | solution.py:101
  136.6 3.3 %reduce_sum.261 = bf16[704,704]{1,0:T(8,128)(2,1)} reduce(bf16[2,704,704]{2,1,0:T(8,128)(2,1)} %all-to-all-done.8, bf16[]{:T(256)} %constant.36.clone.1), dimensions={0}, to_apply=%region_21.22 | reduce | flops 495616 | bytes 2973698 | tf_op jit(solution)/shard_map/reduce_sum | solution.py:47
  139.9 10.7 %all-to-all-done.4 = bf16[32,8,1408]{2,1,0:T(8,128)(2,1)S(1)} async-done(((bf16[32,8,1408]{2,1,0:T(8,128)(2,1)}), bf16[32,8,1408]{2,1,0:T(8,128)(2,1)S(1)}, u32[]{:S(2)}, u32[]{:S(2)}) %all-to-all-start.4) | async-done | bytes 720928 | tf_op jit(solution)/shard_map/all_to_all | solution.py:101
  156.9 4.0 %copy.63 = bf16[1408,704]{1,0:T(8,128)(2,1)} copy(bf16[1408,704]{0,1:T(8,128)(2,1)} %convolution_convert_fusion.1) | data formatting | bytes 3964928 | tf_op jit(solution)/shard_map/convert_element_type | solution.py:42
  164.0 4.8 %all-to-all-start.5 = ((bf16[2,704,704]{2,1,0:T(8,128)(2,1)}), bf16[2,704,704]{2,1,0:T(8,128)(2,1)}, u32[]{:S(2)}, u32[]{:S(2)}) async-start(bf16[2,704,704]{2,1,0:T(8,128)(2,1)} %bitcast.196), calls=%async_computation.5 | async-start | bytes 4325376 | tf_op jit(solution)/shard_map/all_to_all | solution.py:46
  168.9 3.8 %fusion.102 = (f32[8,256]{1,0:T(8,128)S(1)}, f32[8,256,256]{1,2,0:T(8,128)}) fusion(f32[8,256]{1,0:T(8,128)S(1)} %get-tuple-element.14, f32[8,256,256]{1,2,0:T(8,128)} %copy-done.1, f32[8,256]{1,0:T(8,128)S(1)} %neg.29, f32[8,256]{1,0:T(8,128)S(1)} %fusion.63, bf16[8,256,256]{1,2,0:T(8,128)(2,1)} %get-tuple-element.23), kind=kLoop, calls=%fused_computation.154 | loop fusion | flops 3667968 | bytes 5275648 | tf_op jit(solution)/shard_map/transpose(jvp())/reduce_sum | solution.py:26
  172.8 4.3 %all-to-all-start.9 = ((bf16[4,176,704]{2,1,0:T(8,128)(2,1)}), bf16[4,176,704]{2,1,0:T(8,128)(2,1)}, u32[]{:S(2)}, u32[]{:S(2)}) async-start(bf16[4,176,704]{2,1,0:T(8,128)(2,1)} %bitcast.206), calls=%async_computation.9 | async-start | bytes 2162688 | tf_op jit(solution)/shard_map/all_to_all | solution.py:46
  177.0 3.3 %reduce_sum.258 = bf16[704,704]{1,0:T(8,128)(2,1)} reduce(bf16[2,704,704]{2,1,0:T(8,128)(2,1)} %all-to-all-done.5, bf16[]{:T(256)} %constant.36.clone.1), dimensions={0}, to_apply=%region_18.19 | reduce | flops 495616 | bytes 2973698 | tf_op jit(solution)/shard_map/reduce_sum | solution.py:47
  186.3 7.2 %all-to-all-done.9 = bf16[4,176,704]{2,1,0:T(8,128)(2,1)} async-done(((bf16[4,176,704]{2,1,0:T(8,128)(2,1)}), bf16[4,176,704]{2,1,0:T(8,128)(2,1)}, u32[]{:S(2)}, u32[]{:S(2)}) %all-to-all-start.9) | async-done | bytes 991264 | tf_op jit(solution)/shard_map/all_to_all | solution.py:46
  193.5 4.5 %all-to-all-start.6 = ((bf16[4,176,704]{2,1,0:T(8,128)(2,1)}), bf16[4,176,704]{2,1,0:T(8,128)(2,1)}, u32[]{:S(2)}, u32[]{:S(2)}) async-start(bf16[4,176,704]{2,1,0:T(8,128)(2,1)} %bitcast.207), calls=%async_computation.6 | async-start | bytes 2162688 | tf_op jit(solution)/shard_map/all_to_all | solution.py:46
  198.0 6.2 %fusion.37 = (f32[256]{0:T(256)S(1)}, f32[256,1408]{1,0:T(8,128)}) fusion(bf16[1,256,1408]{2,1,0:T(8,128)(2,1)S(1)} %copy-done.3, f32[256]{0:T(256)S(1)} %copy-done.24, bf16[256,2112]{0,1:T(8,128)(2,1)} %bitcast.200, bf16[1408,2112]{0,1:T(8,128)(2,1)} %param.12), kind=kOutput, calls=%fused_computation.54 | convolution fusion | flops 1524694784 | bytes 9193472 | tf_op jit(solution)/shard_map/transpose(jvp())/dot_general | solution.py:17
  210.0 3.4 %all-to-all-done.6 = bf16[4,176,704]{2,1,0:T(8,128)(2,1)} async-done(((bf16[4,176,704]{2,1,0:T(8,128)(2,1)}), bf16[4,176,704]{2,1,0:T(8,128)(2,1)}, u32[]{:S(2)}, u32[]{:S(2)}) %all-to-all-start.6) | async-done | bytes 991264 | tf_op jit(solution)/shard_map/all_to_all | solution.py:46
  213.4 4.2 %all-to-all-start.10 = ((bf16[16,16,704]{2,1,0:T(8,128)(2,1)}), bf16[16,16,704]{2,1,0:T(8,128)(2,1)}, u32[]{:S(2)}, u32[]{:S(2)}) async-start(bf16[16,16,704]{2,1,0:T(8,128)(2,1)} %pad.32), calls=%async_computation.10 | async-start | bytes 786432 | tf_op jit(solution)/shard_map/all_to_all | solution.py:49
  226.7 5.7 %all-to-all-start.7 = ((bf16[16,16,704]{2,1,0:T(8,128)(2,1)}), bf16[16,16,704]{2,1,0:T(8,128)(2,1)}, u32[]{:S(2)}, u32[]{:S(2)}) async-start(bf16[16,16,704]{2,1,0:T(8,128)(2,1)} %pad.31), calls=%async_computation.7 | async-start | bytes 786432 | tf_op jit(solution)/shard_map/all_to_all | solution.py:49
  236.8 4.8 %all-to-all-done.7 = bf16[16,16,704]{2,1,0:T(8,128)(2,1)} async-done(((bf16[16,16,704]{2,1,0:T(8,128)(2,1)}), bf16[16,16,704]{2,1,0:T(8,128)(2,1)}, u32[]{:S(2)}, u32[]{:S(2)}) %all-to-all-start.7) | async-done | bytes 360480 | tf_op jit(solution)/shard_map/all_to_all | solution.py:49
  (124 shorter events, 76.9 us)
Async XLA Ops:
  0.6 20.0 %copy-start = (bf16[1408,704]{0,1:T(8,128)(2,1)S(1)}, bf16[1408,704]{0,1:T(8,128)(2,1)}, u32[]{:S(2)}) copy-start(bf16[1408,704]{0,1:T(8,128)(2,1)} %param.13) | copy-start | bytes 5947396
  0.6 10.2 %copy-start.3 = (bf16[1,256,1408]{2,1,0:T(8,128)(2,1)S(1)}, bf16[1,256,1408]{2,1,0:T(8,128)(2,1)}, u32[]{:S(2)}) copy-start(bf16[1,256,1408]{2,1,0:T(8,128)(2,1)} %param.8) | copy-start | bytes 2162692
  2.2 20.2 %all-to-all-start = ((s32[8,1,64]{2,1,0:T(1,128)}), s32[8,1,64]{2,1,0:T(1,128)S(1)}, u32[]{:S(2)}, u32[]{:S(2)}) async-start(s32[8,1,64]{2,1,0:T(1,128)} %compare_select_fusion), calls=%async_computation | async-start | bytes 8192 | tf_op jit(solution)/shard_map/all_to_all | solution.py:75
  8.9 6.7 %copy-start.23 = (f32[256]{0:T(256)}, f32[256]{0:T(256)S(1)}, u32[]{:S(2)}) copy-start(f32[256]{0:T(256)S(1)} %broadcast_multiply_fusion.1) | copy-start | bytes 3076
  10.9 4.7 %copy-start.25 = (f32[256]{0:T(256)}, f32[256]{0:T(256)S(1)}, u32[]{:S(2)}) copy-start(f32[256]{0:T(256)S(1)} %fusion.89) | copy-start | bytes 3076
  15.5 3.1 %copy-start.10 = (bf16[256,2112]{0,1:T(8,128)(2,1)}, bf16[256,2112]{0,1:T(8,128)(2,1)S(1)}, u32[]{:S(2)}) copy-start(bf16[256,2112]{0,1:T(8,128)(2,1)S(1)} %convolution_convert_fusion) | copy-start | bytes 3244036
  16.0 2.6 %copy-start.1 = (f32[8,256,256]{1,2,0:T(8,128)}, f32[8,256,256]{1,2,0:T(8,128)S(1)}, u32[]{:S(2)}) copy-start(f32[8,256,256]{1,2,0:T(8,128)S(1)} %get-tuple-element.15) | copy-start | bytes 6291460
  22.3 21.5 %all-to-all-start.3 = ((bf16[32,8,1408]{2,1,0:T(8,128)(2,1)}), bf16[32,8,1408]{2,1,0:T(8,128)(2,1)S(1)}, u32[]{:S(2)}, u32[]{:S(2)}) async-start(bf16[32,8,1408]{2,1,0:T(8,128)(2,1)} %fusion.15), calls=%async_computation.3 | async-start | bytes 1441792 | tf_op jit(solution)/shard_map/all_to_all | solution.py:59
  43.8 25.0 %all-to-all-start.1 = ((bf16[8,64,1408]{2,1,0:T(8,128)(2,1)}), bf16[8,64,1408]{2,1,0:T(8,128)(2,1)}, u32[]{:S(2)}, u32[]{:S(2)}) async-start(bf16[8,64,1408]{2,1,0:T(8,128)(2,1)} %bitcast.210), calls=%async_computation.1 | async-start | bytes 2883584 | tf_op jit(solution)/shard_map/all_to_all | solution.py:69
  71.6 18.6 %all-to-all-start.2 = ((bf16[32,8,1408]{2,1,0:T(8,128)(2,1)}), bf16[32,8,1408]{2,1,0:T(8,128)(2,1)}, u32[]{:S(2)}, u32[]{:S(2)}) async-start(bf16[32,8,1408]{2,1,0:T(8,128)(2,1)} %fusion.16), calls=%async_computation.2 | async-start | bytes 1441792 | tf_op jit(solution)/shard_map/all_to_all | solution.py:59
  76.4 2.4 %copy-start.19 = (bf16[1,32,8,1,8,88]{5,4,3,2,1,0:T(8,128)(2,1)S(1)}, bf16[1,32,8,1,8,88]{5,4,3,2,1,0:T(8,128)(2,1)}, u32[]{:S(2)}) copy-start(bf16[1,32,8,1,8,88]{5,4,3,2,1,0:T(8,128)(2,1)} %get-tuple-element.10) | copy-start | bytes 1081348
  96.0 2.1 copy-start.7
  96.0 2.1 copy-start.18
  96.0 2.1 copy-start.20
  96.0 2.1 copy-start.22
  124.8 7.9 %all-to-all-start.8 = ((bf16[2,704,704]{2,1,0:T(8,128)(2,1)}), bf16[2,704,704]{2,1,0:T(8,128)(2,1)}, u32[]{:S(2)}, u32[]{:S(2)}) async-start(bf16[2,704,704]{2,1,0:T(8,128)(2,1)} %bitcast.197), calls=%async_computation.8 | async-start | bytes 4325376 | tf_op jit(solution)/shard_map/all_to_all | solution.py:46
  132.6 17.9 %all-to-all-start.4 = ((bf16[32,8,1408]{2,1,0:T(8,128)(2,1)}), bf16[32,8,1408]{2,1,0:T(8,128)(2,1)S(1)}, u32[]{:S(2)}, u32[]{:S(2)}) async-start(bf16[32,8,1408]{2,1,0:T(8,128)(2,1)} %add_convert_fusion.1), calls=%async_computation.4 | async-start | bytes 1441792 | tf_op jit(solution)/shard_map/all_to_all | solution.py:101
  150.6 1.6 copy-start.2
  151.3 3.6 %copy-start.17 = (bf16[256,704]{0,1:T(8,128)(2,1)}, bf16[256,704]{0,1:T(8,128)(2,1)S(1)}, u32[]{:S(2)}) copy-start(bf16[256,704]{0,1:T(8,128)(2,1)S(1)} %convolution_convert_fusion.13) | copy-start | bytes 1081348
  152.2 2.8 %copy-start.13 = (bf16[8,88,256]{2,1,0:T(8,128)(2,1)S(1)}, bf16[8,88,256]{2,1,0:T(8,128)(2,1)}, u32[]{:S(2)}) copy-start(bf16[8,88,256]{2,1,0:T(8,128)(2,1)} %copy-done.12) | copy-start | bytes 1081348
  164.0 8.7 %all-to-all-start.5 = ((bf16[2,704,704]{2,1,0:T(8,128)(2,1)}), bf16[2,704,704]{2,1,0:T(8,128)(2,1)}, u32[]{:S(2)}, u32[]{:S(2)}) async-start(bf16[2,704,704]{2,1,0:T(8,128)(2,1)} %bitcast.196), calls=%async_computation.5 | async-start | bytes 4325376 | tf_op jit(solution)/shard_map/all_to_all | solution.py:46
  168.9 3.9 %copy-start.21 = (f32[8,256]{1,0:T(8,128)S(1)}, f32[8,256]{1,0:T(8,128)}, u32[]{:S(2)}) copy-start(f32[8,256]{1,0:T(8,128)} %get-tuple-element.5) | copy-start | bytes 24580
  172.8 20.7 %all-to-all-start.9 = ((bf16[4,176,704]{2,1,0:T(8,128)(2,1)}), bf16[4,176,704]{2,1,0:T(8,128)(2,1)}, u32[]{:S(2)}, u32[]{:S(2)}) async-start(bf16[4,176,704]{2,1,0:T(8,128)(2,1)} %bitcast.206), calls=%async_computation.9 | async-start | bytes 2162688 | tf_op jit(solution)/shard_map/all_to_all | solution.py:46
  180.4 1.9 copy-start.9
  180.4 1.9 copy-start.11
  182.3 2.3 copy-start.4
  186.3 11.7 %copy-start.24 = (f32[256]{0:T(256)S(1)}, f32[256]{0:T(256)}, u32[]{:S(2)}) copy-start(f32[256]{0:T(256)} %copy-done.23) | copy-start | bytes 3076
  193.5 19.9 %all-to-all-start.6 = ((bf16[4,176,704]{2,1,0:T(8,128)(2,1)}), bf16[4,176,704]{2,1,0:T(8,128)(2,1)}, u32[]{:S(2)}, u32[]{:S(2)}) async-start(bf16[4,176,704]{2,1,0:T(8,128)(2,1)} %bitcast.207), calls=%async_computation.6 | async-start | bytes 2162688 | tf_op jit(solution)/shard_map/all_to_all | solution.py:46
  198.0 6.2 %copy-start.28 = (f32[256]{0:T(256)S(1)}, f32[256]{0:T(256)}, u32[]{:S(2)}) copy-start(f32[256]{0:T(256)} %copy-done.27) | copy-start | bytes 3076
  206.4 11.2 %copy-start.26 = (f32[256]{0:T(256)S(1)}, f32[256]{0:T(256)}, u32[]{:S(2)}) copy-start(f32[256]{0:T(256)} %copy-done.25) | copy-start | bytes 3076
  213.4 13.3 %all-to-all-start.10 = ((bf16[16,16,704]{2,1,0:T(8,128)(2,1)}), bf16[16,16,704]{2,1,0:T(8,128)(2,1)}, u32[]{:S(2)}, u32[]{:S(2)}) async-start(bf16[16,16,704]{2,1,0:T(8,128)(2,1)} %pad.32), calls=%async_computation.10 | async-start | bytes 786432 | tf_op jit(solution)/shard_map/all_to_all | solution.py:49
  226.7 14.9 %all-to-all-start.7 = ((bf16[16,16,704]{2,1,0:T(8,128)(2,1)}), bf16[16,16,704]{2,1,0:T(8,128)(2,1)}, u32[]{:S(2)}, u32[]{:S(2)}) async-start(bf16[16,16,704]{2,1,0:T(8,128)(2,1)} %pad.31), calls=%async_computation.7 | async-start | bytes 786432 | tf_op jit(solution)/shard_map/all_to_all | solution.py:49
  (8 other events, 8.0 us)

commit v2 on v1

v2 whole, which is shorter than its diff:
```python
import jax, jax.numpy as jnp
from jax import lax
from jax.experimental import pallas as pl
from jax.experimental.pallas import tpu as pltpu
from jax.sharding import Mesh
from jax.sharding import PartitionSpec as P

HEADS = 8
HEAD = 88
EPS = 1e-05
PATCHES = 8
CLIP = ("core", "space")
OWNERS = ("z", "core")
VMEM = pl.BlockSpec(memory_space=pltpu.VMEM)
SMEM = pl.BlockSpec(memory_space=pltpu.SMEM)


LIMIT = pltpu.CompilerParams(vmem_limit_bytes=40 * 2**20)


def cost(flops):
    return pl.CostEstimate(flops=int(flops), bytes_accessed=10_000_000, transcendentals=600_000)


def normalise(stream):
    widened = stream.astype(jnp.float32)
    center = jnp.mean(widened, axis=-1, keepdims=True)
    centered = widened - center
    variance = jnp.mean(centered * centered, axis=-1, keepdims=True)
    scale = lax.rsqrt(variance + EPS)
    return centered * scale, scale


def dot_nt(a, b):
    return lax.dot_general(a, b, (((1,), (1,)), ((), ())), preferred_element_type=jnp.float32)


def dot_tn(a, b):
    return lax.dot_general(a, b, (((0,), (0,)), ((), ())), preferred_element_type=jnp.float32)


def dot_nn(a, b):
    return jnp.dot(a, b, preferred_element_type=jnp.float32)


def same_patch(tokens):
    row = lax.broadcasted_iota(jnp.int32, (tokens, tokens), 0)
    column = lax.broadcasted_iota(jnp.int32, (tokens, tokens), 1)
    return (row % PATCHES) == (column % PATCHES)


def head(projected_ref, part, h):
    at = (part * HEADS + h) * HEAD
    return projected_ref[:, at : at + HEAD]


def forward_kernel(temporal, stream_ref, attend_ref, *rest):
    if temporal:
        projected_ref, probs_ref, mixed_ref = rest
    else:
        output_ref, projected_ref, probs_ref, mixed_ref, out_ref = rest
    tokens = stream_ref.shape[0]
    normed = normalise(stream_ref[...])[0].astype(jnp.bfloat16)
    projected_ref[...] = dot_nt(normed, attend_ref[...]).astype(jnp.bfloat16)
    for h in range(HEADS):
        scores = dot_nt(head(projected_ref, 0, h), head(projected_ref, 1, h)) * HEAD**-0.5
        if temporal:
            scores = jnp.where(same_patch(tokens), scores, -jnp.inf)
        weights = jnp.exp(scores - jnp.max(scores, axis=-1, keepdims=True))
        probs = (weights / jnp.sum(weights, axis=-1, keepdims=True)).astype(jnp.bfloat16)
        probs_ref[h] = probs
        mixed_ref[:, h * HEAD : (h + 1) * HEAD] = dot_nn(probs, head(projected_ref, 2, h)).astype(
            jnp.bfloat16
        )
    if not temporal:
        branch = dot_nn(mixed_ref[...], output_ref[...])
        out_ref[...] = (stream_ref[...].astype(jnp.float32) + branch).astype(jnp.bfloat16)


def forward(stream, attend, output=None):
    temporal = output is None
    tokens, width = stream.shape
    bf = jnp.bfloat16
    shapes = [
        jax.ShapeDtypeStruct((tokens, 3 * HEADS * HEAD), bf),
        jax.ShapeDtypeStruct((HEADS, tokens, tokens), bf),
        jax.ShapeDtypeStruct((tokens, HEADS * HEAD), bf),
    ]
    args = [stream, attend.T]
    if not temporal:
        shapes.append(jax.ShapeDtypeStruct((tokens, width), bf))
        args.append(output.T)
    return pl.pallas_call(
        lambda *refs: forward_kernel(temporal, *refs),
        out_shape=shapes,
        in_specs=[VMEM] * len(args),
        out_specs=[VMEM] * len(shapes),
        compiler_params=LIMIT,
        cost_estimate=cost(2.2e9),
        name="time_forward" if temporal else "space_forward",
    )(*args)


def backward_kernel(grad_ref, stream_ref, projected_ref, probs_ref, attend_ref, output_ref, out_ref, dproj_ref):
    bf = jnp.bfloat16
    grad = grad_ref[...]
    dmixed = dot_nt(grad, output_ref[...]).astype(bf)
    for h in range(HEADS):
        probs = probs_ref[h]
        dm = dmixed[:, h * HEAD : (h + 1) * HEAD]
        dprobs = dot_nt(dm, head(projected_ref, 2, h)).astype(bf).astype(jnp.float32)
        wide = probs.astype(jnp.float32)
        scaled = wide * dprobs
        dscores = (scaled - wide * jnp.sum(scaled, axis=-1, keepdims=True)) * HEAD**-0.5
        dscores = dscores.astype(bf)
        for part, value in (
            (0, dot_nn(dscores, head(projected_ref, 1, h))),
            (1, dot_tn(dscores, head(projected_ref, 0, h))),
            (2, dot_tn(probs, dm)),
        ):
            at = (part * HEADS + h) * HEAD
            dproj_ref[:, at : at + HEAD] = value.astype(bf)
    dnormed = dot_nn(dproj_ref[...], attend_ref[...]).astype(bf).astype(jnp.float32)
    normed, scale = normalise(stream_ref[...])
    mean_d = jnp.mean(dnormed, axis=-1, keepdims=True)
    mean_dn = jnp.mean(dnormed * normed, axis=-1, keepdims=True)
    inner = scale * (dnormed - mean_d - normed * mean_dn)
    out_ref[...] = (grad.astype(jnp.float32) + inner).astype(bf)


def backward(grad, stream, projected, probs, attend, output, name):
    args = [grad, stream, projected, probs, attend.T, output.T]
    return pl.pallas_call(
        backward_kernel,
        out_shape=jax.ShapeDtypeStruct(grad.shape, jnp.bfloat16),
        in_specs=[VMEM] * len(args),
        out_specs=VMEM,
        scratch_shapes=[pltpu.VMEM(projected.shape, jnp.bfloat16)],
        compiler_params=LIMIT,
        cost_estimate=cost(2.6e9),
        name=name,
    )(*args)


def weight_kernel(grad_ref, mixed_ref, out_ref):
    out_ref[...] = dot_tn(grad_ref[...], mixed_ref[...]).astype(jnp.bfloat16)


def weight_partial(grad, mixed, name):
    return pl.pallas_call(
        weight_kernel,
        out_shape=jax.ShapeDtypeStruct((grad.shape[1], mixed.shape[1]), jnp.bfloat16),
        in_specs=[VMEM] * 2,
        out_specs=VMEM,
        compiler_params=LIMIT,
        name=name,
    )(grad, mixed)


def weight_split_kernel(place_ref, grad_ref, mixed_ref, mine_ref, other_ref, total_ref):
    core = place_ref[1]
    chips, rows, _ = mine_ref.shape
    total_ref[...] = dot_tn(grad_ref[...], mixed_ref[...])
    for z in range(chips):
        for ref, of in ((mine_ref, core), (other_ref, 1 - core)):
            at = pl.multiple_of((2 * z + of) * rows, 8)
            ref[z] = total_ref[pl.ds(at, rows), :].astype(jnp.bfloat16)


def weight_split(place, grad, mixed, chips, name):
    rows, columns = grad.shape[1], mixed.shape[1]
    half = jax.ShapeDtypeStruct((chips, rows // (2 * chips), columns), jnp.bfloat16)
    return pl.pallas_call(
        weight_split_kernel,
        out_shape=[half, half],
        in_specs=[SMEM, VMEM, VMEM],
        out_specs=[VMEM] * 2,
        scratch_shapes=[pltpu.VMEM((rows, columns), jnp.float32)],
        compiler_params=LIMIT,
        name=name,
    )(place, grad, mixed)


def pack_kernel(space_ref, time_ref, out_ref):
    devices = out_ref.shape[0]
    total = space_ref[0].astype(jnp.float32)
    for z in range(1, space_ref.shape[0]):
        total = total + space_ref[z].astype(jnp.float32)
    both = jnp.concatenate([total, time_ref[...].astype(jnp.float32)], axis=1)
    share = both.shape[0] // devices
    fill = jnp.zeros((out_ref.shape[1] - share, both.shape[1]), jnp.float32)
    for s in range(devices):
        rows = jnp.concatenate([both[s * share : (s + 1) * share, :], fill], axis=0)
        out_ref[s] = rows.astype(jnp.bfloat16)


def pack(space_parts, time_part, devices):
    columns = time_part.shape[1]
    return pl.pallas_call(
        pack_kernel,
        out_shape=jax.ShapeDtypeStruct((devices, 16, 2 * columns), jnp.bfloat16),
        in_specs=[VMEM] * 2,
        out_specs=VMEM,
        compiler_params=LIMIT,
        name="pack_shares",
    )(space_parts, time_part)


def unpack_kernel(parts_ref, space_ref, time_ref):
    share, columns = space_ref.shape
    total = parts_ref[0].astype(jnp.float32)
    for s in range(1, parts_ref.shape[0]):
        total = total + parts_ref[s].astype(jnp.float32)
    space_ref[...] = total[:share, :columns]
    time_ref[...] = total[:share, columns:]


def unpack(parts, share):
    out = jax.ShapeDtypeStruct((share, parts.shape[2] // 2), jnp.float32)
    return pl.pallas_call(
        unpack_kernel,
        out_shape=[out, out],
        in_specs=[VMEM],
        out_specs=[VMEM] * 2,
        compiler_params=LIMIT,
        name="sum_shares",
    )(parts)


def scatter_kernel(place_ref, aimed_ref, *refs):
    out_ref = refs[-1]
    z, core = place_ref[0], place_ref[1]
    chips = len(refs) - 1
    tokens = out_ref.shape[0]
    total = None
    for d in range(chips):
        source = (z + chips - d) % chips
        aims = [aimed_ref[(source * 2 + of) * 2 * chips + z * 2 + core] for of in (core, 1 - core)]
        aims = jnp.concatenate(aims, axis=1)
        token = lax.broadcasted_iota(jnp.int32, (tokens, aims.shape[1]), 0)
        matches = jnp.where(aims == token, 1.0, 0.0).astype(jnp.bfloat16)
        term = dot_nn(matches, refs[d][...])
        total = term if total is None else total + term
    out_ref[...] = total.astype(jnp.bfloat16)


def scatter_rows(place, aimed, pieces, tokens):
    return pl.pallas_call(
        scatter_kernel,
        out_shape=jax.ShapeDtypeStruct((tokens, pieces[0].shape[1]), jnp.bfloat16),
        in_specs=[SMEM] + [VMEM] * (1 + len(pieces)),
        out_specs=VMEM,
        compiler_params=LIMIT,
        cost_estimate=cost(4e8),
        name="scatter_rows",
    )(place, aimed, *pieces)


def exchange(tokens, axes):
    devices = lax.axis_size(axes)
    cut = tokens.reshape(devices, tokens.shape[0] // devices, tokens.shape[1])
    return lax.all_to_all(cut, axes, split_axis=0, concat_axis=0, tiled=True).reshape(tokens.shape)


def shift(array, axis, by):
    devices = lax.axis_size(axis)
    return lax.ppermute(array, axis, [(i, (i + by) % devices) for i in range(devices)])


def routed(grad_rows, targets, counts, place, tokens):
    chips, cores = lax.axis_size("z"), lax.axis_size("core")
    capacity, width = grad_rows.shape[3:]
    z, core = place[0], place[1]
    rows = grad_rows.reshape(chips, cores, capacity, width)
    aimed = targets.reshape(chips * cores, 1, capacity)
    slot = lax.broadcasted_iota(jnp.int32, aimed.shape, 2)
    aimed = jnp.where(slot < counts.reshape(-1, 1, 1), aimed, -1)
    aimed = lax.all_gather(aimed, OWNERS, axis=0, tiled=True)

    def of_core(which):
        return lax.dynamic_index_in_dim(rows, which, axis=1, keepdims=False)

    got = shift(of_core(1 - core), "core", 1)
    mine = of_core(core)
    pieces = []
    for d in range(chips):
        to = (z + d) % chips
        block = [lax.dynamic_index_in_dim(a, to, axis=0, keepdims=False) for a in (mine, got)]
        block = jnp.concatenate(block, axis=0)
        pieces.append(block if d == 0 else shift(block, "z", d))
    return scatter_rows(place, aimed, pieces, tokens)


def body(
    video_tokens, grad_rows, targets, counts, attend_space, output_space, attend_time, output_time
):
    chips, space = lax.axis_size("z"), lax.axis_size("space")
    stream = video_tokens[0]
    place = jnp.stack([lax.axis_index("z"), lax.axis_index("core")]).astype(jnp.int32)
    grad_out = routed(grad_rows, targets, counts, place, stream.shape[0])
    space_saved = forward(stream, attend_space, output_space)
    hidden = exchange(space_saved[3], CLIP)
    grad = exchange(grad_out, CLIP)
    time_saved = forward(hidden, attend_time)
    grad_hidden = backward(
        grad, hidden, time_saved[0], time_saved[1], attend_time, output_time, "time_backward"
    )
    time_part = weight_partial(grad, time_saved[2], "time_weight")
    time_part = lax.psum_scatter(time_part, OWNERS, scatter_dimension=0, tiled=True)
    grad_hidden = exchange(grad_hidden, CLIP)
    mine, other = weight_split(place, grad_hidden, space_saved[2], chips, "space_weight")
    space_part = mine.astype(jnp.float32) + shift(other, "core", 1).astype(jnp.float32)
    space_part = space_part.astype(jnp.bfloat16)
    space_part = lax.all_to_all(space_part, "z", split_axis=0, concat_axis=0, tiled=True)
    shares = pack(space_part, time_part, space)
    shares = lax.all_to_all(shares, "space", split_axis=0, concat_axis=0, tiled=True)
    space_grad, time_grad = unpack(shares, time_part.shape[0] // space)
    token_grad = backward(
        grad_hidden, stream, space_saved[0], space_saved[1], attend_space, output_space, "space_backward"
    )
    return (token_grad[None], space_grad, time_grad)


def solution(mesh):
    chips = mesh.shape["tm"] // 2
    fine = Mesh(mesh.devices.reshape(chips, 2, mesh.shape["space"]), ("z", "core", "space"))
    whole = ("z", "core", "space")
    in_specs = (
        P(whole, None, None),
        P(OWNERS, "space", None, None, None),
        P(OWNERS, "space", None, None),
        P(OWNERS, "space", None),
        P(),
        P(),
        P(),
        P(),
    )
    out_specs = (P(whole, None, None), P(whole, None), P(whole, None))
    return jax.shard_map(body, mesh=fine, in_specs=in_specs, out_specs=out_specs, check_vma=False)
```

time: 246 us -> 171 us (0.70)
  blocking collectives: 0 us -> 58.9 us
  matrix products: 50.9 us -> 0 us
  waiting for transfers between devices: 54.6 us -> 6.73 us
  other arithmetic: 37.5 us -> 0.52 us
  Pallas kernels: 0 us -> 32.4 us
  starting transfers between devices: 54.5 us -> 25.5 us
  local copies, waits for them, and re-layouts: 44.6 us -> 31.3 us
  between operations: 1.12 us -> 14.3 us
    dot_general x22 -> x0, matrix products: 50.9 us -> none  [the longest x4 21.6 us: sublayer(): jnp.dot(normed, attend, preferred_element_type=jnp.float32)]
    all_to_all x11 -> x3, waiting for transfers between devices: 54.6 us -> 4.01 us  [the longest x2 4 us: exchange(): lax.all_to_all(cut, axes, split_axis=0, concat_axis=0, tiled=True)]
    all_to_all x0 -> x2, blocking collectives: none -> 36.8 us  [the longest x1 19.5 us: body(): lax.all_to_all(space_part, 'z', split_axis=0, concat_axis=0, tiled=True)]
    all_to_all x11 -> x3, starting transfers between devices: 54.5 us -> 18.5 us  [the longest x2 14.9 us: exchange(): lax.all_to_all(cut, axes, split_axis=0, concat_axis=0, tiled=True)]
    pallas_call x0 -> x9, Pallas kernels: none -> 32.4 us  [the longest x2 14.2 us: backward(): pl.pallas_call(backward_kernel, out_shape=jax.ShapeDtypeStruct(grad.shape...]
    reduce_sum x17 -> x0, other arithmetic: 27.4 us -> none  [the longest x4 11 us: summed_share(): sent = jnp.sum(got.astype(jnp.float32), axis=0).astype(jnp.bfloat16)]
    unnamed x58 -> x50, local copies, waits for them, and re-layouts: 4.71 us -> 27.9 us
    all_gather x0 -> x1, blocking collectives: none -> 22.1 us  [routed(): aimed = lax.all_gather(aimed, OWNERS, axis=0, tiled=True)]
  transfers between devices with their start and end apart: 11 -> 9, of which waited for: 8 -> 2; matrix products, arithmetic and copies ran while one was open for 32% -> 1% of each run, Pallas kernels for 0% -> 17%
where the time goes in v2:
time: 171 us; the launch traced here: 170 us
  blocking collectives  58.9 us (34%)
  Pallas kernels  32.4 us (19%)
  local copies, waits for them, and re-layouts  31.3 us (18%)
  starting transfers between devices  25.5 us (15%)
  between operations  14.3 us (8%)
  waiting for transfers between devices  6.73 us (4%)
    unnamed x50, local copies, waits for them, and re-layouts  27.9 us
    all_gather x1, blocking collectives, routed(): aimed = lax.all_gather(aimed, OWNERS, axis=0, tiled=True)  22.1 us
    all_to_all x1, blocking collectives, body(): lax.all_to_all(space_part, 'z', split_axis=0, concat_axis=0, tiled=True)  19.5 us
    all_to_all x1, blocking collectives, exchange(): lax.all_to_all(cut, axes, split_axis=0, concat_axis=0, tiled=True)  17.4 us
    all_to_all x2, starting transfers between devices, exchange(): lax.all_to_all(cut, axes, split_axis=0, concat_axis=0, tiled=True)  14.9 us
    pallas_call x2, Pallas kernels, backward(): pl.pallas_call(backward_kernel, out_shape=jax.ShapeDtypeStruct(grad.shape...  14.2 us
    pallas_call x2, Pallas kernels, forward(): pl.pallas_call(lambda *refs: forward_kernel(temporal, *refs), out_shape=s...  11.1 us
    ppermute x5, starting transfers between devices, shift(): lax.ppermute(array, axis, [(i, (i + by) % devices) for i in range(devices)])  6.81 us
  transfers between devices with their start and end apart: 9, of which 2 were waited for; matrix products, arithmetic and copies ran while one was open for 1% of the time, Pallas kernels for 17%

profile of v2, /device:TPU:0, one launch (start us, length us, event | category | flops | bytes accessed | tf_op | source)
XLA Modules:
  0.0 169.7 jit_solution(8240490316761076653)
XLA Ops:
  7.2 2.1 %dynamic-slice_bitcast_fusion = bf16[4,64,1408]{2,1,0:T(8,128)(2,1)} fusion(bf16[4,2,64,1408]{3,2,1,0:T(8,128)(2,1)} %bitcast.51, s32[]{:T(128)S(6)} %select_n.71), kind=kLoop, calls=%fused_computation.1 | loop fusion | bytes 1441796 | tf_op jit(solution)/shard_map/jit(dynamic_index_in_dim)/squeeze | solution.py:281
  9.3 2.7 %copy-done = bf16[1408,2112]{0,1:T(8,128)(2,1)S(1)} copy-done((bf16[1408,2112]{0,1:T(8,128)(2,1)S(1)}, bf16[1408,2112]{0,1:T(8,128)(2,1)}, u32[]{:S(2)}) %copy-start) | copy-done | bytes 5947416
  12.0 1.5 copy-done.2
  13.5 6.0 %space_forward.1 = (bf16[256,2112]{1,0:T(8,128)(2,1)S(1)}, bf16[8,256,256]{2,1,0:T(8,128)(2,1)S(1)}, bf16[256,704]{1,0:T(8,128)(2,1)S(1)}, bf16[256,1408]{1,0:T(8,128)(2,1)}) custom-call(bf16[256,1408]{1,0:T(8,128)(2,1)S(1)} %bitcast.48, bf16[2112,1408]{1,0:T(8,128)(2,1)S(1)} %bitcast.35, bf16[704,1408]{1,0:T(8,128)(2,1)S(1)} %bitcast.37), custom_call_target="tpu_custom_call" | custom-call | flops 2200000000 | bytes 10000000 | tf_op jit(solution)/shard_map/space_forward/pallas_call | solution.py:93
  22.2 7.6 %all-to-all-start.1 = ((bf16[32,8,1408]{2,1,0:T(8,128)(2,1)}), bf16[32,8,1408]{2,1,0:T(8,128)(2,1)S(1)}, u32[]{:S(2)}, u32[]{:S(2)}) async-start(bf16[32,8,1408]{2,1,0:T(8,128)(2,1)} %bitcast.19), calls=%async_computation.1 | async-start | bytes 1441792 | tf_op jit(solution)/shard_map/all_to_all | solution.py:262
  30.0 1.3 dynamic-slice_bitcast_fusion.1
  31.4 2.0 %collective-permute-start.1 = (bf16[128,1408]{1,0:T(8,128)(2,1)S(1)}, bf16[128,1408]{1,0:T(8,128)(2,1)S(1)}, u32[]{:S(2)}, u32[]{:S(2)}) collective-permute-start(bf16[128,1408]{1,0:T(8,128)(2,1)S(1)} %pad_maximum_fusion.1), channel_id=1, source_target_pairs={{0,32},{32,64},{64,96},{96,0},{1,33},{33,65},{65,97},{97,1},{2,34}... | collective-permute-start | bytes 1081352 | tf_op jit(solution)/shard_map/ppermute | solution.py:267
  33.4 3.7 %collective-permute-start.2 = (bf16[128,1408]{1,0:T(8,128)(2,1)S(1)}, bf16[128,1408]{1,0:T(8,128)(2,1)S(1)}, u32[]{:S(2)}, u32[]{:S(2)}) collective-permute-start(bf16[128,1408]{1,0:T(8,128)(2,1)S(1)} %pad_maximum_fusion.2), channel_id=1, source_target_pairs={{0,64},{32,96},{64,0},{96,32},{1,65},{33,97},{65,1},{97,33},{2,66}... | collective-permute-start | bytes 1081352 | tf_op jit(solution)/shard_map/ppermute | solution.py:267
  37.1 1.1 collective-permute-start.3
  38.2 22.1 %all_gather.3.aimed_ref = s32[64,1,64]{2,1,0:T(1,128)S(1)} all-gather(s32[8,1,64]{2,1,0:T(1,128)S(1)} %compare_select_fusion), channel_id=1, replica_groups=mesh['z'=4,'core'=2,'space'=16] {'z','core'}, dimensions={0}, use_global_device_ids=true | all-gather | bytes 18432 | tf_op jit(solution)/shard_map/all_gather | solution.py:278
  60.5 2.4 %scatter_rows.1 = bf16[256,1408]{1,0:T(8,128)(2,1)} custom-call(s32[2]{0:T(128)S(1)} %pad_add_fusion.place_ref, s32[64,1,64]{2,1,0:T(1,128)S(1)} %all_gather.3.aimed_ref, bf16[128,1408]{1,0:T(8,128)(2,1)S(1)} %pad_maximum_fusion.refs_0_, bf16[128,1408]{1,0:T(8,128)(2,1)S(1)} %collective-permute-done.1.refs_1_, ...), custom_call_target="tpu_custom_call" | custom-call | flops 400000000 | bytes 10000000 | tf_op jit(solution)/shard_map/scatter_rows/pallas_call | solution.py:248
  62.8 7.3 %all-to-all-start = ((bf16[32,8,1408]{2,1,0:T(8,128)(2,1)}), bf16[32,8,1408]{2,1,0:T(8,128)(2,1)S(1)}, u32[]{:S(2)}, u32[]{:S(2)}) async-start(bf16[32,8,1408]{2,1,0:T(8,128)(2,1)} %bitcast.14), calls=%async_computation | async-start | bytes 1441792 | tf_op jit(solution)/shard_map/all_to_all | solution.py:262
  70.3 2.7 %copy-done.4 = bf16[1408,2112]{0,1:T(8,128)(2,1)S(1)} copy-done((bf16[1408,2112]{0,1:T(8,128)(2,1)S(1)}, bf16[1408,2112]{0,1:T(8,128)(2,1)}, u32[]{:S(2)}) %copy-start.4) | copy-done | bytes 5947416
  73.0 5.1 %time_forward.1 = (bf16[256,2112]{1,0:T(8,128)(2,1)S(1)}, bf16[8,256,256]{2,1,0:T(8,128)(2,1)S(1)}, bf16[256,704]{1,0:T(8,128)(2,1)S(1)}) custom-call(bf16[256,1408]{1,0:T(8,128)(2,1)S(1)} %bitcast.45, bf16[2112,1408]{1,0:T(8,128)(2,1)S(1)} %bitcast.43), custom_call_target="tpu_custom_call" | custom-call | flops 2200000000 | bytes 10000000 | tf_op jit(solution)/shard_map/time_forward/pallas_call | solution.py:93
  80.1 4.0 %all-to-all-done = bf16[32,8,1408]{2,1,0:T(8,128)(2,1)S(1)} async-done(((bf16[32,8,1408]{2,1,0:T(8,128)(2,1)}), bf16[32,8,1408]{2,1,0:T(8,128)(2,1)S(1)}, u32[]{:S(2)}, u32[]{:S(2)}) %all-to-all-start) | async-done | bytes 720928 | tf_op jit(solution)/shard_map/all_to_all | solution.py:262
  84.1 2.1 %time_weight.1 = bf16[1408,704]{1,0:T(8,128)(2,1)} custom-call(bf16[256,1408]{1,0:T(8,128)(2,1)S(1)} %bitcast.41, bf16[256,704]{1,0:T(8,128)(2,1)S(1)} %get-tuple-element.22.mixed_ref), custom_call_target="tpu_custom_call" | custom-call | tf_op jit(solution)/shard_map/time_weight/pallas_call | solution.py:150
  86.3 1.5 copy-done.10
  87.8 2.7 %copy-done.5 = bf16[1408,2112]{0,1:T(8,128)(2,1)S(1)} copy-done((bf16[1408,2112]{0,1:T(8,128)(2,1)S(1)}, bf16[1408,2112]{0,1:T(8,128)(2,1)}, u32[]{:S(2)}) %copy-start.5) | copy-done | bytes 5947416
  90.5 1.2 copy-done.14
  91.8 1.3 copy-done.18
  93.0 6.7 %time_backward.1 = bf16[256,1408]{1,0:T(8,128)(2,1)S(1)} custom-call(bf16[256,1408]{1,0:T(8,128)(2,1)S(1)} %bitcast.42, bf16[256,1408]{1,0:T(8,128)(2,1)S(1)} %bitcast.46, bf16[256,2112]{1,0:T(8,128)(2,1)S(1)} %copy-done.14, bf16[8,256,256]{2,1,0:T(8,128)(2,1)S(1)} %copy-done.18, bf16[2112,1408]{1,0:T(8,128)(2,1)S(1)} %bitcast.44, bf16[704,1408]{1,0:T(8,128)(2,1)S(1)} %bitcast.50), custom_call_target="tpu_custom_call" | custom-call | flops 2600000000 | bytes 10000000 | tf_op jit(solution)/shard_map/time_backward/pallas_call | solution.py:133
  99.7 17.4 %all_to_all.25 = bf16[32,8,1408]{2,1,0:T(8,128)(2,1)S(1)} all-to-all(bf16[32,8,1408]{2,1,0:T(8,128)(2,1)S(1)} %bitcast.47), channel_id=1, replica_groups=mesh['z'=4,'core'=2,'space'=16] {'core','space'}, dimensions={0} | all-to-all | bytes 1441792 | tf_op jit(solution)/shard_map/all_to_all | solution.py:262
  117.1 1.5 space_weight.1
  118.7 2.7 %collective-permute-done.4 = bf16[4,176,704]{2,1,0:T(8,128)(2,1)S(1)} collective-permute-done((bf16[4,176,704]{2,1,0:T(8,128)(2,1)S(1)}, bf16[4,176,704]{2,1,0:T(8,128)(2,1)S(1)}, u32[]{:S(2)}, u32[]{:S(2)}) %collective-permute-start.4) | collective-permute-done | bytes 991264 | tf_op jit(solution)/shard_map/ppermute | solution.py:267
  121.7 19.5 %all_to_all.26.space_ref = bf16[4,176,704]{2,1,0:T(8,128)(2,1)} all-to-all(bf16[4,176,704]{2,1,0:T(8,128)(2,1)S(1)} %add_convert_fusion), channel_id=1, replica_groups=mesh['z'=4,'core'=2,'space'=16] {'z'}, dimensions={0} | all-to-all | bytes 1982464 | tf_op jit(solution)/shard_map/all_to_all | solution.py:314
  141.1 1.4 copy-done.6
  144.6 3.6 %all-to-all-start.4 = ((bf16[16,16,1408]{2,1,0:T(8,128)(2,1)}), bf16[16,16,1408]{2,1,0:T(8,128)(2,1)S(1)}, u32[]{:S(2)}, u32[]{:S(2)}) async-start(bf16[16,16,1408]{2,1,0:T(8,128)(2,1)} %copy-done.7), calls=%async_computation.5 | async-start | bytes 1441792 | tf_op jit(solution)/shard_map/all_to_all | solution.py:316
  148.3 2.7 %copy-done.1 = bf16[1408,2112]{0,1:T(8,128)(2,1)S(1)} copy-done((bf16[1408,2112]{0,1:T(8,128)(2,1)S(1)}, bf16[1408,2112]{0,1:T(8,128)(2,1)}, u32[]{:S(2)}) %copy-start.1) | copy-done | bytes 5947416
  150.9 1.1 copy-done.9
  152.1 1.2 copy-done.12
  153.3 1.2 copy-done.16
  154.5 7.5 %space_backward.1 = bf16[256,1408]{1,0:T(8,128)(2,1)} custom-call(bf16[256,1408]{1,0:T(8,128)(2,1)S(1)} %bitcast.40, bf16[256,1408]{1,0:T(8,128)(2,1)S(1)} %bitcast.49, bf16[256,2112]{1,0:T(8,128)(2,1)S(1)} %copy-done.12, bf16[8,256,256]{2,1,0:T(8,128)(2,1)S(1)} %copy-done.16, bf16[2112,1408]{1,0:T(8,128)(2,1)S(1)} %bitcast.36, bf16[704,1408]{1,0:T(8,128)(2,1)S(1)} %bitcast.38), custom_call_target="tpu_custom_call" | custom-call | flops 2600000000 | bytes 10000000 | tf_op jit(solution)/shard_map/space_backward/pallas_call | solution.py:133
  (59 shorter events, 8.6 us)
Async XLA Ops:
  7.2 2.1 %copy-start.8 = (bf16[1,256,1408]{2,1,0:T(8,128)(2,1)S(1)}, bf16[1,256,1408]{2,1,0:T(8,128)(2,1)}, u32[]{:S(2)}) copy-start(bf16[1,256,1408]{2,1,0:T(8,128)(2,1)} %param.8) | copy-start | bytes 2162692
  9.3 20.8 %collective-permute-start = (bf16[4,64,1408]{2,1,0:T(8,128)(2,1)}, bf16[4,64,1408]{2,1,0:T(8,128)(2,1)}, u32[]{:S(2)}, u32[]{:S(2)}) collective-permute-start(bf16[4,64,1408]{2,1,0:T(8,128)(2,1)} %dynamic-slice_bitcast_fusion), channel_id=1, source_target_pairs={{0,16},{16,0},{1,17},{17,1},{2,18},{18,2},{3,19},{19,3},{4,20},{20... | collective-permute-start | bytes 2162696 | tf_op jit(solution)/shard_map/ppermute | solution.py:267
  9.3 2.7 %copy-start = (bf16[1408,2112]{0,1:T(8,128)(2,1)S(1)}, bf16[1408,2112]{0,1:T(8,128)(2,1)}, u32[]{:S(2)}) copy-start(bf16[1408,2112]{0,1:T(8,128)(2,1)} %param.12) | copy-start | bytes 17842180
  12.0 1.6 copy-start.2
  19.5 1.0 copy-start.11
  20.5 1.0 copy-start.15
  22.2 7.7 %copy-start.22 = (bf16[1,1,8,64,1408]{4,3,2,1,0:T(8,128)(2,1)S(1)}, bf16[1,1,8,64,1408]{4,3,2,1,0:T(8,128)(2,1)}, u32[]{:S(2)}) copy-start(bf16[1,1,8,64,1408]{4,3,2,1,0:T(8,128)(2,1)} %param.9) | copy-start | bytes 4325380
  22.2 40.6 %all-to-all-start.1 = ((bf16[32,8,1408]{2,1,0:T(8,128)(2,1)}), bf16[32,8,1408]{2,1,0:T(8,128)(2,1)S(1)}, u32[]{:S(2)}, u32[]{:S(2)}) async-start(bf16[32,8,1408]{2,1,0:T(8,128)(2,1)} %bitcast.19), calls=%async_computation.1 | async-start | bytes 1441792 | tf_op jit(solution)/shard_map/all_to_all | solution.py:262
  31.3 6.9 %copy-start.23 = (s32[1,1,8,64]{3,2,1,0:T(8,128)S(1)}, s32[1,1,8,64]{3,2,1,0:T(8,128)}, u32[]{:S(2)}) copy-start(s32[1,1,8,64]{3,2,1,0:T(8,128)} %param.10) | copy-start | bytes 6148
  31.3 6.8 %copy-start.24 = (s32[1,1,8]{2,1,0:T(1,128)S(1)}, s32[1,1,8]{2,1,0:T(1,128)}, u32[]{:S(2)}) copy-start(s32[1,1,8]{2,1,0:T(1,128)} %param.11) | copy-start | bytes 100
  31.4 29.1 %collective-permute-start.1 = (bf16[128,1408]{1,0:T(8,128)(2,1)S(1)}, bf16[128,1408]{1,0:T(8,128)(2,1)S(1)}, u32[]{:S(2)}, u32[]{:S(2)}) collective-permute-start(bf16[128,1408]{1,0:T(8,128)(2,1)S(1)} %pad_maximum_fusion.1), channel_id=1, source_target_pairs={{0,32},{32,64},{64,96},{96,0},{1,33},{33,65},{65,97},{97,1},{2,34}... | collective-permute-start | bytes 1081352 | tf_op jit(solution)/shard_map/ppermute | solution.py:267
  33.4 27.1 %collective-permute-start.2 = (bf16[128,1408]{1,0:T(8,128)(2,1)S(1)}, bf16[128,1408]{1,0:T(8,128)(2,1)S(1)}, u32[]{:S(2)}, u32[]{:S(2)}) collective-permute-start(bf16[128,1408]{1,0:T(8,128)(2,1)S(1)} %pad_maximum_fusion.2), channel_id=1, source_target_pairs={{0,64},{32,96},{64,0},{96,32},{1,65},{33,97},{65,1},{97,33},{2,66}... | collective-permute-start | bytes 1081352 | tf_op jit(solution)/shard_map/ppermute | solution.py:267
  37.1 23.4 %collective-permute-start.3 = (bf16[128,1408]{1,0:T(8,128)(2,1)S(1)}, bf16[128,1408]{1,0:T(8,128)(2,1)S(1)}, u32[]{:S(2)}, u32[]{:S(2)}) collective-permute-start(bf16[128,1408]{1,0:T(8,128)(2,1)S(1)} %pad_maximum_fusion.3), channel_id=1, source_target_pairs={{0,96},{32,0},{64,32},{96,64},{1,97},{33,1},{65,33},{97,65},{2,98}... | collective-permute-start | bytes 1081352 | tf_op jit(solution)/shard_map/ppermute | solution.py:267
  62.8 21.3 %all-to-all-start = ((bf16[32,8,1408]{2,1,0:T(8,128)(2,1)}), bf16[32,8,1408]{2,1,0:T(8,128)(2,1)S(1)}, u32[]{:S(2)}, u32[]{:S(2)}) async-start(bf16[32,8,1408]{2,1,0:T(8,128)(2,1)} %bitcast.14), calls=%async_computation | async-start | bytes 1441792 | tf_op jit(solution)/shard_map/all_to_all | solution.py:262
  70.1 71.0 %reduce-scatter.2.cloned.1.call-start = ((), (), s32[]{:S(2)}) async-start(), calls=%async_computation.6 | async-start | bytes 2433024 | tf_op jit(solution)/shard_map/reduce_scatter | solution.py:309
  70.3 2.7 %copy-start.4 = (bf16[1408,2112]{0,1:T(8,128)(2,1)S(1)}, bf16[1408,2112]{0,1:T(8,128)(2,1)}, u32[]{:S(2)}) copy-start(bf16[1408,2112]{0,1:T(8,128)(2,1)} %param.14) | copy-start | bytes 17842180
  78.1 1.0 copy-start.13
  79.1 1.0 copy-start.17
  86.3 1.6 copy-start.10
  87.8 2.7 %copy-start.5 = (bf16[1408,2112]{0,1:T(8,128)(2,1)S(1)}, bf16[1408,2112]{0,1:T(8,128)(2,1)}, u32[]{:S(2)}) copy-start(bf16[1408,2112]{0,1:T(8,128)(2,1)} %param.14) | copy-start | bytes 17842180
  90.5 1.2 copy-start.14
  91.7 1.3 copy-start.18
  99.7 17.4 %copy-start.20 = (bf16[256,704]{1,0:T(8,128)(2,1)S(1)}, bf16[256,704]{1,0:T(8,128)(2,1)}, u32[]{:S(2)}) copy-start(bf16[256,704]{1,0:T(8,128)(2,1)} %copy-done.19) | copy-start | bytes 1081348
  118.6 2.8 %collective-permute-start.4 = (bf16[4,176,704]{2,1,0:T(8,128)(2,1)S(1)}, bf16[4,176,704]{2,1,0:T(8,128)(2,1)S(1)}, u32[]{:S(2)}, u32[]{:S(2)}) collective-permute-start(bf16[4,176,704]{2,1,0:T(8,128)(2,1)S(1)} %get-tuple-element.21), channel_id=1, source_target_pairs={{0,16},{16,0},{1,17},{17,1},{2,18},{18,2},{3,19},{19,3},{4,20},{20... | collective-permute-start | bytes 2973704 | tf_op jit(solution)/shard_map/ppermute | solution.py:267
  141.1 7.1 %copy-start.3 = (bf16[1408,704]{0,1:T(8,128)(2,1)S(1)}, bf16[1408,704]{0,1:T(8,128)(2,1)}, u32[]{:S(2)}) copy-start(bf16[1408,704]{0,1:T(8,128)(2,1)} %param.13) | copy-start | bytes 5947396
  141.1 1.4 copy-start.6
  142.5 1.0 copy-start.21
  144.6 17.4 %all-to-all-start.4 = ((bf16[16,16,1408]{2,1,0:T(8,128)(2,1)}), bf16[16,16,1408]{2,1,0:T(8,128)(2,1)S(1)}, u32[]{:S(2)}, u32[]{:S(2)}) async-start(bf16[16,16,1408]{2,1,0:T(8,128)(2,1)} %copy-done.7), calls=%async_computation.5 | async-start | bytes 1441792 | tf_op jit(solution)/shard_map/all_to_all | solution.py:316
  148.3 2.7 %copy-start.1 = (bf16[1408,2112]{0,1:T(8,128)(2,1)S(1)}, bf16[1408,2112]{0,1:T(8,128)(2,1)}, u32[]{:S(2)}) copy-start(bf16[1408,2112]{0,1:T(8,128)(2,1)} %param.12) | copy-start | bytes 17842180
  150.9 1.1 copy-start.9
  152.1 1.2 copy-start.12
  153.3 1.2 copy-start.16
  (2 other events, 1.6 us)
Sparse Core Ops, SparseCore 0:
  86.4 31.2 reduce-scatter.1

commit v3 on v2

v3 whole, which is shorter than its diff:
```python
import jax, jax.numpy as jnp
from jax import lax
from jax.experimental import pallas as pl
from jax.experimental.pallas import tpu as pltpu
from jax.sharding import Mesh
from jax.sharding import PartitionSpec as P

HEADS = 8
HEAD = 88
EPS = 1e-05
PATCHES = 8
WIDE = HEADS * HEAD
CLIP = ("core", "space")
OWNERS = ("z", "core")
VMEM = pl.BlockSpec(memory_space=pltpu.VMEM)
SMEM = pl.BlockSpec(memory_space=pltpu.SMEM)


LIMIT = pltpu.CompilerParams(vmem_limit_bytes=16 * 2**20)


def cost(flops):
    return pl.CostEstimate(flops=int(flops), bytes_accessed=10_000_000, transcendentals=600_000)


def normalise(stream):
    widened = stream.astype(jnp.float32)
    center = jnp.mean(widened, axis=-1, keepdims=True)
    centered = widened - center
    variance = jnp.mean(centered * centered, axis=-1, keepdims=True)
    scale = lax.rsqrt(variance + EPS)
    return centered * scale, scale


def dot_nt(a, b):
    return lax.dot_general(a, b, (((1,), (1,)), ((), ())), preferred_element_type=jnp.float32)


def dot_tn(a, b):
    return lax.dot_general(a, b, (((0,), (0,)), ((), ())), preferred_element_type=jnp.float32)


def dot_nn(a, b):
    return jnp.dot(a, b, preferred_element_type=jnp.float32)


def same_patch(tokens):
    row = lax.broadcasted_iota(jnp.int32, (tokens, tokens), 0)
    column = lax.broadcasted_iota(jnp.int32, (tokens, tokens), 1)
    return (row % PATCHES) == (column % PATCHES)


def head(projected_ref, part, h):
    at = (part * HEADS + h) * HEAD
    return projected_ref[:, at : at + HEAD]


def forward_kernel(temporal, stream_ref, attend_ref, *rest):
    if temporal:
        projected_ref, probs_ref, mixed_ref = rest
    else:
        output_ref, projected_ref, probs_ref, mixed_ref, out_ref = rest
    tokens = stream_ref.shape[0]
    normed = normalise(stream_ref[...])[0].astype(jnp.bfloat16)
    projected_ref[...] = dot_nt(normed, attend_ref[...]).astype(jnp.bfloat16)
    for h in range(HEADS):
        scores = dot_nt(head(projected_ref, 0, h), head(projected_ref, 1, h)) * HEAD**-0.5
        if temporal:
            scores = jnp.where(same_patch(tokens), scores, -jnp.inf)
        weights = jnp.exp(scores - jnp.max(scores, axis=-1, keepdims=True))
        probs = (weights / jnp.sum(weights, axis=-1, keepdims=True)).astype(jnp.bfloat16)
        probs_ref[h] = probs
        mixed_ref[:, h * HEAD : (h + 1) * HEAD] = dot_nn(probs, head(projected_ref, 2, h)).astype(
            jnp.bfloat16
        )
    if not temporal:
        branch = dot_nn(mixed_ref[...], output_ref[...])
        out_ref[...] = (stream_ref[...].astype(jnp.float32) + branch).astype(jnp.bfloat16)


def forward(stream, attend, output=None):
    temporal = output is None
    tokens, width = stream.shape
    bf = jnp.bfloat16
    shapes = [
        jax.ShapeDtypeStruct((tokens, 3 * HEADS * HEAD), bf),
        jax.ShapeDtypeStruct((HEADS, tokens, tokens), bf),
        jax.ShapeDtypeStruct((tokens, HEADS * HEAD), bf),
    ]
    args = [stream, attend.T]
    if not temporal:
        shapes.append(jax.ShapeDtypeStruct((tokens, width), bf))
        args.append(output.T)
    return pl.pallas_call(
        lambda *refs: forward_kernel(temporal, *refs),
        out_shape=shapes,
        in_specs=[VMEM] * len(args),
        out_specs=[VMEM] * len(shapes),
        compiler_params=LIMIT,
        cost_estimate=cost(2.2e9),
        name="time_forward" if temporal else "space_forward",
    )(*args)


def backward_kernel(grad_ref, stream_ref, projected_ref, probs_ref, attend_ref, output_ref, out_ref, dproj_ref):
    bf = jnp.bfloat16
    grad = grad_ref[...]
    dmixed = dot_nt(grad, output_ref[...]).astype(bf)
    for h in range(HEADS):
        probs = probs_ref[h]
        dm = dmixed[:, h * HEAD : (h + 1) * HEAD]
        dprobs = dot_nt(dm, head(projected_ref, 2, h)).astype(bf).astype(jnp.float32)
        wide = probs.astype(jnp.float32)
        scaled = wide * dprobs
        dscores = (scaled - wide * jnp.sum(scaled, axis=-1, keepdims=True)) * HEAD**-0.5
        dscores = dscores.astype(bf)
        for part, value in (
            (0, dot_nn(dscores, head(projected_ref, 1, h))),
            (1, dot_tn(dscores, head(projected_ref, 0, h))),
            (2, dot_tn(probs, dm)),
        ):
            at = (part * HEADS + h) * HEAD
            dproj_ref[:, at : at + HEAD] = value.astype(bf)
    dnormed = dot_nn(dproj_ref[...], attend_ref[...]).astype(bf).astype(jnp.float32)
    normed, scale = normalise(stream_ref[...])
    mean_d = jnp.mean(dnormed, axis=-1, keepdims=True)
    mean_dn = jnp.mean(dnormed * normed, axis=-1, keepdims=True)
    inner = scale * (dnormed - mean_d - normed * mean_dn)
    out_ref[...] = (grad.astype(jnp.float32) + inner).astype(bf)


def backward(grad, stream, projected, probs, attend, output, name):
    args = [grad, stream, projected, probs, attend.T, output.T]
    return pl.pallas_call(
        backward_kernel,
        out_shape=jax.ShapeDtypeStruct(grad.shape, jnp.bfloat16),
        in_specs=[VMEM] * len(args),
        out_specs=VMEM,
        scratch_shapes=[pltpu.VMEM(projected.shape, jnp.bfloat16)],
        compiler_params=LIMIT,
        cost_estimate=cost(2.6e9),
        name=name,
    )(*args)


def call(kernel, outs, args, name, smem=0, flops=1e9, scratch=()):
    return pl.pallas_call(
        kernel,
        out_shape=outs,
        in_specs=[SMEM] * smem + [VMEM] * (len(args) - smem),
        out_specs=[VMEM] * len(outs) if isinstance(outs, list) else VMEM,
        scratch_shapes=scratch,
        compiler_params=LIMIT,
        cost_estimate=cost(flops),
        name=name,
    )(*args)


def bf16(*shape):
    return jax.ShapeDtypeStruct(shape, jnp.bfloat16)


def aim_kernel(place_ref, counts_ref, targets_ref, rows_ref, *piece_refs):
    chips = len(piece_refs)
    for d, piece_ref in enumerate(piece_refs):
        to = (place_ref[0] + d) % chips
        piece_ref[:128, :] = rows_ref[to]
        piece_ref[128:, :] = jnp.zeros((16, piece_ref.shape[1]), jnp.bfloat16)
        line = lax.broadcasted_iota(jnp.int32, (16, 64), 0)
        slot = lax.broadcasted_iota(jnp.int32, (16, 64), 1)
        aims = jnp.zeros((16, 64), jnp.int32)
        for core in range(2):
            valid = (line == core) & (slot < counts_ref[2 * to + core])
            row = jnp.where(valid, targets_ref[2 * to + core], -1)
            aims = jnp.where(line == core, row, aims)
        piece_ref[128:, :64] = aims.astype(jnp.float32).astype(jnp.bfloat16)


def scatter_kernel(place_ref, *refs):
    pieces, (mine_ref, other_ref) = refs[:-2], refs[-2:]
    tokens = mine_ref.shape[0]
    line = lax.broadcasted_iota(jnp.int32, (16, 64), 0)
    token = lax.broadcasted_iota(jnp.int32, (tokens, 64), 0).astype(jnp.float32)
    for out_ref, core in ((mine_ref, place_ref[1]), (other_ref, 1 - place_ref[1])):
        total = jnp.zeros(out_ref.shape, jnp.float32)
        for piece_ref in pieces:
            info = piece_ref[128:, :64].astype(jnp.float32)
            aims = jnp.sum(jnp.where(line == core, info, 0.0), axis=0, keepdims=True)
            matches = jnp.where(aims == token, 1.0, 0.0).astype(jnp.bfloat16)
            at = pl.multiple_of(core * 64, 64)
            total = total + dot_nn(matches, piece_ref[pl.ds(at, 64), :])
        out_ref[...] = total.astype(jnp.bfloat16)


def split_kernel(chips, place_ref, grad_ref, mine_ref, other_ref):
    grad = grad_ref[...]
    step = grad.shape[1] // (2 * chips)
    halves = [
        jnp.concatenate([grad[:, (2 * z + c) * step : (2 * z + c + 1) * step] for z in range(chips)], axis=1)
        for c in range(2)
    ]
    first = place_ref[1] == 0
    mine_ref[...] = jnp.where(first, halves[0], halves[1])
    other_ref[...] = jnp.where(first, halves[1], halves[0])


def split(place, grad, chips, name):
    half = bf16(grad.shape[0], grad.shape[1] // 2)
    return call(lambda *refs: split_kernel(chips, *refs), [half, half], [place, grad], name, smem=1)


def chip_product_kernel(grad_ref, mixed_ref, got_ref, out_ref):
    tokens = grad_ref.shape[0]
    total = dot_tn(grad_ref[...], mixed_ref[...]) + dot_tn(got_ref[:tokens, :], got_ref[tokens:, :])
    out_ref[...] = total.astype(jnp.bfloat16)


SHARE = 11
CUT = 640


def pack_kernel(time_ref, grad_ref, grad_got_ref, mixed_ref, mixed_got_ref, out_ref):
    space = dot_tn(grad_ref[...], mixed_ref[...]) + dot_tn(grad_got_ref[...], mixed_got_ref[...])
    time = time_ref[...].astype(jnp.float32)
    main = jnp.concatenate([time[:, :CUT], space[:, :384]], axis=1)
    left = jnp.concatenate([space[:, 384:CUT], time[:, CUT:], space[:, CUT:]], axis=1)
    zero = jnp.zeros((2, 128), jnp.float32)
    for k in range(out_ref.shape[0]):
        x = left[k * SHARE : (k + 1) * SHARE, :]
        cut = [x[:, 128 * t : 128 * (t + 1)] for t in range(3)]
        low = [part[5 * u : 5 * u + 5] for part in cut for u in range(2)]
        low.append(jnp.concatenate([part[10:] for part in cut] + [zero], axis=0))
        low.append(jnp.zeros((5, 128), jnp.float32))
        rows = [main[k * SHARE : (k + 1) * SHARE, :], jnp.concatenate(low, axis=1)]
        out_ref[k] = jnp.concatenate(rows, axis=0).astype(jnp.bfloat16)


def unpack_kernel(parts_ref, space_ref, time_ref):
    total = parts_ref[0].astype(jnp.float32)
    for k in range(1, parts_ref.shape[0]):
        total = total + parts_ref[k].astype(jnp.float32)
    low = [total[SHARE:, 128 * t : 128 * (t + 1)] for t in range(7)]
    left = [
        jnp.concatenate([low[2 * t], low[2 * t + 1], low[6][t : t + 1]], axis=0) for t in range(3)
    ]
    time_ref[...] = jnp.concatenate([total[:SHARE, :CUT], left[2][:, :64]], axis=1)
    space_ref[...] = jnp.concatenate([total[:SHARE, CUT:], left[0], left[1], left[2][:, 64:]], axis=1)


def exchange(tokens, axes):
    devices = lax.axis_size(axes)
    cut = tokens.reshape(devices, tokens.shape[0] // devices, tokens.shape[1])
    return lax.all_to_all(cut, axes, split_axis=0, concat_axis=0, tiled=True).reshape(tokens.shape)


def shift(array, axis, by):
    devices = lax.axis_size(axis)
    return lax.ppermute(array, axis, [(i, (i + by) % devices) for i in range(devices)])


def routed(grad_rows, targets, counts, place, tokens):
    chips = lax.axis_size("z")
    width = grad_rows.shape[4]
    args = [place, counts.reshape(-1), targets.reshape(2 * chips, 1, 64), grad_rows.reshape(chips, 128, width)]
    pieces = call(aim_kernel, [bf16(144, width)] * chips, args, "aim_rows", smem=2)
    pieces = [piece if d == 0 else shift(piece, "z", d) for d, piece in enumerate(pieces)]
    mine, other = call(scatter_kernel, [bf16(tokens, width)] * 2, [place, *pieces], "scatter_rows", smem=1)
    return mine + shift(other, "core", 1)


def body(
    video_tokens, grad_rows, targets, counts, attend_space, output_space, attend_time, output_time
):
    chips = lax.axis_size("z")
    stream = video_tokens[0]
    width = stream.shape[1]
    place = jnp.stack([lax.axis_index("z"), lax.axis_index("core")]).astype(jnp.int32)
    grad_out = routed(grad_rows, targets, counts, place, stream.shape[0])
    space_saved = forward(stream, attend_space, output_space)
    hidden = exchange(space_saved[3], CLIP)
    grad = exchange(grad_out, CLIP)
    time_saved = forward(hidden, attend_time)
    space_mixed_got = shift(space_saved[2], "core", 1)
    time_mine, time_other = split(place, grad, chips, "time_split")
    time_got = shift(jnp.concatenate([time_other, time_saved[2]], axis=0), "core", 1)
    grad_hidden = backward(
        grad, hidden, time_saved[0], time_saved[1], attend_time, output_time, "time_backward"
    )
    time_sum = call(
        chip_product_kernel, bf16(width // 2, WIDE), [time_mine, time_saved[2], time_got], "time_weight"
    )
    grad_hidden = exchange(grad_hidden, CLIP)
    space_mine, space_other = split(place, grad_hidden, chips, "space_split")
    space_got = shift(space_other, "core", 1)
    keepers = lax.axis_size(("z", "space"))
    packed = call(
        pack_kernel,
        bf16(keepers, 16, 1024),
        [time_sum, space_mine, space_got, space_saved[2], space_mixed_got],
        "pack_shares",
    )
    packed = lax.all_to_all(packed, ("z", "space"), split_axis=0, concat_axis=0, tiled=True)
    share = jax.ShapeDtypeStruct((SHARE, WIDE), jnp.float32)
    space_grad, time_grad = call(unpack_kernel, [share, share], [packed], "sum_shares")
    token_grad = backward(
        grad_hidden, stream, space_saved[0], space_saved[1], attend_space, output_space, "space_backward"
    )
    return (token_grad[None], space_grad, time_grad)


def solution(mesh):
    chips = mesh.shape["tm"] // 2
    fine = Mesh(mesh.devices.reshape(chips, 2, mesh.shape["space"]), ("z", "core", "space"))
    whole = ("z", "core", "space")
    in_specs = (
        P(whole, None, None),
        P(OWNERS, "space", None, None, None),
        P(OWNERS, "space", None, None),
        P(OWNERS, "space", None),
        P(),
        P(),
        P(),
        P(),
    )
    out_specs = (P(whole, None, None), P(whole, None), P(whole, None))
    return jax.shard_map(body, mesh=fine, in_specs=in_specs, out_specs=out_specs, check_vma=False)
```

time: 171 us -> 159 us (0.930)
  blocking collectives: 58.9 us -> 0 us
  waiting for transfers between devices: 6.73 us -> 61.1 us
  between operations: 14.3 us -> 0.84 us
  Pallas kernels: 32.4 us -> 38.1 us
  local copies, waits for them, and re-layouts: 31.3 us -> 27.3 us
  starting transfers between devices: 25.5 us -> 28.8 us
    all_to_all x2 -> x0, blocking collectives: 36.8 us -> none  [the longest x1 19.5 us: body(): lax.all_to_all(space_part, 'z', split_axis=0, concat_axis=0, tiled=True)]
    all_to_all x2 -> x3, waiting for transfers between devices: 4 us -> 26.9 us  [exchange(): lax.all_to_all(cut, axes, split_axis=0, concat_axis=0, tiled=True)]
    all_gather x1 -> x0, blocking collectives: 22.1 us -> none  [routed(): aimed = lax.all_gather(aimed, OWNERS, axis=0, tiled=True)]
    all_to_all x1, waiting for transfers between devices: 0.01 us -> 17.3 us  [body(): lax.all_to_all(packed, ('z', 'space'), split_axis=0, concat_axis=0, tiled...]
    ppermute x5 -> x7, waiting for transfers between devices: 2.7 us -> 16.8 us  [shift(): lax.ppermute(array, axis, [(i, (i + by) % devices) for i in range(devices)])]
    pallas_call x5 -> x7, Pallas kernels: 7.1 us -> 12 us  [call(): pl.pallas_call(kernel, out_shape=outs, in_specs=[SMEM] * smem + [VMEM] *...]
    squeeze x3 -> x0, local copies, waits for them, and re-layouts: 3.42 us -> none  [the longest x1 2.1 us: of_core(): return lax.dynamic_index_in_dim(rows, which, axis=1, keepdims=False)]
    unnamed x50 -> x48, local copies, waits for them, and re-layouts: 27.9 us -> 24.8 us
  transfers between devices with their start and end apart: 9 -> 11, of which waited for: 2 -> 6; matrix products, arithmetic and copies ran while one was open for 1% -> 3% of each run, Pallas kernels for 17% -> 14%
where the time goes in v3:
time: 159 us; the launch traced here: 158 us
  waiting for transfers between devices  61.1 us (38%)
  Pallas kernels  38.1 us (24%)
  starting transfers between devices  28.8 us (18%)
  local copies, waits for them, and re-layouts  27.3 us (17%)
  other arithmetic  2.2 us (1%)
    all_to_all x3, waiting for transfers between devices, exchange(): lax.all_to_all(cut, axes, split_axis=0, concat_axis=0, tiled=True)  26.9 us
    unnamed x48, local copies, waits for them, and re-layouts  24.8 us
    all_to_all x1, waiting for transfers between devices, body(): lax.all_to_all(packed, ('z', 'space'), split_axis=0, concat_axis=0, tiled...  17.3 us
    ppermute x7, waiting for transfers between devices, shift(): lax.ppermute(array, axis, [(i, (i + by) % devices) for i in range(devices)])  16.8 us
    all_to_all x3, starting transfers between devices, exchange(): lax.all_to_all(cut, axes, split_axis=0, concat_axis=0, tiled=True)  15.4 us
    pallas_call x2, Pallas kernels, backward(): pl.pallas_call(backward_kernel, out_shape=jax.ShapeDtypeStruct(grad.shape...  15.1 us
    pallas_call x7, Pallas kernels, call(): pl.pallas_call(kernel, out_shape=outs, in_specs=[SMEM] * smem + [VMEM] *...  12 us
    pallas_call x2, Pallas kernels, forward(): pl.pallas_call(lambda *refs: forward_kernel(temporal, *refs), out_shape=s...  11 us
  transfers between devices with their start and end apart: 11, of which 6 were waited for; matrix products, arithmetic and copies ran while one was open for 3% of the time, Pallas kernels for 14%

profile of v3, /device:TPU:0, one launch (start us, length us, event | category | flops | bytes accessed | tf_op | source)
XLA Modules:
  0.0 158.4 jit_solution(3726371453268230761)
XLA Ops:
  0.7 1.4 copy-done.19
  4.1 2.1 %collective-permute-start = (bf16[144,1408]{1,0:T(8,128)(2,1)S(1)}, bf16[144,1408]{1,0:T(8,128)(2,1)S(1)}, u32[]{:S(2)}, u32[]{:S(2)}) collective-permute-start(bf16[144,1408]{1,0:T(8,128)(2,1)S(1)} %get-tuple-element.23), channel_id=1, source_target_pairs={{0,32},{32,64},{64,96},{96,0},{1,33},{33,65},{65,97},{97,1},{2,34}... | collective-permute-start | bytes 1216520 | tf_op jit(solution)/shard_map/ppermute | solution.py:258
  6.2 3.6 %collective-permute-start.1 = (bf16[144,1408]{1,0:T(8,128)(2,1)S(1)}, bf16[144,1408]{1,0:T(8,128)(2,1)S(1)}, u32[]{:S(2)}, u32[]{:S(2)}) collective-permute-start(bf16[144,1408]{1,0:T(8,128)(2,1)S(1)} %get-tuple-element.24), channel_id=1, source_target_pairs={{0,64},{32,96},{64,0},{96,32},{1,65},{33,97},{65,1},{97,33},{2,66}... | collective-permute-start | bytes 1216520 | tf_op jit(solution)/shard_map/ppermute | solution.py:258
  10.7 6.9 %collective-permute-done.refs_1_ = bf16[144,1408]{1,0:T(8,128)(2,1)S(1)} collective-permute-done((bf16[144,1408]{1,0:T(8,128)(2,1)S(1)}, bf16[144,1408]{1,0:T(8,128)(2,1)S(1)}, u32[]{:S(2)}, u32[]{:S(2)}) %collective-permute-start) | collective-permute-done | bytes 405536 | tf_op jit(solution)/shard_map/ppermute | solution.py:258
  17.7 9.9 %collective-permute-done.1.refs_2_ = bf16[144,1408]{1,0:T(8,128)(2,1)S(1)} collective-permute-done((bf16[144,1408]{1,0:T(8,128)(2,1)S(1)}, bf16[144,1408]{1,0:T(8,128)(2,1)S(1)}, u32[]{:S(2)}, u32[]{:S(2)}) %collective-permute-start.1) | collective-permute-done | bytes 405536 | tf_op jit(solution)/shard_map/ppermute | solution.py:258
  27.5 2.2 %scatter_rows.1 = (bf16[256,1408]{1,0:T(8,128)(2,1)S(1)}, bf16[256,1408]{1,0:T(8,128)(2,1)S(1)}) custom-call(s32[2]{0:T(128)S(1)} %pad_add_fusion.place_ref.refs_0_, bf16[144,1408]{1,0:T(8,128)(2,1)S(1)} %get-tuple-element.22.refs_0_, bf16[144,1408]{1,0:T(8,128)(2,1)S(1)} %collective-permute-done.refs_1_, ...), custom_call_target="tpu_custom_call" | custom-call | flops 1000000000 | bytes 10000000 | tf_op jit(solution)/shard_map/scatter_rows/pallas_call | solution.py:147
  29.8 1.5 copy-done.2
  31.4 6.0 %space_forward.1 = (bf16[256,2112]{1,0:T(8,128)(2,1)S(1)}, bf16[8,256,256]{2,1,0:T(8,128)(2,1)S(1)}, bf16[256,704]{1,0:T(8,128)(2,1)S(1)}, bf16[256,1408]{1,0:T(8,128)(2,1)}) custom-call(bf16[256,1408]{1,0:T(8,128)(2,1)S(1)} %bitcast.30, bf16[2112,1408]{1,0:T(8,128)(2,1)S(1)} %bitcast.18, bf16[704,1408]{1,0:T(8,128)(2,1)S(1)} %bitcast.20), custom_call_target="tpu_custom_call" | custom-call | flops 2200000000 | bytes 10000000 | tf_op jit(solution)/shard_map/space_forward/pallas_call | solution.py:94
  40.1 7.4 %all-to-all-start.1 = ((bf16[32,8,1408]{2,1,0:T(8,128)(2,1)}), bf16[32,8,1408]{2,1,0:T(8,128)(2,1)S(1)}, u32[]{:S(2)}, u32[]{:S(2)}) async-start(bf16[32,8,1408]{2,1,0:T(8,128)(2,1)} %bitcast.10), calls=%async_computation.1 | async-start | bytes 1441792 | tf_op jit(solution)/shard_map/all_to_all | solution.py:253
  47.5 2.0 %add_bitcast_fusion = bf16[32,8,1408]{2,1,0:T(8,128)(2,1)} fusion(bf16[256,1408]{1,0:T(8,128)(2,1)S(1)} %get-tuple-element.26, bf16[256,1408]{1,0:T(8,128)(2,1)} %collective-permute-done.3), kind=kLoop, calls=%fused_computation.1 | loop fusion | flops 360448 | bytes 2162688 | tf_op jit(solution)/shard_map/reshape | solution.py:252
  49.6 12.0 %all-to-all-done.1 = bf16[32,8,1408]{2,1,0:T(8,128)(2,1)S(1)} async-done(((bf16[32,8,1408]{2,1,0:T(8,128)(2,1)}), bf16[32,8,1408]{2,1,0:T(8,128)(2,1)S(1)}, u32[]{:S(2)}, u32[]{:S(2)}) %all-to-all-start.1) | async-done | bytes 720928 | tf_op jit(solution)/shard_map/all_to_all | solution.py:253
  61.5 4.1 %all-to-all-start = ((bf16[32,8,1408]{2,1,0:T(8,128)(2,1)}), bf16[32,8,1408]{2,1,0:T(8,128)(2,1)S(1)}, u32[]{:S(2)}, u32[]{:S(2)}) async-start(bf16[32,8,1408]{2,1,0:T(8,128)(2,1)} %add_bitcast_fusion), calls=%async_computation | async-start | bytes 1441792 | tf_op jit(solution)/shard_map/all_to_all | solution.py:253
  65.7 2.7 %copy-done.4 = bf16[1408,2112]{0,1:T(8,128)(2,1)S(1)} copy-done((bf16[1408,2112]{0,1:T(8,128)(2,1)S(1)}, bf16[1408,2112]{0,1:T(8,128)(2,1)}, u32[]{:S(2)}) %copy-start.4) | copy-done | bytes 5947416
  68.3 5.1 %time_forward.1 = (bf16[256,2112]{1,0:T(8,128)(2,1)S(1)}, bf16[8,256,256]{2,1,0:T(8,128)(2,1)S(1)}, bf16[256,704]{1,0:T(8,128)(2,1)S(1)}) custom-call(bf16[256,1408]{1,0:T(8,128)(2,1)S(1)} %bitcast.26, bf16[2112,1408]{1,0:T(8,128)(2,1)S(1)} %bitcast.22), custom_call_target="tpu_custom_call" | custom-call | flops 2200000000 | bytes 10000000 | tf_op jit(solution)/shard_map/time_forward/pallas_call | solution.py:94
  75.2 4.3 %all-to-all-done = bf16[32,8,1408]{2,1,0:T(8,128)(2,1)S(1)} async-done(((bf16[32,8,1408]{2,1,0:T(8,128)(2,1)}), bf16[32,8,1408]{2,1,0:T(8,128)(2,1)S(1)}, u32[]{:S(2)}, u32[]{:S(2)}) %all-to-all-start) | async-done | bytes 720928 | tf_op jit(solution)/shard_map/all_to_all | solution.py:253
  79.5 2.7 %copy-done.5 = bf16[1408,2112]{0,1:T(8,128)(2,1)S(1)} copy-done((bf16[1408,2112]{0,1:T(8,128)(2,1)S(1)}, bf16[1408,2112]{0,1:T(8,128)(2,1)}, u32[]{:S(2)}) %copy-start.5) | copy-done | bytes 5947416
  82.2 1.5 copy-done.7
  83.7 1.2 copy-done.13
  84.9 7.5 %time_backward.1 = bf16[256,1408]{1,0:T(8,128)(2,1)} custom-call(bf16[256,1408]{1,0:T(8,128)(2,1)S(1)} %bitcast.28, bf16[256,1408]{1,0:T(8,128)(2,1)S(1)} %bitcast.27, bf16[256,2112]{1,0:T(8,128)(2,1)S(1)} %get-tuple-element.29.projected_ref, bf16[8,256,256]{2,1,0:T(8,128)(2,1)S(1)} %copy-done.13, bf16[2112,1408]{1,0:T(8,128)(2,1)S(1)} %bitcast.23, ...), custom_call_target="tpu_custom_call" | custom-call | flops 2600000000 | bytes 10000000 | tf_op jit(solution)/shard_map/time_backward/pallas_call | solution.py:134
  92.5 3.9 %all-to-all-start.2 = ((bf16[32,8,1408]{2,1,0:T(8,128)(2,1)}), bf16[32,8,1408]{2,1,0:T(8,128)(2,1)S(1)}, u32[]{:S(2)}, u32[]{:S(2)}) async-start(bf16[32,8,1408]{2,1,0:T(8,128)(2,1)} %bitcast.14), calls=%async_computation.2 | async-start | bytes 1441792 | tf_op jit(solution)/shard_map/all_to_all | solution.py:253
  98.1 1.1 copy.11
  99.7 10.7 %all-to-all-done.2 = bf16[32,8,1408]{2,1,0:T(8,128)(2,1)S(1)} async-done(((bf16[32,8,1408]{2,1,0:T(8,128)(2,1)}), bf16[32,8,1408]{2,1,0:T(8,128)(2,1)S(1)}, u32[]{:S(2)}, u32[]{:S(2)}) %all-to-all-start.2) | async-done | bytes 720928 | tf_op jit(solution)/shard_map/all_to_all | solution.py:253
  110.4 1.6 space_split.1
  112.0 1.4 copy.12.got_ref
  116.2 3.4 %pack_shares.1 = bf16[64,16,1024]{2,1,0:T(8,128)(2,1)} custom-call(bf16[704,704]{1,0:T(8,128)(2,1)S(1)} %time_weight.1.time_ref, bf16[256,704]{1,0:T(8,128)(2,1)S(1)} %get-tuple-element.36.grad_ref, bf16[256,704]{1,0:T(8,128)(2,1)} %collective-permute-done.5.grad_got_ref, bf16[256,704]{1,0:T(8,128)(2,1)S(1)} %copy-done.15, ...), custom_call_target="tpu_custom_call" | custom-call | flops 1000000000 | bytes 10000000 | tf_op jit(solution)/shard_map/pack_shares/pallas_call | solution.py:147
  119.6 6.2 %all-to-all-start.3 = ((bf16[64,16,1024]{2,1,0:T(8,128)(2,1)}), bf16[64,16,1024]{2,1,0:T(8,128)(2,1)}, u32[]{:S(2)}, u32[]{:S(2)}) async-start(bf16[64,16,1024]{2,1,0:T(8,128)(2,1)} %pack_shares.1), calls=%async_computation.3 | async-start | bytes 4194304 | tf_op jit(solution)/shard_map/all_to_all | solution.py:302
  125.8 2.7 %copy-done.1 = bf16[1408,2112]{0,1:T(8,128)(2,1)S(1)} copy-done((bf16[1408,2112]{0,1:T(8,128)(2,1)S(1)}, bf16[1408,2112]{0,1:T(8,128)(2,1)}, u32[]{:S(2)}) %copy-start.1) | copy-done | bytes 5947416
  128.5 1.2 copy-done.9
  129.7 1.2 copy-done.11
  131.0 7.5 %space_backward.1 = bf16[256,1408]{1,0:T(8,128)(2,1)} custom-call(bf16[256,1408]{1,0:T(8,128)(2,1)S(1)} %bitcast.25, bf16[256,1408]{1,0:T(8,128)(2,1)S(1)} %bitcast.31, bf16[256,2112]{1,0:T(8,128)(2,1)S(1)} %copy-done.9, bf16[8,256,256]{2,1,0:T(8,128)(2,1)S(1)} %copy-done.11, bf16[2112,1408]{1,0:T(8,128)(2,1)S(1)} %bitcast.19, bf16[704,1408]{1,0:T(8,128)(2,1)S(1)} %bitcast.21), custom_call_target="tpu_custom_call" | custom-call | flops 2600000000 | bytes 10000000 | tf_op jit(solution)/shard_map/space_backward/pallas_call | solution.py:134
  138.5 17.3 %all-to-all-done.3.parts_ref = bf16[64,16,1024]{2,1,0:T(8,128)(2,1)} async-done(((bf16[64,16,1024]{2,1,0:T(8,128)(2,1)}), bf16[64,16,1024]{2,1,0:T(8,128)(2,1)}, u32[]{:S(2)}, u32[]{:S(2)}) %all-to-all-start.3) | async-done | bytes 2097184 | tf_op jit(solution)/shard_map/all_to_all | solution.py:302
  155.8 2.5 %sum_shares.1 = (f32[11,704]{1,0:T(8,128)}, f32[11,704]{1,0:T(8,128)}) custom-call(bf16[64,16,1024]{2,1,0:T(8,128)(2,1)} %all-to-all-done.3.parts_ref), custom_call_target="tpu_custom_call" | custom-call | flops 1000000000 | bytes 10000000 | tf_op jit(solution)/shard_map/sum_shares/pallas_call | solution.py:147
  (54 shorter events, 12.6 us)
Async XLA Ops:
  0.7 1.4 copy-start.19
  3.4 26.4 %copy-start = (bf16[1408,2112]{0,1:T(8,128)(2,1)S(1)}, bf16[1408,2112]{0,1:T(8,128)(2,1)}, u32[]{:S(2)}) copy-start(bf16[1408,2112]{0,1:T(8,128)(2,1)} %param.12) | copy-start | bytes 17842180
  4.1 13.6 %collective-permute-start = (bf16[144,1408]{1,0:T(8,128)(2,1)S(1)}, bf16[144,1408]{1,0:T(8,128)(2,1)S(1)}, u32[]{:S(2)}, u32[]{:S(2)}) collective-permute-start(bf16[144,1408]{1,0:T(8,128)(2,1)S(1)} %get-tuple-element.23), channel_id=1, source_target_pairs={{0,32},{32,64},{64,96},{96,0},{1,33},{33,65},{65,97},{97,1},{2,34}... | collective-permute-start | bytes 1216520 | tf_op jit(solution)/shard_map/ppermute | solution.py:258
  6.2 21.4 %collective-permute-start.1 = (bf16[144,1408]{1,0:T(8,128)(2,1)S(1)}, bf16[144,1408]{1,0:T(8,128)(2,1)S(1)}, u32[]{:S(2)}, u32[]{:S(2)}) collective-permute-start(bf16[144,1408]{1,0:T(8,128)(2,1)S(1)} %get-tuple-element.24), channel_id=1, source_target_pairs={{0,64},{32,96},{64,0},{96,32},{1,65},{33,97},{65,1},{97,33},{2,66}... | collective-permute-start | bytes 1216520 | tf_op jit(solution)/shard_map/ppermute | solution.py:258
  9.7 17.8 %collective-permute-start.2 = (bf16[144,1408]{1,0:T(8,128)(2,1)S(1)}, bf16[144,1408]{1,0:T(8,128)(2,1)S(1)}, u32[]{:S(2)}, u32[]{:S(2)}) collective-permute-start(bf16[144,1408]{1,0:T(8,128)(2,1)S(1)} %get-tuple-element.25), channel_id=1, source_target_pairs={{0,96},{32,0},{64,32},{96,64},{1,97},{33,1},{65,33},{97,65},{2,98}... | collective-permute-start | bytes 1216520 | tf_op jit(solution)/shard_map/ppermute | solution.py:258
  27.5 2.3 %copy-start.6 = (bf16[1,256,1408]{2,1,0:T(8,128)(2,1)S(1)}, bf16[1,256,1408]{2,1,0:T(8,128)(2,1)}, u32[]{:S(2)}) copy-start(bf16[1,256,1408]{2,1,0:T(8,128)(2,1)} %param.8) | copy-start | bytes 2162692
  29.7 17.8 %collective-permute-start.3 = (bf16[256,1408]{1,0:T(8,128)(2,1)S(1)}, bf16[256,1408]{1,0:T(8,128)(2,1)}, u32[]{:S(2)}, u32[]{:S(2)}) collective-permute-start(bf16[256,1408]{1,0:T(8,128)(2,1)S(1)} %get-tuple-element.27), channel_id=1, source_target_pairs={{0,16},{16,0},{1,17},{17,1},{2,18},{18,2},{3,19},{19,3},{4,20},{20... | collective-permute-start | bytes 2162696 | tf_op jit(solution)/shard_map/ppermute | solution.py:258
  29.8 1.6 copy-start.2
  37.4 1.0 copy-start.8
  38.4 1.0 copy-start.10
  39.4 0.7 copy-start.14
  40.1 21.4 %all-to-all-start.1 = ((bf16[32,8,1408]{2,1,0:T(8,128)(2,1)}), bf16[32,8,1408]{2,1,0:T(8,128)(2,1)S(1)}, u32[]{:S(2)}, u32[]{:S(2)}) async-start(bf16[32,8,1408]{2,1,0:T(8,128)(2,1)} %bitcast.10), calls=%async_computation.1 | async-start | bytes 1441792 | tf_op jit(solution)/shard_map/all_to_all | solution.py:253
  61.5 17.9 %all-to-all-start = ((bf16[32,8,1408]{2,1,0:T(8,128)(2,1)}), bf16[32,8,1408]{2,1,0:T(8,128)(2,1)S(1)}, u32[]{:S(2)}, u32[]{:S(2)}) async-start(bf16[32,8,1408]{2,1,0:T(8,128)(2,1)} %add_bitcast_fusion), calls=%async_computation | async-start | bytes 1441792 | tf_op jit(solution)/shard_map/all_to_all | solution.py:253
  65.6 2.7 %copy-start.4 = (bf16[1408,2112]{0,1:T(8,128)(2,1)S(1)}, bf16[1408,2112]{0,1:T(8,128)(2,1)}, u32[]{:S(2)}) copy-start(bf16[1408,2112]{0,1:T(8,128)(2,1)} %param.14) | copy-start | bytes 17842180
  73.4 1.0 copy-start.12
  79.5 2.7 %copy-start.5 = (bf16[1408,2112]{0,1:T(8,128)(2,1)S(1)}, bf16[1408,2112]{0,1:T(8,128)(2,1)}, u32[]{:S(2)}) copy-start(bf16[1408,2112]{0,1:T(8,128)(2,1)} %param.14) | copy-start | bytes 17842180
  82.2 1.6 copy-start.7
  83.7 1.2 copy-start.13
  92.5 17.9 %all-to-all-start.2 = ((bf16[32,8,1408]{2,1,0:T(8,128)(2,1)}), bf16[32,8,1408]{2,1,0:T(8,128)(2,1)S(1)}, u32[]{:S(2)}, u32[]{:S(2)}) async-start(bf16[32,8,1408]{2,1,0:T(8,128)(2,1)} %bitcast.14), calls=%async_computation.2 | async-start | bytes 1441792 | tf_op jit(solution)/shard_map/all_to_all | solution.py:253
  96.4 1.6 %copy-start.17 = (bf16[256,704]{1,0:T(8,128)(2,1)S(1)}, bf16[256,704]{1,0:T(8,128)(2,1)}, u32[]{:S(2)}) copy-start(bf16[256,704]{1,0:T(8,128)(2,1)} %copy-done.16) | copy-start | bytes 1081348
  97.2 0.8 copy-start.22
  98.0 1.5 copy-start.15
  99.2 12.8 %collective-permute-start.4 = (bf16[512,704]{0,1:T(8,128)(2,1)}, bf16[512,704]{0,1:T(8,128)(2,1)}, u32[]{:S(2)}, u32[]{:S(2)}) collective-permute-start(bf16[512,704]{0,1:T(8,128)(2,1)} %copy.11), channel_id=1, source_target_pairs={{0,16},{16,0},{1,17},{17,1},{2,18},{18,2},{3,19},{19,3},{4,20},{20... | collective-permute-start | bytes 2162696 | tf_op jit(solution)/shard_map/ppermute | solution.py:258
  99.5 16.6 %collective-permute-start.6 = (bf16[256,704]{1,0:T(8,128)(2,1)S(1)}, bf16[256,704]{1,0:T(8,128)(2,1)S(1)}, u32[]{:S(2)}, u32[]{:S(2)}) collective-permute-start(bf16[256,704]{1,0:T(8,128)(2,1)S(1)} %copy-done.15), channel_id=1, source_target_pairs={{0,16},{16,0},{1,17},{17,1},{2,18},{18,2},{3,19},{19,3},{4,20},{20... | collective-permute-start | bytes 1081352 | tf_op jit(solution)/shard_map/ppermute | solution.py:258
  112.0 4.2 %collective-permute-start.5 = (bf16[256,704]{1,0:T(8,128)(2,1)}, bf16[256,704]{1,0:T(8,128)(2,1)}, u32[]{:S(2)}, u32[]{:S(2)}) collective-permute-start(bf16[256,704]{1,0:T(8,128)(2,1)} %get-tuple-element.37), channel_id=1, source_target_pairs={{0,16},{16,0},{1,17},{17,1},{2,18},{18,2},{3,19},{19,3},{4,20},{20... | collective-permute-start | bytes 1081352 | tf_op jit(solution)/shard_map/ppermute | solution.py:258
  113.4 1.0 copy-start.18
  114.4 1.0 copy-start.23
  119.6 6.2 %copy-start.3 = (bf16[1408,704]{0,1:T(8,128)(2,1)S(1)}, bf16[1408,704]{0,1:T(8,128)(2,1)}, u32[]{:S(2)}) copy-start(bf16[1408,704]{0,1:T(8,128)(2,1)} %param.13) | copy-start | bytes 5947396
  119.6 36.2 %all-to-all-start.3 = ((bf16[64,16,1024]{2,1,0:T(8,128)(2,1)}), bf16[64,16,1024]{2,1,0:T(8,128)(2,1)}, u32[]{:S(2)}, u32[]{:S(2)}) async-start(bf16[64,16,1024]{2,1,0:T(8,128)(2,1)} %pack_shares.1), calls=%async_computation.3 | async-start | bytes 4194304 | tf_op jit(solution)/shard_map/all_to_all | solution.py:302
  125.8 2.7 %copy-start.1 = (bf16[1408,2112]{0,1:T(8,128)(2,1)S(1)}, bf16[1408,2112]{0,1:T(8,128)(2,1)}, u32[]{:S(2)}) copy-start(bf16[1408,2112]{0,1:T(8,128)(2,1)} %param.12) | copy-start | bytes 17842180
  128.5 1.2 copy-start.9
  129.7 1.2 copy-start.11
  (3 other events, 2.1 us)

commit v4 on v3

v4 whole, which is shorter than its diff:
```python
import jax
import jax.numpy as jnp
from jax import lax
from jax.experimental import pallas as pl
from jax.experimental.pallas import tpu as pltpu
from jax.sharding import Mesh
from jax.sharding import PartitionSpec as P

HEADS = 8
HEAD = 88
WIDE = HEADS * HEAD
EPS = 1e-05
PATCHES = 8
SHARE = 11
CUT = 640
CLIP = ("core", "space")
OWNERS = ("z", "core")
ATTEND_CUTS = ((0, 768), (768, 1344))
VMEM = pl.BlockSpec(memory_space=pltpu.VMEM)
SMEM = pl.BlockSpec(memory_space=pltpu.SMEM)
ANY = pl.BlockSpec(memory_space=pl.ANY)


def bf16(*shape):
    return jax.ShapeDtypeStruct(shape, jnp.bfloat16)


def held(*shape):
    return pltpu.VMEM(shape, jnp.bfloat16)


def call(kernel, outs, args, name, spaces, scratch=(), flops=1e6, room=20):
    spec = {"s": SMEM, "v": VMEM, "a": ANY}
    spaces = [spec[c] for c in spaces]
    many = isinstance(outs, list)
    return pl.pallas_call(
        kernel,
        out_shape=outs,
        in_specs=spaces[: len(args)],
        out_specs=spaces[len(args) :] if many else spaces[-1],
        scratch_shapes=scratch,
        compiler_params=pltpu.CompilerParams(vmem_limit_bytes=room * 2**20),
        cost_estimate=pl.CostEstimate(
            flops=int(flops), bytes_accessed=int(flops / 200), transcendentals=0
        ),
        name=name,
    )(*args)


def normalise(stream):
    widened = stream.astype(jnp.float32)
    center = jnp.mean(widened, axis=-1, keepdims=True)
    centered = widened - center
    variance = jnp.mean(centered * centered, axis=-1, keepdims=True)
    scale = lax.rsqrt(variance + EPS)
    return centered * scale, scale


def dot_nt(a, b):
    return lax.dot_general(a, b, (((1,), (1,)), ((), ())), preferred_element_type=jnp.float32)


def dot_tn(a, b):
    return lax.dot_general(a, b, (((0,), (0,)), ((), ())), preferred_element_type=jnp.float32)


def dot_nn(a, b):
    return jnp.dot(a, b, preferred_element_type=jnp.float32)


def same_patch(tokens):
    row = lax.broadcasted_iota(jnp.int32, (tokens, tokens), 0)
    column = lax.broadcasted_iota(jnp.int32, (tokens, tokens), 1)
    return (row % PATCHES) == (column % PATCHES)


def head(projected_ref, part, h):
    at = (part * HEADS + h) * HEAD
    return projected_ref[:, at : at + HEAD]


def forward_kernel(temporal, *refs):
    if temporal:
        stream_in, attend_in, projected_out, probs_out, mixed_out = refs[:5]
        stream, attend, projected, probs, mixed, sems = refs[5:]
    else:
        stream_in, attend_in, output_in, projected_out, probs_out, mixed_out, result_out = refs[:7]
        stream, attend, projected, probs, mixed, output, result, sems = refs[7:]

    def copy(source, target, at):
        return pltpu.make_async_copy(source, target, sems.at[at])

    load = copy(stream_in, stream, 0)
    load.start()
    parts = [
        copy(attend_in.at[pl.ds(a, n)], attend.at[pl.ds(a, n)], 1 + i)
        for i, (a, n) in enumerate(ATTEND_CUTS)
    ]
    for part in parts:
        part.start()
    if not temporal:
        load_output = copy(output_in, output, 4)
        load_output.start()
    load.wait()
    normed = normalise(stream[...])[0].astype(jnp.bfloat16)
    for part, (a, n) in zip(parts, ATTEND_CUTS):
        part.wait()
        projected[:, a : a + n] = dot_nt(normed, attend[a : a + n, :]).astype(jnp.bfloat16)
    stores = [copy(projected, projected_out, 5)]
    stores[0].start()
    tokens = stream.shape[0]
    if temporal:
        allowed = same_patch(tokens)
    for h in range(HEADS):
        scores = dot_nt(head(projected, 0, h), head(projected, 1, h)) * HEAD**-0.5
        if temporal:
            scores = jnp.where(allowed, scores, -jnp.inf)
        weights = jnp.exp(scores - jnp.max(scores, axis=-1, keepdims=True))
        chances = (weights / jnp.sum(weights, axis=-1, keepdims=True)).astype(jnp.bfloat16)
        probs[h] = chances
        mixed[:, h * HEAD : (h + 1) * HEAD] = dot_nn(chances, head(projected, 2, h)).astype(
            jnp.bfloat16
        )
    stores += [copy(mixed, mixed_out, 6), copy(probs, probs_out, 8)]
    stores[1].start()
    stores[2].start()
    if not temporal:
        load_output.wait()
        branch = dot_nn(mixed[...], output[...])
        result[...] = (stream[...].astype(jnp.float32) + branch).astype(jnp.bfloat16)
        stores.append(copy(result, result_out, 7))
        stores[-1].start()
    for store in stores:
        store.wait()


def forward(stream, attend, output=None):
    temporal = output is None
    tokens, width = stream.shape
    shapes = [(tokens, 3 * WIDE), (HEADS, tokens, tokens), (tokens, WIDE)]
    outs = [bf16(*shape) for shape in shapes]
    scratch = [held(tokens, width), held(3 * WIDE, width)] + [held(*shape) for shape in shapes]
    args = [stream, attend.T]
    if not temporal:
        args.append(output.T)
        outs.append(bf16(tokens, width))
        scratch += [held(WIDE, width), held(tokens, width)]
    scratch.append(pltpu.SemaphoreType.DMA((16,)))
    name = "time_forward" if temporal else "space_forward"
    spaces = "a" * (len(args) + len(outs))
    return call(lambda *refs: forward_kernel(temporal, *refs), outs, args, name, spaces, scratch, 2.2e9, 60)


def backward_kernel(
    grad_in, stream_in, projected_in, probs_in, attend_in, output_in, result_out,
    grad, stream, projected, probs, attend, output, result, dproj, sems,
):
    bf = jnp.bfloat16

    def copy(source, target, at):
        return pltpu.make_async_copy(source, target, sems.at[at])

    load_grad, load_output = copy(grad_in, grad, 0), copy(output_in, output, 1)
    load_projected = copy(projected_in, projected, 2)
    load_probs = copy(probs_in, probs, 7)
    load_attend, load_stream = copy(attend_in, attend, 3), copy(stream_in, stream, 4)
    for load in (load_grad, load_output, load_projected, load_probs, load_attend, load_stream):
        load.start()
    load_grad.wait()
    load_output.wait()
    dmixed = dot_nt(grad[...], output[...]).astype(bf)
    load_projected.wait()
    load_probs.wait()
    for h in range(HEADS):
        chances = probs[h]
        dm = dmixed[:, h * HEAD : (h + 1) * HEAD]
        dprobs = dot_nt(dm, head(projected, 2, h)).astype(bf).astype(jnp.float32)
        wide = chances.astype(jnp.float32)
        scaled = wide * dprobs
        dscores = (scaled - wide * jnp.sum(scaled, axis=-1, keepdims=True)) * HEAD**-0.5
        dscores = dscores.astype(bf)
        for part, value in (
            (0, dot_nn(dscores, head(projected, 1, h))),
            (1, dot_tn(dscores, head(projected, 0, h))),
            (2, dot_tn(chances, dm)),
        ):
            at = (part * HEADS + h) * HEAD
            dproj[:, at : at + HEAD] = value.astype(bf)
    load_attend.wait()
    load_stream.wait()
    tokens = grad.shape[0]
    for i in range(2):
        rows = slice(i * tokens // 2, (i + 1) * tokens // 2)
        dnormed = dot_nn(dproj[rows, :], attend[...]).astype(bf).astype(jnp.float32)
        normed, scale = normalise(stream[rows, :])
        mean_d = jnp.mean(dnormed, axis=-1, keepdims=True)
        mean_dn = jnp.mean(dnormed * normed, axis=-1, keepdims=True)
        inner = scale * (dnormed - mean_d - normed * mean_dn)
        result[rows, :] = (grad[rows, :].astype(jnp.float32) + inner).astype(bf)
    store = copy(result, result_out, 5)
    store.start()
    store.wait()


def backward(grad, stream, projected, probs, attend, output, name):
    args = [grad, stream, projected, probs, attend.T, output.T]
    scratch = [held(*arg.shape) for arg in args] + [held(*grad.shape), held(*projected.shape)]
    scratch.append(pltpu.SemaphoreType.DMA((16,)))
    return call(backward_kernel, bf16(*grad.shape), args, name, "a" * 7, scratch, 2.6e9, 60)


def aim_kernel(place_ref, counts_ref, targets_in, rows_in, *refs):
    piece_refs, (targets, sems) = refs[:-2], refs[-2:]
    chips = len(piece_refs)
    aimed = pltpu.make_async_copy(targets_in, targets, sems.at[chips])
    aimed.start()
    loads = []
    for d in range(chips):
        to = (place_ref[0] + d) % chips
        into = piece_refs[d].at[pl.ds(0, 128)]
        loads.append(pltpu.make_async_copy(rows_in.at[to], into, sems.at[d]))
        loads[-1].start()
    aimed.wait()
    line = lax.broadcasted_iota(jnp.int32, (16, 64), 0)
    slot = lax.broadcasted_iota(jnp.int32, (16, 64), 1)
    for d, piece_ref in enumerate(piece_refs):
        to = (place_ref[0] + d) % chips
        piece_ref[128:, :] = jnp.zeros((16, piece_ref.shape[1]), jnp.bfloat16)
        aims = jnp.full((16, 64), -1, jnp.int32)
        for core in range(2):
            valid = (line == core) & (slot < counts_ref[0, 0, 2 * to + core])
            aims = jnp.where(valid, targets[0, 0, pl.ds(2 * to + core, 1), :], aims)
        piece_ref[128:, :64] = aims.astype(jnp.float32).astype(jnp.bfloat16)
    for load in loads:
        load.wait()


def scatter_kernel(chips, place_ref, *refs):
    pieces, mine_ref, other_refs = refs[:chips], refs[chips], refs[chips + 1 :]
    tokens = mine_ref.shape[0]
    line = lax.broadcasted_iota(jnp.int32, (16, 64), 0)
    token = lax.broadcasted_iota(jnp.int32, (tokens, 64), 0).astype(jnp.float32)
    for out_refs, core in ((other_refs, 1 - place_ref[1]), ((mine_ref,), place_ref[1])):
        total = jnp.zeros(mine_ref.shape, jnp.float32)
        for piece_ref in pieces:
            info = piece_ref[128:, :64].astype(jnp.float32)
            aims = jnp.sum(jnp.where(line == core, info, 0.0), axis=0, keepdims=True)
            matches = jnp.where(aims == token, 1.0, 0.0).astype(jnp.bfloat16)
            at = pl.multiple_of(core * 64, 64)
            total = total + dot_nn(matches, piece_ref[pl.ds(at, 64), :])
        step = tokens // len(out_refs)
        for i, out_ref in enumerate(out_refs):
            out_ref[...] = total[i * step : (i + 1) * step].astype(jnp.bfloat16)


def join_kernel(mine_ref, *refs):
    got_refs, out_ref = refs[:-1], refs[-1]
    step = mine_ref.shape[0] // len(got_refs)
    for i, got_ref in enumerate(got_refs):
        rows = slice(i * step, (i + 1) * step)
        out_ref[rows, :] = mine_ref[rows, :] + got_ref[...]


def halves_of(grad, chips):
    step = grad.shape[1] // (2 * chips)
    return [
        jnp.concatenate([grad[:, (2 * z + c) * step : (2 * z + c + 1) * step] for z in range(chips)], axis=1)
        for c in range(2)
    ]


def split_kernel(chips, place_ref, grad_ref, *refs):
    mine_ref, other_ref = refs[-2:]
    halves = halves_of(grad_ref[...], chips)
    first = place_ref[1] == 0
    half = mine_ref.shape[1]
    mine_ref[...] = jnp.where(first, halves[0], halves[1])
    other_ref[:, :half] = jnp.where(first, halves[1], halves[0])
    if len(refs) == 3:
        other_ref[:, half:] = refs[0][...]


def chip_product_kernel(grad_ref, mixed_ref, got_ref, out_ref):
    half = grad_ref.shape[1]
    total = dot_tn(grad_ref[...], mixed_ref[...]) + dot_tn(got_ref[:, :half], got_ref[:, half:])
    out_ref[...] = total.astype(jnp.bfloat16)


def pack_kernel(time_in, grad_in, grad_got_in, mixed_in, mixed_got_in, packed_out, *scratch):
    time_ref, grad, grad_got, mixed, mixed_got, packed, sems = scratch
    loads = [
        pltpu.make_async_copy(source, target, sems.at[i])
        for i, (source, target) in enumerate(
            ((mixed_in, mixed), (grad_in, grad), (mixed_got_in, mixed_got), (grad_got_in, grad_got), (time_in, time_ref))
        )
    ]
    for load in loads:
        load.start()
    for load in loads:
        load.wait()
    space = dot_tn(grad[...], mixed[...]) + dot_tn(grad_got[...], mixed_got[...])
    time = time_ref[...].astype(jnp.float32)
    main = jnp.concatenate([time[:, :CUT], space[:, :384]], axis=1)
    left = jnp.concatenate([space[:, 384:CUT], time[:, CUT:], space[:, CUT:]], axis=1)
    zero = jnp.zeros((2, 128), jnp.float32)
    blocks, stores = packed.shape[0], []
    for k in range(blocks):
        x = left[k * SHARE : (k + 1) * SHARE, :]
        cut = [x[:, 128 * t : 128 * (t + 1)] for t in range(3)]
        low = [part[5 * u : 5 * u + 5] for part in cut for u in range(2)]
        low.append(jnp.concatenate([part[10:] for part in cut] + [zero], axis=0))
        low.append(jnp.zeros((5, 128), jnp.float32))
        rows = [main[k * SHARE : (k + 1) * SHARE, :], jnp.concatenate(low, axis=1)]
        packed[k] = jnp.concatenate(rows, axis=0).astype(jnp.bfloat16)
        if (k + 1) % 16 == 0:
            at = pl.ds(k - 15, 16)
            stores.append(pltpu.make_async_copy(packed.at[at], packed_out.at[at], sems.at[5 + k // 16]))
            stores[-1].start()
    for store in stores:
        store.wait()


def pack(arrays, blocks):
    scratch = [held(*array.shape) for array in arrays]
    scratch += [held(blocks, 16, 1024), pltpu.SemaphoreType.DMA((5 + blocks // 16,))]
    return call(pack_kernel, bf16(blocks, 16, 1024), arrays, "pack_shares", "aaaaaa", scratch)


def unpack_kernel(parts_ref, space_ref, time_ref):
    total = parts_ref[0].astype(jnp.float32)
    for k in range(1, parts_ref.shape[0]):
        total = total + parts_ref[k].astype(jnp.float32)
    low = [total[SHARE:, 128 * t : 128 * (t + 1)] for t in range(7)]
    left = [
        jnp.concatenate([low[2 * t], low[2 * t + 1], low[6][t : t + 1]], axis=0) for t in range(3)
    ]
    time_ref[...] = jnp.concatenate([total[:SHARE, :CUT], left[2][:, :64]], axis=1)
    space_ref[...] = jnp.concatenate([total[:SHARE, CUT:], left[0], left[1], left[2][:, 64:]], axis=1)


def exchange(tokens, axes):
    devices = lax.axis_size(axes)
    cut = tokens.reshape(devices, tokens.shape[0] // devices, tokens.shape[1])
    return lax.all_to_all(cut, axes, split_axis=0, concat_axis=0, tiled=True).reshape(tokens.shape)


def shift(array, axis, by):
    devices = lax.axis_size(axis)
    return lax.ppermute(array, axis, [(i, (i + by) % devices) for i in range(devices)])


def after(array, *others):
    return lax.optimization_barrier((array, *others))[0]


def body(
    video_tokens, grad_rows, targets, counts, attend_space, output_space, attend_time, output_time
):
    chips = lax.axis_size("z")
    stream = video_tokens[0]
    tokens, width = stream.shape
    place = jnp.stack([lax.axis_index("z"), lax.axis_index("core")]).astype(jnp.int32)

    args = [place, counts, targets, grad_rows.reshape(chips, 128, width)]
    scratch = [pltpu.VMEM(targets.shape, jnp.int32), pltpu.SemaphoreType.DMA((chips + 1,))]
    pieces = call(aim_kernel, [bf16(144, width)] * chips, args, "aim_rows", "ssaa" + "v" * chips, scratch, room=60)
    pieces = [piece if d == 0 else shift(piece, "z", d) for d, piece in enumerate(pieces)]

    space_saved = forward(stream, attend_space, output_space)
    hidden = exchange(space_saved[3], CLIP)

    place = after(place, space_saved[3])
    args = [place, *pieces]
    cuts = 2
    outs = [bf16(tokens, width)] + [bf16(tokens // cuts, width)] * cuts
    mine, *others = call(
        lambda *refs: scatter_kernel(chips, *refs), outs, args, "scatter_rows", "s" + "v" * (chips + 1 + cuts)
    )
    args = [mine] + [shift(other, "core", 1) for other in others]
    grad_out = call(join_kernel, bf16(tokens, width), args, "join_rows", "v" * (cuts + 2))
    grad = exchange(grad_out, CLIP)
    time_saved = forward(hidden, attend_time)
    space_mixed_got = shift(space_saved[2], "core", 1)
    grad_hidden = backward(
        grad, hidden, time_saved[0], time_saved[1], attend_time, output_time, "time_backward"
    )
    time_halves = [bf16(tokens, width // 2), bf16(tokens, width)]
    time_mine, time_other = call(
        lambda *refs: split_kernel(chips, *refs),
        time_halves,
        [after(place, grad_hidden), grad, time_saved[2]],
        "time_split",
        "svvvv",
    )
    time_got = shift(time_other, "core", 1)
    args = [time_mine, time_saved[2], time_got]
    time_sum = call(chip_product_kernel, bf16(width // 2, WIDE), args, "time_weight", "vvvv")

    grad_hidden = exchange(grad_hidden, CLIP)
    half = bf16(tokens, width // 2)
    space_mine, space_other = call(
        lambda *refs: split_kernel(chips, *refs),
        [half, half],
        [after(place, time_sum), grad_hidden],
        "space_split",
        "svvv",
    )
    space_got = shift(space_other, "core", 1)
    packed = pack(
        [time_sum, space_mine, space_got, space_saved[2], space_mixed_got],
        lax.axis_size(("z", "space")),
    )
    packed = lax.all_to_all(packed, ("z", "space"), split_axis=0, concat_axis=0, tiled=True)
    share = jax.ShapeDtypeStruct((SHARE, WIDE), jnp.float32)
    space_grad, time_grad = call(unpack_kernel, [share, share], [packed], "sum_shares", "vvv")
    token_grad = backward(
        grad_hidden, stream, space_saved[0], space_saved[1], attend_space, output_space, "space_backward"
    )
    return (token_grad[None], space_grad, time_grad)


def solution(mesh):
    chips = mesh.shape["tm"] // 2
    fine = Mesh(mesh.devices.reshape(chips, 2, mesh.shape["space"]), ("z", "core", "space"))
    whole = ("z", "core", "space")
    in_specs = (
        P(whole, None, None),
        P(OWNERS, "space", None, None, None),
        P(OWNERS, "space", None, None),
        P(OWNERS, "space", None),
        P(),
        P(),
        P(),
        P(),
    )
    out_specs = (P(whole, None, None), P(whole, None), P(whole, None))
    return jax.shard_map(body, mesh=fine, in_specs=in_specs, out_specs=out_specs, check_vma=False)
```

time: 159 us -> 134 us (0.84)
  local copies, waits for them, and re-layouts: 27.3 us -> 3.72 us
  Pallas kernels: 38.1 us -> 51.7 us
  waiting for transfers between devices: 61.1 us -> 48.7 us
    unnamed x48 -> x20, local copies, waits for them, and re-layouts: 24.8 us -> 3.72 us
    pallas_call x11 -> x12, Pallas kernels: 38.1 us -> 51.7 us  [call(): pl.pallas_call(kernel, out_shape=outs, in_specs=spaces[:len(args)], out_s...]
    ppermute x7 -> x8, waiting for transfers between devices: 16.8 us -> 3.97 us  [shift(): lax.ppermute(array, axis, [(i, (i + by) % devices) for i in range(devices)])]
    all_to_all x1, waiting for transfers between devices: 17.3 us -> 19.9 us  [body(): lax.all_to_all(packed, ('z', 'space'), split_axis=0, concat_axis=0, tiled...]
    all_to_all x3, waiting for transfers between devices: 26.9 us -> 24.8 us  [exchange(): lax.all_to_all(cut, axes, split_axis=0, concat_axis=0, tiled=True)]
    reshape x1 -> x0, other arithmetic: 2.05 us -> none  [exchange(): cut = tokens.reshape(devices, tokens.shape[0] // devices, tokens.shape[1])]
    ppermute x7 -> x8, starting transfers between devices: 7.26 us -> 7.92 us  [shift(): lax.ppermute(array, axis, [(i, (i + by) % devices) for i in range(devices)])]
  transfers between devices with their start and end apart: 11 -> 12, of which waited for: 6 -> 8; matrix products, arithmetic and copies ran while one was open for 3% -> 0% of each run, Pallas kernels for 14% -> 24%
where the time goes in v4:
time: 134 us
  Pallas kernels  51.7 us (39%)
  waiting for transfers between devices  48.7 us (36%)
  starting transfers between devices  28 us (21%)
  local copies, waits for them, and re-layouts  3.72 us (3%)
    pallas_call x12, Pallas kernels, call(): pl.pallas_call(kernel, out_shape=outs, in_specs=spaces[:len(args)], out_s...  51.7 us
    all_to_all x3, waiting for transfers between devices, exchange(): lax.all_to_all(cut, axes, split_axis=0, concat_axis=0, tiled=True)  24.8 us
    all_to_all x1, waiting for transfers between devices, body(): lax.all_to_all(packed, ('z', 'space'), split_axis=0, concat_axis=0, tiled...  19.9 us
    all_to_all x3, starting transfers between devices, exchange(): lax.all_to_all(cut, axes, split_axis=0, concat_axis=0, tiled=True)  15.3 us
    ppermute x8, starting transfers between devices, shift(): lax.ppermute(array, axis, [(i, (i + by) % devices) for i in range(devices)])  7.92 us
    all_to_all x1, starting transfers between devices, body(): lax.all_to_all(packed, ('z', 'space'), split_axis=0, concat_axis=0, tiled...  4.7 us
    ppermute x8, waiting for transfers between devices, shift(): lax.ppermute(array, axis, [(i, (i + by) % devices) for i in range(devices)])  3.97 us
    unnamed x20, local copies, waits for them, and re-layouts  3.72 us
  transfers between devices with their start and end apart: 12, of which 8 were waited for; matrix products, arithmetic and copies ran while one was open for 0% of the time, Pallas kernels for 24%

profile of v4, /device:TPU:0, one launch (start us, length us, event | category | flops | bytes accessed | tf_op | source)
XLA Modules:
  0.0 133.6 jit_solution(7980104673672641436)
XLA Ops:
  0.6 0.7 pad_add_fusion.place_ref.refs_0_
  1.3 3.2 %aim_rows.1 = (bf16[144,1408]{1,0:T(8,128)(2,1)}, bf16[144,1408]{1,0:T(8,128)(2,1)}, bf16[144,1408]{1,0:T(8,128)(2,1)}, bf16[144,1408]{1,0:T(8,128)(2,1)}) custom-call(s32[2]{0:T(128)} %pad_add_fusion.place_ref.refs_0_, s32[1,1,8]{2,1,0:T(1,128)} %counts_ref.1, s32[1,1,8,64]{3,2,1,0:T(8,128)} %targets_in.1, bf16[4,128,1408]{2,1,0:T(8,128)(2,1)} %bitcast.31), custom_call_target="tpu_custom_call" | custom-call | flops 1000000 | bytes 5000 | tf_op jit(solution)/shard_map/aim_rows/pallas_call | solution.py:36
  4.5 2.1 %collective-permute-start = (bf16[144,1408]{1,0:T(8,128)(2,1)}, bf16[144,1408]{1,0:T(8,128)(2,1)S(1)}, u32[]{:S(2)}, u32[]{:S(2)}) collective-permute-start(bf16[144,1408]{1,0:T(8,128)(2,1)} %get-tuple-element.29), channel_id=1, source_target_pairs={{0,32},{32,64},{64,96},{96,0},{1,33},{33,65},{65,97},{97,1},{2,34}... | collective-permute-start | bytes 1216520 | tf_op jit(solution)/shard_map/ppermute | solution.py:349
  6.6 3.6 %collective-permute-start.1 = (bf16[144,1408]{1,0:T(8,128)(2,1)}, bf16[144,1408]{1,0:T(8,128)(2,1)S(1)}, u32[]{:S(2)}, u32[]{:S(2)}) collective-permute-start(bf16[144,1408]{1,0:T(8,128)(2,1)} %get-tuple-element.30), channel_id=1, source_target_pairs={{0,64},{32,96},{64,0},{96,32},{1,65},{33,97},{65,1},{97,33},{2,66}... | collective-permute-start | bytes 1216520 | tf_op jit(solution)/shard_map/ppermute | solution.py:349
  10.2 1.0 collective-permute-start.2
  11.2 9.0 %space_forward.1 = (bf16[256,2112]{1,0:T(8,128)(2,1)}, bf16[8,256,256]{2,1,0:T(8,128)(2,1)}, bf16[256,704]{1,0:T(8,128)(2,1)}, bf16[256,1408]{1,0:T(8,128)(2,1)}) custom-call(bf16[256,1408]{1,0:T(8,128)(2,1)} %bitcast.28, bf16[2112,1408]{1,0:T(8,128)(2,1)} %bitcast.19, bf16[704,1408]{1,0:T(8,128)(2,1)} %bitcast.21), custom_call_target="tpu_custom_call" | custom-call | flops 2200000000 | bytes 11000000 | tf_op jit(solution)/shard_map/space_forward/pallas_call | solution.py:36
  20.2 7.3 %all-to-all-start.1 = ((bf16[32,8,1408]{2,1,0:T(8,128)(2,1)}), bf16[32,8,1408]{2,1,0:T(8,128)(2,1)S(1)}, u32[]{:S(2)}, u32[]{:S(2)}) async-start(bf16[32,8,1408]{2,1,0:T(8,128)(2,1)} %bitcast.32), calls=%async_computation.1 | async-start | bytes 1441792 | tf_op jit(solution)/shard_map/all_to_all | solution.py:344
  27.6 0.6 collective-permute-done.1.refs_3_
  28.2 2.2 %scatter_rows.1 = (bf16[256,1408]{1,0:T(8,128)(2,1)S(1)}, bf16[128,1408]{1,0:T(8,128)(2,1)S(1)}, bf16[128,1408]{1,0:T(8,128)(2,1)S(1)}) custom-call(s32[2]{0:T(128)S(1)} %copy-done.8, bf16[144,1408]{1,0:T(8,128)(2,1)S(1)} %copy-done.4, bf16[144,1408]{1,0:T(8,128)(2,1)S(1)} %collective-permute-done.refs_2_, ...), custom_call_target="tpu_custom_call" | custom-call | flops 1000000 | bytes 5000 | tf_op jit(solution)/shard_map/scatter_rows/pallas_call | solution.py:36
  30.9 1.2 collective-permute-done.3.refs_0_
  32.6 0.9 join_rows.1
  33.6 8.0 %all-to-all-done.1 = bf16[32,8,1408]{2,1,0:T(8,128)(2,1)S(1)} async-done(((bf16[32,8,1408]{2,1,0:T(8,128)(2,1)}), bf16[32,8,1408]{2,1,0:T(8,128)(2,1)S(1)}, u32[]{:S(2)}, u32[]{:S(2)}) %all-to-all-start.1) | async-done | bytes 720928 | tf_op jit(solution)/shard_map/all_to_all | solution.py:344
  41.6 4.1 %all-to-all-start = ((bf16[32,8,1408]{2,1,0:T(8,128)(2,1)}), bf16[32,8,1408]{2,1,0:T(8,128)(2,1)S(1)}, u32[]{:S(2)}, u32[]{:S(2)}) async-start(bf16[32,8,1408]{2,1,0:T(8,128)(2,1)} %bitcast.6), calls=%async_computation | async-start | bytes 1441792 | tf_op jit(solution)/shard_map/all_to_all | solution.py:344
  45.7 8.5 %time_forward.1 = (bf16[256,2112]{1,0:T(8,128)(2,1)}, bf16[8,256,256]{2,1,0:T(8,128)(2,1)}, bf16[256,704]{1,0:T(8,128)(2,1)}) custom-call(bf16[256,1408]{1,0:T(8,128)(2,1)} %bitcast.25, bf16[2112,1408]{1,0:T(8,128)(2,1)} %bitcast.23), custom_call_target="tpu_custom_call" | custom-call | flops 2200000000 | bytes 11000000 | tf_op jit(solution)/shard_map/time_forward/pallas_call | solution.py:36
  54.2 5.3 %all-to-all-done = bf16[32,8,1408]{2,1,0:T(8,128)(2,1)S(1)} async-done(((bf16[32,8,1408]{2,1,0:T(8,128)(2,1)}), bf16[32,8,1408]{2,1,0:T(8,128)(2,1)S(1)}, u32[]{:S(2)}, u32[]{:S(2)}) %all-to-all-start) | async-done | bytes 720928 | tf_op jit(solution)/shard_map/all_to_all | solution.py:344
  59.5 0.9 copy-done.1
  60.4 10.3 %time_backward.1 = bf16[256,1408]{1,0:T(8,128)(2,1)} custom-call(bf16[256,1408]{1,0:T(8,128)(2,1)} %bitcast.17, bf16[256,1408]{1,0:T(8,128)(2,1)} %bitcast.26, bf16[256,2112]{1,0:T(8,128)(2,1)} %get-tuple-element.35.projected_in, bf16[8,256,256]{2,1,0:T(8,128)(2,1)} %get-tuple-element.36.probs_in, bf16[2112,1408]{1,0:T(8,128)(2,1)} %bitcast.24, ...), custom_call_target="tpu_custom_call" | custom-call | flops 2600000000 | bytes 13000000 | tf_op jit(solution)/shard_map/time_backward/pallas_call | solution.py:36
  70.7 1.1 copy-done.2
  71.8 0.9 time_split.1
  72.8 0.7 copy-done.6
  73.5 3.9 %all-to-all-start.2 = ((bf16[32,8,1408]{2,1,0:T(8,128)(2,1)}), bf16[32,8,1408]{2,1,0:T(8,128)(2,1)S(1)}, u32[]{:S(2)}, u32[]{:S(2)}) async-start(bf16[32,8,1408]{2,1,0:T(8,128)(2,1)} %bitcast.27), calls=%async_computation.2 | async-start | bytes 1441792 | tf_op jit(solution)/shard_map/all_to_all | solution.py:344
  77.5 0.6 collective-permute-start.7
  78.1 1.0 copy-done.7
  79.1 0.9 time_weight.1.time_in
  79.9 11.5 %all-to-all-done.2 = bf16[32,8,1408]{2,1,0:T(8,128)(2,1)S(1)} async-done(((bf16[32,8,1408]{2,1,0:T(8,128)(2,1)}), bf16[32,8,1408]{2,1,0:T(8,128)(2,1)S(1)}, u32[]{:S(2)}, u32[]{:S(2)}) %all-to-all-start.2) | async-done | bytes 720928 | tf_op jit(solution)/shard_map/all_to_all | solution.py:344
  91.5 0.8 space_split.1
  92.4 1.7 %collective-permute-done.6.grad_got_in = bf16[256,704]{1,0:T(8,128)(2,1)S(1)} collective-permute-done((bf16[256,704]{1,0:T(8,128)(2,1)S(1)}, bf16[256,704]{1,0:T(8,128)(2,1)S(1)}, u32[]{:S(2)}, u32[]{:S(2)}) %collective-permute-start.6) | collective-permute-done | bytes 360480 | tf_op jit(solution)/shard_map/ppermute | solution.py:349
  94.1 3.6 %pack_shares.1 = bf16[64,16,1024]{2,1,0:T(8,128)(2,1)} custom-call(bf16[704,704]{1,0:T(8,128)(2,1)S(1)} %time_weight.1.time_in, bf16[256,704]{1,0:T(8,128)(2,1)S(1)} %get-tuple-element.44.grad_in, bf16[256,704]{1,0:T(8,128)(2,1)S(1)} %collective-permute-done.6.grad_got_in, bf16[256,704]{1,0:T(8,128)(2,1)S(1)} %copy-done.5, ...), custom_call_target="tpu_custom_call" | custom-call | flops 1000000 | bytes 5000 | tf_op jit(solution)/shard_map/pack_shares/pallas_call | solution.py:36
  97.7 4.7 %all-to-all-start.3 = ((bf16[64,16,1024]{2,1,0:T(8,128)(2,1)}), bf16[64,16,1024]{2,1,0:T(8,128)(2,1)S(1)}, u32[]{:S(2)}, u32[]{:S(2)}) async-start(bf16[64,16,1024]{2,1,0:T(8,128)(2,1)} %pack_shares.1), calls=%async_computation.3 | async-start | bytes 4194304 | tf_op jit(solution)/shard_map/all_to_all | solution.py:413
  102.4 10.3 %space_backward.1 = bf16[256,1408]{1,0:T(8,128)(2,1)} custom-call(bf16[256,1408]{1,0:T(8,128)(2,1)} %bitcast.16, bf16[256,1408]{1,0:T(8,128)(2,1)} %bitcast.29, bf16[256,2112]{1,0:T(8,128)(2,1)} %get-tuple-element.37.projected_in, bf16[8,256,256]{2,1,0:T(8,128)(2,1)} %get-tuple-element.38.probs_in, bf16[2112,1408]{1,0:T(8,128)(2,1)} %bitcast.20, ...), custom_call_target="tpu_custom_call" | custom-call | flops 2600000000 | bytes 13000000 | tf_op jit(solution)/shard_map/space_backward/pallas_call | solution.py:36
  112.7 19.9 %all-to-all-done.3.parts_ref = bf16[64,16,1024]{2,1,0:T(8,128)(2,1)S(1)} async-done(((bf16[64,16,1024]{2,1,0:T(8,128)(2,1)}), bf16[64,16,1024]{2,1,0:T(8,128)(2,1)S(1)}, u32[]{:S(2)}, u32[]{:S(2)}) %all-to-all-start.3) | async-done | bytes 2097184 | tf_op jit(solution)/shard_map/all_to_all | solution.py:413
  132.6 0.9 sum_shares.1
  (25 shorter events, 1.2 us)
Async XLA Ops:
  4.5 23.1 %collective-permute-start = (bf16[144,1408]{1,0:T(8,128)(2,1)}, bf16[144,1408]{1,0:T(8,128)(2,1)S(1)}, u32[]{:S(2)}, u32[]{:S(2)}) collective-permute-start(bf16[144,1408]{1,0:T(8,128)(2,1)} %get-tuple-element.29), channel_id=1, source_target_pairs={{0,32},{32,64},{64,96},{96,0},{1,33},{33,65},{65,97},{97,1},{2,34}... | collective-permute-start | bytes 1216520 | tf_op jit(solution)/shard_map/ppermute | solution.py:349
  6.6 21.6 %collective-permute-start.1 = (bf16[144,1408]{1,0:T(8,128)(2,1)}, bf16[144,1408]{1,0:T(8,128)(2,1)S(1)}, u32[]{:S(2)}, u32[]{:S(2)}) collective-permute-start(bf16[144,1408]{1,0:T(8,128)(2,1)} %get-tuple-element.30), channel_id=1, source_target_pairs={{0,64},{32,96},{64,0},{96,32},{1,65},{33,97},{65,1},{97,33},{2,66}... | collective-permute-start | bytes 1216520 | tf_op jit(solution)/shard_map/ppermute | solution.py:349
  10.2 18.0 %collective-permute-start.2 = (bf16[144,1408]{1,0:T(8,128)(2,1)}, bf16[144,1408]{1,0:T(8,128)(2,1)S(1)}, u32[]{:S(2)}, u32[]{:S(2)}) collective-permute-start(bf16[144,1408]{1,0:T(8,128)(2,1)} %get-tuple-element.31), channel_id=1, source_target_pairs={{0,96},{32,0},{64,32},{96,64},{1,97},{33,1},{65,33},{97,65},{2,98}... | collective-permute-start | bytes 1216520 | tf_op jit(solution)/shard_map/ppermute | solution.py:349
  11.2 17.0 %copy-start.4 = (bf16[144,1408]{1,0:T(8,128)(2,1)S(1)}, bf16[144,1408]{1,0:T(8,128)(2,1)}, u32[]{:S(2)}) copy-start(bf16[144,1408]{1,0:T(8,128)(2,1)} %get-tuple-element.28.refs_1_) | copy-start | bytes 1216516
  11.2 17.0 %copy-start.8 = (s32[2]{0:T(128)S(1)}, s32[2]{0:T(128)}, u32[]{:S(2)}) copy-start(s32[2]{0:T(128)} %pad_add_fusion.place_ref.refs_0_) | copy-start | bytes 28
  20.2 21.3 %all-to-all-start.1 = ((bf16[32,8,1408]{2,1,0:T(8,128)(2,1)}), bf16[32,8,1408]{2,1,0:T(8,128)(2,1)S(1)}, u32[]{:S(2)}, u32[]{:S(2)}) async-start(bf16[32,8,1408]{2,1,0:T(8,128)(2,1)} %bitcast.32), calls=%async_computation.1 | async-start | bytes 1441792 | tf_op jit(solution)/shard_map/all_to_all | solution.py:344
  30.4 1.8 %collective-permute-start.3 = (bf16[128,1408]{1,0:T(8,128)(2,1)S(1)}, bf16[128,1408]{1,0:T(8,128)(2,1)S(1)}, u32[]{:S(2)}, u32[]{:S(2)}) collective-permute-start(bf16[128,1408]{1,0:T(8,128)(2,1)S(1)} %get-tuple-element.33), channel_id=1, source_target_pairs={{0,16},{16,0},{1,17},{17,1},{2,18},{18,2},{3,19},{19,3},{4,20},{20... | collective-permute-start | bytes 1081352 | tf_op jit(solution)/shard_map/ppermute | solution.py:349
  30.4 2.2 %collective-permute-start.4 = (bf16[128,1408]{1,0:T(8,128)(2,1)S(1)}, bf16[128,1408]{1,0:T(8,128)(2,1)S(1)}, u32[]{:S(2)}, u32[]{:S(2)}) collective-permute-start(bf16[128,1408]{1,0:T(8,128)(2,1)S(1)} %get-tuple-element.34), channel_id=1, source_target_pairs={{0,16},{16,0},{1,17},{17,1},{2,18},{18,2},{3,19},{19,3},{4,20},{20... | collective-permute-start | bytes 1081352 | tf_op jit(solution)/shard_map/ppermute | solution.py:349
  41.6 4.1 %copy-start.9 = (bf16[32,8,1408]{2,1,0:T(8,128)(2,1)}, bf16[32,8,1408]{2,1,0:T(8,128)(2,1)S(1)}, u32[]{:S(2)}) copy-start(bf16[32,8,1408]{2,1,0:T(8,128)(2,1)S(1)} %all-to-all-done.1) | copy-start | bytes 2162692
  41.6 17.9 %all-to-all-start = ((bf16[32,8,1408]{2,1,0:T(8,128)(2,1)}), bf16[32,8,1408]{2,1,0:T(8,128)(2,1)S(1)}, u32[]{:S(2)}, u32[]{:S(2)}) async-start(bf16[32,8,1408]{2,1,0:T(8,128)(2,1)} %bitcast.6), calls=%async_computation | async-start | bytes 1441792 | tf_op jit(solution)/shard_map/all_to_all | solution.py:344
  59.5 0.9 copy-start.1
  60.4 10.4 %copy-start.3 = (bf16[256,704]{1,0:T(8,128)(2,1)S(1)}, bf16[256,704]{1,0:T(8,128)(2,1)}, u32[]{:S(2)}) copy-start(bf16[256,704]{1,0:T(8,128)(2,1)} %get-tuple-element.40.refs_2_.mixed_ref) | copy-start | bytes 1081348
  70.7 1.1 copy-start.2
  71.8 5.6 %copy-start.5 = (bf16[256,704]{1,0:T(8,128)(2,1)S(1)}, bf16[256,704]{1,0:T(8,128)(2,1)}, u32[]{:S(2)}) copy-start(bf16[256,704]{1,0:T(8,128)(2,1)} %get-tuple-element.46.mixed_in) | copy-start | bytes 1081348
  72.8 0.7 copy-start.6
  73.5 4.5 %collective-permute-start.5 = (bf16[256,1408]{1,0:T(8,128)(2,1)S(1)}, bf16[256,1408]{1,0:T(8,128)(2,1)S(1)}, u32[]{:S(2)}, u32[]{:S(2)}) collective-permute-start(bf16[256,1408]{1,0:T(8,128)(2,1)S(1)} %get-tuple-element.42), channel_id=1, source_target_pairs={{0,16},{16,0},{1,17},{17,1},{2,18},{18,2},{3,19},{19,3},{4,20},{20... | collective-permute-start | bytes 2162696 | tf_op jit(solution)/shard_map/ppermute | solution.py:349
  73.5 17.9 %all-to-all-start.2 = ((bf16[32,8,1408]{2,1,0:T(8,128)(2,1)}), bf16[32,8,1408]{2,1,0:T(8,128)(2,1)S(1)}, u32[]{:S(2)}, u32[]{:S(2)}) async-start(bf16[32,8,1408]{2,1,0:T(8,128)(2,1)} %bitcast.27), calls=%async_computation.2 | async-start | bytes 1441792 | tf_op jit(solution)/shard_map/all_to_all | solution.py:344
  77.5 14.9 %collective-permute-start.7 = (bf16[256,704]{1,0:T(8,128)(2,1)S(1)}, bf16[256,704]{1,0:T(8,128)(2,1)}, u32[]{:S(2)}, u32[]{:S(2)}) collective-permute-start(bf16[256,704]{1,0:T(8,128)(2,1)S(1)} %copy-done.5), channel_id=1, source_target_pairs={{0,16},{16,0},{1,17},{17,1},{2,18},{18,2},{3,19},{19,3},{4,20},{20... | collective-permute-start | bytes 1081352 | tf_op jit(solution)/shard_map/ppermute | solution.py:349
  78.1 1.0 copy-start.7
  91.5 6.2 %copy-start = (bf16[32,8,1408]{2,1,0:T(8,128)(2,1)}, bf16[32,8,1408]{2,1,0:T(8,128)(2,1)S(1)}, u32[]{:S(2)}) copy-start(bf16[32,8,1408]{2,1,0:T(8,128)(2,1)S(1)} %all-to-all-done.2) | copy-start | bytes 2162692
  92.3 1.8 %collective-permute-start.6 = (bf16[256,704]{1,0:T(8,128)(2,1)S(1)}, bf16[256,704]{1,0:T(8,128)(2,1)S(1)}, u32[]{:S(2)}, u32[]{:S(2)}) collective-permute-start(bf16[256,704]{1,0:T(8,128)(2,1)S(1)} %get-tuple-element.45), channel_id=1, source_target_pairs={{0,16},{16,0},{1,17},{17,1},{2,18},{18,2},{3,19},{19,3},{4,20},{20... | collective-permute-start | bytes 1081352 | tf_op jit(solution)/shard_map/ppermute | solution.py:349
  97.7 34.9 %all-to-all-start.3 = ((bf16[64,16,1024]{2,1,0:T(8,128)(2,1)}), bf16[64,16,1024]{2,1,0:T(8,128)(2,1)S(1)}, u32[]{:S(2)}, u32[]{:S(2)}) async-start(bf16[64,16,1024]{2,1,0:T(8,128)(2,1)} %pack_shares.1), calls=%async_computation.3 | async-start | bytes 4194304 | tf_op jit(solution)/shard_map/all_to_all | solution.py:413

commit v5 on v4

--- a/solution.py
+++ b/solution.py
@@ -84,13 +84,15 @@
         stream_in, attend_in, projected_out, probs_out, mixed_out = refs[:5]
         stream, attend, projected, probs, mixed, sems = refs[5:]
     else:
-        stream_in, attend_in, output_in, projected_out, probs_out, mixed_out, result_out = refs[:7]
-        stream, attend, projected, probs, mixed, output, result, sems = refs[7:]
+        stream_in, attend_in, output_in, projected_out, probs_out, result_out = refs[:6]
+        stream, attend, projected, probs, output, result, sems = refs[6:]
+        mixed = result.at[:, pl.ds(stream.shape[1], WIDE)]
+    width = stream.shape[1]
 
     def copy(source, target, at):
         return pltpu.make_async_copy(source, target, sems.at[at])
 
-    load = copy(stream_in, stream, 0)
+    load = copy(stream_in.at[:, pl.ds(0, width)] if temporal else stream_in, stream, 0)
     load.start()
     parts = [
         copy(attend_in.at[pl.ds(a, n)], attend.at[pl.ds(a, n)], 1 + i)
@@ -121,30 +123,31 @@
         mixed[:, h * HEAD : (h + 1) * HEAD] = dot_nn(chances, head(projected, 2, h)).astype(
             jnp.bfloat16
         )
-    stores += [copy(mixed, mixed_out, 6), copy(probs, probs_out, 8)]
+    stores.append(copy(probs, probs_out, 7))
     stores[1].start()
-    stores[2].start()
-    if not temporal:
+    if temporal:
+        stores.append(copy(mixed, mixed_out, 6))
+    else:
         load_output.wait()
         branch = dot_nn(mixed[...], output[...])
-        result[...] = (stream[...].astype(jnp.float32) + branch).astype(jnp.bfloat16)
-        stores.append(copy(result, result_out, 7))
-        stores[-1].start()
+        result[:, :width] = (stream[...].astype(jnp.float32) + branch).astype(jnp.bfloat16)
+        stores.append(copy(result, result_out, 6))
+    stores[2].start()
     for store in stores:
         store.wait()
 
 
 def forward(stream, attend, output=None):
     temporal = output is None
-    tokens, width = stream.shape
-    shapes = [(tokens, 3 * WIDE), (HEADS, tokens, tokens), (tokens, WIDE)]
+    tokens, width = stream.shape[0], attend.shape[0]
+    last = (tokens, WIDE) if temporal else (tokens, width + WIDE)
+    shapes = [(tokens, 3 * WIDE), (HEADS, tokens, tokens), last]
     outs = [bf16(*shape) for shape in shapes]
     scratch = [held(tokens, width), held(3 * WIDE, width)] + [held(*shape) for shape in shapes]
     args = [stream, attend.T]
     if not temporal:
         args.append(output.T)
-        outs.append(bf16(tokens, width))
-        scratch += [held(WIDE, width), held(tokens, width)]
+        scratch.insert(4, held(WIDE, width))
     scratch.append(pltpu.SemaphoreType.DMA((16,)))
     name = "time_forward" if temporal else "space_forward"
     spaces = "a" * (len(args) + len(outs))
@@ -163,7 +166,7 @@
     load_grad, load_output = copy(grad_in, grad, 0), copy(output_in, output, 1)
     load_projected = copy(projected_in, projected, 2)
     load_probs = copy(probs_in, probs, 7)
-    load_attend, load_stream = copy(attend_in, attend, 3), copy(stream_in, stream, 4)
+    load_attend, load_stream = copy(attend_in, attend, 3), copy(stream_in.at[:, pl.ds(0, stream.shape[1])], stream, 4)
     for load in (load_grad, load_output, load_projected, load_probs, load_attend, load_stream):
         load.start()
     load_grad.wait()
@@ -202,52 +205,59 @@
     store.wait()
 
 
-def backward(grad, stream, projected, probs, attend, output, name):
+def backward(grad, stream, projected, probs, attend, output, name, room):
     args = [grad, stream, projected, probs, attend.T, output.T]
-    scratch = [held(*arg.shape) for arg in args] + [held(*grad.shape), held(*projected.shape)]
+    scratch = [held(*arg.shape) for arg in [grad, grad] + args[2:] + [grad, projected]]
     scratch.append(pltpu.SemaphoreType.DMA((16,)))
-    return call(backward_kernel, bf16(*grad.shape), args, name, "a" * 7, scratch, 2.6e9, 60)
-
-
-def aim_kernel(place_ref, counts_ref, targets_in, rows_in, *refs):
-    piece_refs, (targets, sems) = refs[:-2], refs[-2:]
-    chips = len(piece_refs)
-    aimed = pltpu.make_async_copy(targets_in, targets, sems.at[chips])
-    aimed.start()
-    loads = []
-    for d in range(chips):
-        to = (place_ref[0] + d) % chips
-        into = piece_refs[d].at[pl.ds(0, 128)]
-        loads.append(pltpu.make_async_copy(rows_in.at[to], into, sems.at[d]))
-        loads[-1].start()
-    aimed.wait()
+    return call(backward_kernel, bf16(*grad.shape), args, name, "a" * 7, scratch, 2.6e9, room)
+
+
+def aim_kernel(counts_ref, targets_in, rows_in, keep_ref, next_ref, last_ref, targets, sems):
+    chips = rows_in.shape[0]
+    own = lax.axis_index("z")
+    far = (own + 2) % chips
+    near = ((keep_ref, own), (next_ref, (own + 1) % chips), (last_ref, (own + chips - 1) % chips))
+    loads = [pltpu.make_async_copy(targets_in, targets, sems.at[0])]
+    for i, (ref, to) in enumerate(near):
+        loads.append(pltpu.make_async_copy(rows_in.at[to], ref.at[pl.ds(0, 128)], sems.at[1 + i]))
+    for i, ref in enumerate((next_ref, last_ref)):
+        source = rows_in.at[far, pl.ds(64 * i, 64)]
+        loads.append(pltpu.make_async_copy(source, ref.at[pl.ds(144, 64)], sems.at[4 + i]))
+    for load in loads:
+        load.start()
     line = lax.broadcasted_iota(jnp.int32, (16, 64), 0)
     slot = lax.broadcasted_iota(jnp.int32, (16, 64), 1)
-    for d, piece_ref in enumerate(piece_refs):
-        to = (place_ref[0] + d) % chips
-        piece_ref[128:, :] = jnp.zeros((16, piece_ref.shape[1]), jnp.bfloat16)
+    loads[0].wait()
+    for ref, to, at in [(ref, to, 128) for ref, to in near] + [(next_ref, far, 208), (last_ref, far, 208)]:
         aims = jnp.full((16, 64), -1, jnp.int32)
         for core in range(2):
             valid = (line == core) & (slot < counts_ref[0, 0, 2 * to + core])
             aims = jnp.where(valid, targets[0, 0, pl.ds(2 * to + core, 1), :], aims)
-        piece_ref[128:, :64] = aims.astype(jnp.float32).astype(jnp.bfloat16)
-    for load in loads:
+        ref[at : at + 16, :] = jnp.zeros((16, ref.shape[1]), jnp.bfloat16)
+        ref[at : at + 16, :64] = aims.astype(jnp.float32).astype(jnp.bfloat16)
+    for load in loads[1:]:
         load.wait()
 
 
-def scatter_kernel(chips, place_ref, *refs):
-    pieces, mine_ref, other_refs = refs[:chips], refs[chips], refs[chips + 1 :]
+def scatter_kernel(place_ref, keep_ref, next_ref, last_ref, far0_ref, far1_ref, mine_ref, *other_refs):
     tokens = mine_ref.shape[0]
     line = lax.broadcasted_iota(jnp.int32, (16, 64), 0)
     token = lax.broadcasted_iota(jnp.int32, (tokens, 64), 0).astype(jnp.float32)
     for out_refs, core in ((other_refs, 1 - place_ref[1]), ((mine_ref,), place_ref[1])):
+        at = pl.multiple_of(core * 64, 64)
+        terms = [(ref[128:144, :64], ref[pl.ds(at, 64), :]) for ref in (keep_ref, next_ref, last_ref)]
+        terms.append(
+            (
+                jnp.where(core == 0, far0_ref[64:80, :64], far1_ref[64:80, :64]),
+                jnp.where(core == 0, far0_ref[:64, :], far1_ref[:64, :]),
+            )
+        )
         total = jnp.zeros(mine_ref.shape, jnp.float32)
-        for piece_ref in pieces:
-            info = piece_ref[128:, :64].astype(jnp.float32)
+        for info, rows in terms:
+            info = info.astype(jnp.float32)
             aims = jnp.sum(jnp.where(line == core, info, 0.0), axis=0, keepdims=True)
             matches = jnp.where(aims == token, 1.0, 0.0).astype(jnp.bfloat16)
-            at = pl.multiple_of(core * 64, 64)
-            total = total + dot_nn(matches, piece_ref[pl.ds(at, 64), :])
+            total = total + dot_nn(matches, rows)
         step = tokens // len(out_refs)
         for i, out_ref in enumerate(out_refs):
             out_ref[...] = total[i * step : (i + 1) * step].astype(jnp.bfloat16)
@@ -269,37 +279,20 @@
     ]
 
 
-def split_kernel(chips, place_ref, grad_ref, *refs):
-    mine_ref, other_ref = refs[-2:]
-    halves = halves_of(grad_ref[...], chips)
+def split_kernel(chips, place_ref, *refs):
     first = place_ref[1] == 0
-    half = mine_ref.shape[1]
-    mine_ref[...] = jnp.where(first, halves[0], halves[1])
-    other_ref[:, :half] = jnp.where(first, halves[1], halves[0])
-    if len(refs) == 3:
-        other_ref[:, half:] = refs[0][...]
-
-
-def chip_product_kernel(grad_ref, mixed_ref, got_ref, out_ref):
-    half = grad_ref.shape[1]
-    total = dot_tn(grad_ref[...], mixed_ref[...]) + dot_tn(got_ref[:, :half], got_ref[:, half:])
-    out_ref[...] = total.astype(jnp.bfloat16)
-
-
-def pack_kernel(time_in, grad_in, grad_got_in, mixed_in, mixed_got_in, packed_out, *scratch):
-    time_ref, grad, grad_got, mixed, mixed_got, packed, sems = scratch
-    loads = [
-        pltpu.make_async_copy(source, target, sems.at[i])
-        for i, (source, target) in enumerate(
-            ((mixed_in, mixed), (grad_in, grad), (mixed_got_in, mixed_got), (grad_got_in, grad_got), (time_in, time_ref))
-        )
-    ]
-    for load in loads:
-        load.start()
-    for load in loads:
-        load.wait()
-    space = dot_tn(grad[...], mixed[...]) + dot_tn(grad_got[...], mixed_got[...])
-    time = time_ref[...].astype(jnp.float32)
+    for grad_ref, mine_ref, other_ref in (refs[:1] + refs[2:4], refs[1:2] + refs[4:6]):
+        halves = halves_of(grad_ref[...], chips)
+        mine_ref[...] = jnp.where(first, halves[0], halves[1])
+        other_ref[...] = jnp.where(first, halves[1], halves[0])
+
+
+def pack_kernel(*refs):
+    packed_out, packed, sems = refs[8:]
+    time, space = (
+        dot_tn(grad[...], mixed[...]) + dot_tn(grad_got[...], mixed_got[...])
+        for grad, mixed, grad_got, mixed_got in (refs[:4], refs[4:8])
+    )
     main = jnp.concatenate([time[:, :CUT], space[:, :384]], axis=1)
     left = jnp.concatenate([space[:, 384:CUT], time[:, CUT:], space[:, CUT:]], axis=1)
     zero = jnp.zeros((2, 128), jnp.float32)
@@ -314,16 +307,15 @@
         packed[k] = jnp.concatenate(rows, axis=0).astype(jnp.bfloat16)
         if (k + 1) % 16 == 0:
             at = pl.ds(k - 15, 16)
-            stores.append(pltpu.make_async_copy(packed.at[at], packed_out.at[at], sems.at[5 + k // 16]))
+            stores.append(pltpu.make_async_copy(packed.at[at], packed_out.at[at], sems.at[k // 16]))
             stores[-1].start()
     for store in stores:
         store.wait()
 
 
 def pack(arrays, blocks):
-    scratch = [held(*array.shape) for array in arrays]
-    scratch += [held(blocks, 16, 1024), pltpu.SemaphoreType.DMA((5 + blocks // 16,))]
-    return call(pack_kernel, bf16(blocks, 16, 1024), arrays, "pack_shares", "aaaaaa", scratch)
+    scratch = [held(blocks, 16, 1024), pltpu.SemaphoreType.DMA((blocks // 16,))]
+    return call(pack_kernel, bf16(blocks, 16, 1024), arrays, "pack_shares", "vvvvvvvva", scratch)
 
 
 def unpack_kernel(parts_ref, space_ref, time_ref):
@@ -361,60 +353,48 @@
     tokens, width = stream.shape
     place = jnp.stack([lax.axis_index("z"), lax.axis_index("core")]).astype(jnp.int32)
 
-    args = [place, counts, targets, grad_rows.reshape(chips, 128, width)]
-    scratch = [pltpu.VMEM(targets.shape, jnp.int32), pltpu.SemaphoreType.DMA((chips + 1,))]
-    pieces = call(aim_kernel, [bf16(144, width)] * chips, args, "aim_rows", "ssaa" + "v" * chips, scratch, room=60)
-    pieces = [piece if d == 0 else shift(piece, "z", d) for d, piece in enumerate(pieces)]
+    args = [counts, targets, grad_rows.reshape(chips, 128, width)]
+    scratch = [pltpu.VMEM(targets.shape, jnp.int32), pltpu.SemaphoreType.DMA((6,))]
+    outs = [bf16(144, width), bf16(224, width), bf16(224, width)]
+    keep, to_next, to_last = call(aim_kernel, outs, args, "aim_rows", "saavvv", scratch, room=60)
+    from_last, from_next = shift(to_next, "z", 1), shift(to_last, "z", chips - 1)
+    far = [shift(from_last[144:], "z", 1), shift(from_next[144:], "z", chips - 1)]
 
     space_saved = forward(stream, attend_space, output_space)
-    hidden = exchange(space_saved[3], CLIP)
-
-    place = after(place, space_saved[3])
-    args = [place, *pieces]
+    hidden = exchange(space_saved[2], CLIP)
+
+    place = after(place, space_saved[2])
+    args = [place, keep, from_last, from_next, *far]
     cuts = 2
     outs = [bf16(tokens, width)] + [bf16(tokens // cuts, width)] * cuts
-    mine, *others = call(
-        lambda *refs: scatter_kernel(chips, *refs), outs, args, "scatter_rows", "s" + "v" * (chips + 1 + cuts)
-    )
+    mine, *others = call(scatter_kernel, outs, args, "scatter_rows", "svvvvv" + "v" * (1 + cuts))
     args = [mine] + [shift(other, "core", 1) for other in others]
     grad_out = call(join_kernel, bf16(tokens, width), args, "join_rows", "v" * (cuts + 2))
     grad = exchange(grad_out, CLIP)
     time_saved = forward(hidden, attend_time)
-    space_mixed_got = shift(space_saved[2], "core", 1)
+    time_mixed, space_mixed = time_saved[2], hidden[:, width:]
+    time_mixed_got, space_mixed_got = shift(time_mixed, "core", 1), shift(space_mixed, "core", 1)
     grad_hidden = backward(
-        grad, hidden, time_saved[0], time_saved[1], attend_time, output_time, "time_backward"
+        grad, hidden, time_saved[0], time_saved[1], attend_time, output_time, "time_backward", 60
     )
-    time_halves = [bf16(tokens, width // 2), bf16(tokens, width)]
-    time_mine, time_other = call(
+    half = bf16(tokens, width // 2)
+    time_mine, time_other, space_mine, space_other = call(
         lambda *refs: split_kernel(chips, *refs),
-        time_halves,
-        [after(place, grad_hidden), grad, time_saved[2]],
-        "time_split",
-        "svvvv",
+        [half] * 4,
+        [place, grad, grad_hidden],
+        "split_features",
+        "svvvvvv",
     )
-    time_got = shift(time_other, "core", 1)
-    args = [time_mine, time_saved[2], time_got]
-    time_sum = call(chip_product_kernel, bf16(width // 2, WIDE), args, "time_weight", "vvvv")
-
+    args = [time_mine, time_mixed, shift(time_other, "core", 1), time_mixed_got]
+    args += [space_mine, space_mixed, shift(space_other, "core", 1), space_mixed_got]
+    packed = pack(args, lax.axis_size(("z", "space")))
     grad_hidden = exchange(grad_hidden, CLIP)
-    half = bf16(tokens, width // 2)
-    space_mine, space_other = call(
-        lambda *refs: split_kernel(chips, *refs),
-        [half, half],
-        [after(place, time_sum), grad_hidden],
-        "space_split",
-        "svvv",
-    )
-    space_got = shift(space_other, "core", 1)
-    packed = pack(
-        [time_sum, space_mine, space_got, space_saved[2], space_mixed_got],
-        lax.axis_size(("z", "space")),
-    )
+    packed = after(packed, grad_hidden)
     packed = lax.all_to_all(packed, ("z", "space"), split_axis=0, concat_axis=0, tiled=True)
     share = jax.ShapeDtypeStruct((SHARE, WIDE), jnp.float32)
     space_grad, time_grad = call(unpack_kernel, [share, share], [packed], "sum_shares", "vvv")
     token_grad = backward(
-        grad_hidden, stream, space_saved[0], space_saved[1], attend_space, output_space, "space_backward"
+        grad_hidden, stream, space_saved[0], space_saved[1], attend_space, output_space, "space_backward", 40
     )
     return (token_grad[None], space_grad, time_grad)
 

time: 134 us -> 128 us (0.955)
  waiting for transfers between devices: 48.7 us -> 37.2 us
  local copies, waits for them, and re-layouts: 3.72 us -> 8.64 us
  starting transfers between devices: 28 us -> 31.4 us
  Pallas kernels: 51.7 us -> 49 us
    all_to_all x3, waiting for transfers between devices: 24.8 us -> 15.5 us  [exchange(): lax.all_to_all(cut, axes, split_axis=0, concat_axis=0, tiled=True)]
    all_to_all x1, waiting for transfers between devices: 19.9 us -> 12.9 us  [body(): lax.all_to_all(packed, ('z', 'space'), split_axis=0, concat_axis=0, tiled...]
    ppermute x8 -> x10, waiting for transfers between devices: 3.97 us -> 8.9 us  [shift(): lax.ppermute(array, axis, [(i, (i + by) % devices) for i in range(devices)])]
    unnamed x20, local copies, waits for them, and re-layouts: 3.72 us -> 7.58 us
    pallas_call x12 -> x10, Pallas kernels: 51.7 us -> 49 us  [call(): pl.pallas_call(kernel, out_shape=outs, in_specs=spaces[:len(args)], out_s...]
    all_to_all x1, starting transfers between devices: 4.7 us -> 6.25 us  [body(): lax.all_to_all(packed, ('z', 'space'), split_axis=0, concat_axis=0, tiled...]
    ppermute x8 -> x10, starting transfers between devices: 7.92 us -> 9.45 us  [shift(): lax.ppermute(array, axis, [(i, (i + by) % devices) for i in range(devices)])]
  transfers between devices with their start and end apart: 12 -> 14, of which waited for: 8 -> 9; matrix products, arithmetic and copies ran while one was open for 0% -> 1% of each run, Pallas kernels for 24% -> 27%
where the time goes in v5:
time: 128 us; the launch traced here: 127 us
  Pallas kernels  49 us (38%)
  waiting for transfers between devices  37.2 us (29%)
  starting transfers between devices  31.4 us (25%)
  local copies, waits for them, and re-layouts  8.64 us (7%)
    pallas_call x10, Pallas kernels, call(): pl.pallas_call(kernel, out_shape=outs, in_specs=spaces[:len(args)], out_s...  49 us
    all_to_all x3, starting transfers between devices, exchange(): lax.all_to_all(cut, axes, split_axis=0, concat_axis=0, tiled=True)  15.7 us
    all_to_all x3, waiting for transfers between devices, exchange(): lax.all_to_all(cut, axes, split_axis=0, concat_axis=0, tiled=True)  15.5 us
    all_to_all x1, waiting for transfers between devices, body(): lax.all_to_all(packed, ('z', 'space'), split_axis=0, concat_axis=0, tiled...  12.9 us
    ppermute x10, starting transfers between devices, shift(): lax.ppermute(array, axis, [(i, (i + by) % devices) for i in range(devices)])  9.45 us
    ppermute x10, waiting for transfers between devices, shift(): lax.ppermute(array, axis, [(i, (i + by) % devices) for i in range(devices)])  8.9 us
    unnamed x20, local copies, waits for them, and re-layouts  7.58 us
    all_to_all x1, starting transfers between devices, body(): lax.all_to_all(packed, ('z', 'space'), split_axis=0, concat_axis=0, tiled...  6.25 us
  transfers between devices with their start and end apart: 14, of which 9 were waited for; matrix products, arithmetic and copies ran while one was open for 1% of the time, Pallas kernels for 27%

profile of v5, /device:TPU:0, one launch (start us, length us, event | category | flops | bytes accessed | tf_op | source)
XLA Modules:
  0.0 127.2 jit_solution(7948324286263731511)
XLA Ops:
  0.6 3.2 %aim_rows.1 = (bf16[144,1408]{1,0:T(8,128)(2,1)}, bf16[224,1408]{1,0:T(8,128)(2,1)}, bf16[224,1408]{1,0:T(8,128)(2,1)}) custom-call(s32[1,1,8]{2,1,0:T(1,128)} %counts_ref.1, s32[1,1,8,64]{3,2,1,0:T(8,128)} %targets_in.1, bf16[4,128,1408]{2,1,0:T(8,128)(2,1)} %bitcast.28), custom_call_target="tpu_custom_call" | custom-call | flops 1000000 | bytes 5000 | tf_op jit(solution)/shard_map/aim_rows/pallas_call | solution.py:36
  3.8 2.1 %collective-permute-start = (bf16[224,1408]{1,0:T(8,128)(2,1)}, bf16[224,1408]{1,0:T(8,128)(2,1)S(1)}, u32[]{:S(2)}, u32[]{:S(2)}) collective-permute-start(bf16[224,1408]{1,0:T(8,128)(2,1)} %get-tuple-element.26), channel_id=1, source_target_pairs={{0,32},{32,64},{64,96},{96,0},{1,33},{33,65},{65,97},{97,1},{2,34}... | collective-permute-start | bytes 1892360 | tf_op jit(solution)/shard_map/ppermute | solution.py:341
  5.9 2.2 %collective-permute-start.1 = (bf16[224,1408]{1,0:T(8,128)(2,1)}, bf16[224,1408]{1,0:T(8,128)(2,1)S(1)}, u32[]{:S(2)}, u32[]{:S(2)}) collective-permute-start(bf16[224,1408]{1,0:T(8,128)(2,1)} %get-tuple-element.27), channel_id=1, source_target_pairs={{0,96},{32,0},{64,32},{96,64},{1,97},{33,1},{65,33},{97,65},{2,98}... | collective-permute-start | bytes 1892360 | tf_op jit(solution)/shard_map/ppermute | solution.py:341
  8.1 9.1 %space_forward.1 = (bf16[256,2112]{1,0:T(8,128)(2,1)}, bf16[8,256,256]{2,1,0:T(8,128)(2,1)}, bf16[256,2112]{1,0:T(8,128)(2,1)}) custom-call(bf16[256,1408]{1,0:T(8,128)(2,1)} %bitcast.23, bf16[2112,1408]{1,0:T(8,128)(2,1)} %bitcast.15, bf16[704,1408]{1,0:T(8,128)(2,1)} %bitcast.17), custom_call_target="tpu_custom_call" | custom-call | flops 2200000000 | bytes 11000000 | tf_op jit(solution)/shard_map/space_forward/pallas_call | solution.py:36
  17.3 7.6 %all-to-all-start.1 = ((bf16[32,8,2112]{2,1,0:T(8,128)(2,1)}), bf16[32,8,2112]{2,1,0:T(8,128)(2,1)}, u32[]{:S(2)}, u32[]{:S(2)}) async-start(bf16[32,8,2112]{2,1,0:T(8,128)(2,1)} %bitcast.29), calls=%async_computation.1 | async-start | bytes 2228224 | tf_op jit(solution)/shard_map/all_to_all | solution.py:336
  25.0 3.3 %collective-permute-start.3 = (bf16[80,1408]{1,0:T(8,128)(2,1)S(1)}, bf16[80,1408]{1,0:T(8,128)(2,1)S(1)}, u32[]{:S(2)}, u32[]{:S(2)}) collective-permute-start(bf16[80,1408]{1,0:T(8,128)(2,1)S(1)} %slice.13), channel_id=1, source_target_pairs={{0,96},{32,0},{64,32},{96,64},{1,97},{33,1},{65,33},{97,65},{2,98}... | collective-permute-start | bytes 675848 | tf_op jit(solution)/shard_map/ppermute | solution.py:341
  28.4 5.4 %collective-permute-done.2.far0_ref = bf16[80,1408]{1,0:T(8,128)(2,1)S(1)} collective-permute-done((bf16[80,1408]{1,0:T(8,128)(2,1)S(1)}, bf16[80,1408]{1,0:T(8,128)(2,1)S(1)}, u32[]{:S(2)}, u32[]{:S(2)}) %collective-permute-start.2) | collective-permute-done | bytes 225312 | tf_op jit(solution)/shard_map/ppermute | solution.py:341
  33.8 2.2 %scatter_rows.1 = (bf16[256,1408]{1,0:T(8,128)(2,1)S(1)}, bf16[128,1408]{1,0:T(8,128)(2,1)S(1)}, bf16[128,1408]{1,0:T(8,128)(2,1)S(1)}) custom-call(s32[2]{0:T(128)S(1)} %pad_add_fusion.place_ref.refs_0_, bf16[144,1408]{1,0:T(8,128)(2,1)S(1)} %copy-done.8, bf16[224,1408]{1,0:T(8,128)(2,1)S(1)} %collective-permute-done.next_ref, ...), custom_call_target="tpu_custom_call" | custom-call | flops 1000000 | bytes 5000 | tf_op jit(solution)/shard_map/scatter_rows/pallas_call | solution.py:36
  36.6 1.2 collective-permute-done.4.refs_0_
  37.8 0.5 collective-permute-done.5.refs_1_
  38.3 0.9 join_rows.1
  39.2 3.8 %all-to-all-done.1 = bf16[32,8,2112]{2,1,0:T(8,128)(2,1)} async-done(((bf16[32,8,2112]{2,1,0:T(8,128)(2,1)}), bf16[32,8,2112]{2,1,0:T(8,128)(2,1)}, u32[]{:S(2)}, u32[]{:S(2)}) %all-to-all-start.1) | async-done | bytes 1081376 | tf_op jit(solution)/shard_map/all_to_all | solution.py:336
  43.0 4.1 %all-to-all-start = ((bf16[32,8,1408]{2,1,0:T(8,128)(2,1)}), bf16[32,8,1408]{2,1,0:T(8,128)(2,1)S(1)}, u32[]{:S(2)}, u32[]{:S(2)}) async-start(bf16[32,8,1408]{2,1,0:T(8,128)(2,1)} %bitcast.6), calls=%async_computation | async-start | bytes 1441792 | tf_op jit(solution)/shard_map/all_to_all | solution.py:336
  47.1 8.3 %time_forward.1 = (bf16[256,2112]{1,0:T(8,128)(2,1)}, bf16[8,256,256]{2,1,0:T(8,128)(2,1)}, bf16[256,704]{1,0:T(8,128)(2,1)}) custom-call(bf16[256,2112]{1,0:T(8,128)(2,1)} %bitcast.9.refs_0_.stream_in, bf16[2112,1408]{1,0:T(8,128)(2,1)} %bitcast.25), custom_call_target="tpu_custom_call" | custom-call | flops 2200000000 | bytes 11000000 | tf_op jit(solution)/shard_map/time_forward/pallas_call | solution.py:36
  55.4 5.5 %all-to-all-done = bf16[32,8,1408]{2,1,0:T(8,128)(2,1)S(1)} async-done(((bf16[32,8,1408]{2,1,0:T(8,128)(2,1)}), bf16[32,8,1408]{2,1,0:T(8,128)(2,1)S(1)}, u32[]{:S(2)}, u32[]{:S(2)}) %all-to-all-start) | async-done | bytes 720928 | tf_op jit(solution)/shard_map/all_to_all | solution.py:336
  60.9 0.9 copy-done.3
  61.8 10.3 %time_backward.1.refs_2_ = bf16[256,1408]{1,0:T(8,128)(2,1)} custom-call(bf16[256,1408]{1,0:T(8,128)(2,1)} %bitcast.20, bf16[256,2112]{1,0:T(8,128)(2,1)} %bitcast.9.refs_0_.stream_in, bf16[256,2112]{1,0:T(8,128)(2,1)} %get-tuple-element.31.projected_in, bf16[8,256,256]{2,1,0:T(8,128)(2,1)} %get-tuple-element.32.probs_in, bf16[2112,1408]{1,0:T(8,128)(2,1)} %bitcast.26, ...), custom_call_target="tpu_custom_call" | custom-call | flops 2600000000 | bytes 13000000 | tf_op jit(solution)/shard_map/time_backward/pallas_call | solution.py:36
  72.1 4.0 %all-to-all-start.2 = ((bf16[32,8,1408]{2,1,0:T(8,128)(2,1)}), bf16[32,8,1408]{2,1,0:T(8,128)(2,1)S(1)}, u32[]{:S(2)}, u32[]{:S(2)}) async-start(bf16[32,8,1408]{2,1,0:T(8,128)(2,1)} %bitcast.19), calls=%async_computation.2 | async-start | bytes 1441792 | tf_op jit(solution)/shard_map/all_to_all | solution.py:336
  76.1 1.0 slice.14.refs_5_
  77.8 1.1 split_features.1
  79.5 1.2 collective-permute-done.6.refs_2_
  80.7 0.6 collective-permute-done.8.refs_6_
  81.3 2.7 %pack_shares.1 = bf16[64,16,1024]{2,1,0:T(8,128)(2,1)} custom-call(bf16[256,704]{1,0:T(8,128)(2,1)S(1)} %get-tuple-element.35.refs_0_, bf16[256,704]{1,0:T(8,128)(2,1)S(1)} %copy-done.9, bf16[256,704]{1,0:T(8,128)(2,1)S(1)} %collective-permute-done.6.refs_2_, bf16[256,704]{1,0:T(8,128)(2,1)S(1)} %collective-permute-done.7.refs_3_, ...), custom_call_target="tpu_custom_call" | custom-call | flops 1000000 | bytes 5000 | tf_op jit(solution)/shard_map/pack_shares/pallas_call | solution.py:36
  84.0 6.2 %all-to-all-done.2 = bf16[32,8,1408]{2,1,0:T(8,128)(2,1)S(1)} async-done(((bf16[32,8,1408]{2,1,0:T(8,128)(2,1)}), bf16[32,8,1408]{2,1,0:T(8,128)(2,1)S(1)}, u32[]{:S(2)}, u32[]{:S(2)}) %all-to-all-start.2) | async-done | bytes 720928 | tf_op jit(solution)/shard_map/all_to_all | solution.py:336
  90.2 6.3 %all-to-all-start.3 = ((bf16[64,16,1024]{2,1,0:T(8,128)(2,1)}), bf16[64,16,1024]{2,1,0:T(8,128)(2,1)S(1)}, u32[]{:S(2)}, u32[]{:S(2)}) async-start(bf16[64,16,1024]{2,1,0:T(8,128)(2,1)} %pack_shares.1), calls=%async_computation.3 | async-start | bytes 4194304 | tf_op jit(solution)/shard_map/all_to_all | solution.py:393
  96.4 2.7 %copy-done = bf16[1408,2112]{0,1:T(8,128)(2,1)S(1)} copy-done((bf16[1408,2112]{0,1:T(8,128)(2,1)S(1)}, bf16[1408,2112]{0,1:T(8,128)(2,1)}, u32[]{:S(2)}) %copy-start) | copy-done | bytes 5947416
  99.1 1.5 %copy-done.1 = bf16[1408,704]{0,1:T(8,128)(2,1)S(1)} copy-done((bf16[1408,704]{0,1:T(8,128)(2,1)S(1)}, bf16[1408,704]{0,1:T(8,128)(2,1)}, u32[]{:S(2)}) %copy-start.1) | copy-done | bytes 1982488
  100.7 1.2 copy-done.6
  101.9 1.2 copy-done.7
  103.1 10.2 %space_backward.1 = bf16[256,1408]{1,0:T(8,128)(2,1)} custom-call(bf16[256,1408]{1,0:T(8,128)(2,1)S(1)} %bitcast.22, bf16[256,1408]{1,0:T(8,128)(2,1)S(1)} %bitcast.24, bf16[256,2112]{1,0:T(8,128)(2,1)S(1)} %copy-done.6, bf16[8,256,256]{2,1,0:T(8,128)(2,1)S(1)} %copy-done.7, bf16[2112,1408]{1,0:T(8,128)(2,1)S(1)} %bitcast.16, bf16[704,1408]{1,0:T(8,128)(2,1)S(1)} %bitcast.18), custom_call_target="tpu_custom_call" | custom-call | flops 2600000000 | bytes 13000000 | tf_op jit(solution)/shard_map/space_backward/pallas_call | solution.py:36
  113.4 12.9 %all-to-all-done.3.parts_ref = bf16[64,16,1024]{2,1,0:T(8,128)(2,1)S(1)} async-done(((bf16[64,16,1024]{2,1,0:T(8,128)(2,1)}), bf16[64,16,1024]{2,1,0:T(8,128)(2,1)S(1)}, u32[]{:S(2)}, u32[]{:S(2)}) %all-to-all-start.3) | async-done | bytes 2097184 | tf_op jit(solution)/shard_map/all_to_all | solution.py:393
  126.3 1.0 sum_shares.1
  (30 shorter events, 2.1 us)
Async XLA Ops:
  3.8 21.0 %collective-permute-start = (bf16[224,1408]{1,0:T(8,128)(2,1)}, bf16[224,1408]{1,0:T(8,128)(2,1)S(1)}, u32[]{:S(2)}, u32[]{:S(2)}) collective-permute-start(bf16[224,1408]{1,0:T(8,128)(2,1)} %get-tuple-element.26), channel_id=1, source_target_pairs={{0,32},{32,64},{64,96},{96,0},{1,33},{33,65},{65,97},{97,1},{2,34}... | collective-permute-start | bytes 1892360 | tf_op jit(solution)/shard_map/ppermute | solution.py:341
  5.9 19.1 %collective-permute-start.1 = (bf16[224,1408]{1,0:T(8,128)(2,1)}, bf16[224,1408]{1,0:T(8,128)(2,1)S(1)}, u32[]{:S(2)}, u32[]{:S(2)}) collective-permute-start(bf16[224,1408]{1,0:T(8,128)(2,1)} %get-tuple-element.27), channel_id=1, source_target_pairs={{0,96},{32,0},{64,32},{96,64},{1,97},{33,1},{65,33},{97,65},{2,98}... | collective-permute-start | bytes 1892360 | tf_op jit(solution)/shard_map/ppermute | solution.py:341
  17.3 16.6 %copy-start.8 = (bf16[144,1408]{1,0:T(8,128)(2,1)S(1)}, bf16[144,1408]{1,0:T(8,128)(2,1)}, u32[]{:S(2)}) copy-start(bf16[144,1408]{1,0:T(8,128)(2,1)} %get-tuple-element.25.keep_ref) | copy-start | bytes 1216516
  17.3 25.7 %all-to-all-start.1 = ((bf16[32,8,2112]{2,1,0:T(8,128)(2,1)}), bf16[32,8,2112]{2,1,0:T(8,128)(2,1)}, u32[]{:S(2)}, u32[]{:S(2)}) async-start(bf16[32,8,2112]{2,1,0:T(8,128)(2,1)} %bitcast.29), calls=%async_computation.1 | async-start | bytes 2228224 | tf_op jit(solution)/shard_map/all_to_all | solution.py:336
  24.9 8.9 %collective-permute-start.2 = (bf16[80,1408]{1,0:T(8,128)(2,1)S(1)}, bf16[80,1408]{1,0:T(8,128)(2,1)S(1)}, u32[]{:S(2)}, u32[]{:S(2)}) collective-permute-start(bf16[80,1408]{1,0:T(8,128)(2,1)S(1)} %slice.12), channel_id=1, source_target_pairs={{0,32},{32,64},{64,96},{96,0},{1,33},{33,65},{65,97},{97,1},{2,34}... | collective-permute-start | bytes 675848 | tf_op jit(solution)/shard_map/ppermute | solution.py:341
  25.0 8.8 %collective-permute-start.3 = (bf16[80,1408]{1,0:T(8,128)(2,1)S(1)}, bf16[80,1408]{1,0:T(8,128)(2,1)S(1)}, u32[]{:S(2)}, u32[]{:S(2)}) collective-permute-start(bf16[80,1408]{1,0:T(8,128)(2,1)S(1)} %slice.13), channel_id=1, source_target_pairs={{0,96},{32,0},{64,32},{96,64},{1,97},{33,1},{65,33},{97,65},{2,98}... | collective-permute-start | bytes 675848 | tf_op jit(solution)/shard_map/ppermute | solution.py:341
  36.0 1.8 %collective-permute-start.4 = (bf16[128,1408]{1,0:T(8,128)(2,1)S(1)}, bf16[128,1408]{1,0:T(8,128)(2,1)S(1)}, u32[]{:S(2)}, u32[]{:S(2)}) collective-permute-start(bf16[128,1408]{1,0:T(8,128)(2,1)S(1)} %get-tuple-element.29), channel_id=1, source_target_pairs={{0,16},{16,0},{1,17},{17,1},{2,18},{18,2},{3,19},{19,3},{4,20},{20... | collective-permute-start | bytes 1081352 | tf_op jit(solution)/shard_map/ppermute | solution.py:341
  36.1 2.2 %collective-permute-start.5 = (bf16[128,1408]{1,0:T(8,128)(2,1)S(1)}, bf16[128,1408]{1,0:T(8,128)(2,1)S(1)}, u32[]{:S(2)}, u32[]{:S(2)}) collective-permute-start(bf16[128,1408]{1,0:T(8,128)(2,1)S(1)} %get-tuple-element.30), channel_id=1, source_target_pairs={{0,16},{16,0},{1,17},{17,1},{2,18},{18,2},{3,19},{19,3},{4,20},{20... | collective-permute-start | bytes 1081352 | tf_op jit(solution)/shard_map/ppermute | solution.py:341
  43.0 17.9 %all-to-all-start = ((bf16[32,8,1408]{2,1,0:T(8,128)(2,1)}), bf16[32,8,1408]{2,1,0:T(8,128)(2,1)S(1)}, u32[]{:S(2)}, u32[]{:S(2)}) async-start(bf16[32,8,1408]{2,1,0:T(8,128)(2,1)} %bitcast.6), calls=%async_computation | async-start | bytes 1441792 | tf_op jit(solution)/shard_map/all_to_all | solution.py:336
  60.9 0.9 copy-start.3
  72.1 5.1 %copy-start.9 = (bf16[256,704]{1,0:T(8,128)(2,1)S(1)}, bf16[256,704]{1,0:T(8,128)(2,1)}, u32[]{:S(2)}) copy-start(bf16[256,704]{1,0:T(8,128)(2,1)} %get-tuple-element.36.refs_1_) | copy-start | bytes 1081348
  72.1 5.8 %copy-start.2 = (bf16[256,1408]{1,0:T(8,128)(2,1)S(1)}, bf16[256,1408]{1,0:T(8,128)(2,1)}, u32[]{:S(2)}) copy-start(bf16[256,1408]{1,0:T(8,128)(2,1)} %time_backward.1.refs_2_) | copy-start | bytes 2162692
  72.1 5.8 %copy-start.4 = (bf16[32,8,1408]{2,1,0:T(8,128)(2,1)S(1)}, bf16[32,8,1408]{2,1,0:T(8,128)(2,1)}, u32[]{:S(2)}) copy-start(bf16[32,8,1408]{2,1,0:T(8,128)(2,1)} %copy-done.3) | copy-start | bytes 2162692
  72.1 18.1 %all-to-all-start.2 = ((bf16[32,8,1408]{2,1,0:T(8,128)(2,1)}), bf16[32,8,1408]{2,1,0:T(8,128)(2,1)S(1)}, u32[]{:S(2)}, u32[]{:S(2)}) async-start(bf16[32,8,1408]{2,1,0:T(8,128)(2,1)} %bitcast.19), calls=%async_computation.2 | async-start | bytes 1441792 | tf_op jit(solution)/shard_map/all_to_all | solution.py:336
  77.2 2.3 %collective-permute-start.7 = (bf16[256,704]{1,0:T(8,128)(2,1)S(1)}, bf16[256,704]{1,0:T(8,128)(2,1)S(1)}, u32[]{:S(2)}, u32[]{:S(2)}) collective-permute-start(bf16[256,704]{1,0:T(8,128)(2,1)S(1)} %copy-done.9), channel_id=1, source_target_pairs={{0,16},{16,0},{1,17},{17,1},{2,18},{18,2},{3,19},{19,3},{4,20},{20... | collective-permute-start | bytes 1081352 | tf_op jit(solution)/shard_map/ppermute | solution.py:341
  77.5 2.0 %collective-permute-start.9 = (bf16[256,704]{1,0:T(8,128)(2,1)S(1)}, bf16[256,704]{1,0:T(8,128)(2,1)S(1)}, u32[]{:S(2)}, u32[]{:S(2)}) collective-permute-start(bf16[256,704]{1,0:T(8,128)(2,1)S(1)} %slice.14.refs_5_), channel_id=1, source_target_pairs={{0,16},{16,0},{1,17},{17,1},{2,18},{18,2},{3,19},{19,3},{4,20},{20... | collective-permute-start | bytes 1081352 | tf_op jit(solution)/shard_map/ppermute | solution.py:341
  78.9 1.8 %collective-permute-start.6 = (bf16[256,704]{1,0:T(8,128)(2,1)S(1)}, bf16[256,704]{1,0:T(8,128)(2,1)S(1)}, u32[]{:S(2)}, u32[]{:S(2)}) collective-permute-start(bf16[256,704]{1,0:T(8,128)(2,1)S(1)} %get-tuple-element.37), channel_id=1, source_target_pairs={{0,16},{16,0},{1,17},{17,1},{2,18},{18,2},{3,19},{19,3},{4,20},{20... | collective-permute-start | bytes 1081352 | tf_op jit(solution)/shard_map/ppermute | solution.py:341
  79.2 2.0 %collective-permute-start.8 = (bf16[256,704]{1,0:T(8,128)(2,1)S(1)}, bf16[256,704]{1,0:T(8,128)(2,1)S(1)}, u32[]{:S(2)}, u32[]{:S(2)}) collective-permute-start(bf16[256,704]{1,0:T(8,128)(2,1)S(1)} %get-tuple-element.39), channel_id=1, source_target_pairs={{0,16},{16,0},{1,17},{17,1},{2,18},{18,2},{3,19},{19,3},{4,20},{20... | collective-permute-start | bytes 1081352 | tf_op jit(solution)/shard_map/ppermute | solution.py:341
  90.2 6.3 %copy-start.5 = (bf16[1,256,1408]{2,1,0:T(8,128)(2,1)S(1)}, bf16[1,256,1408]{2,1,0:T(8,128)(2,1)}, u32[]{:S(2)}) copy-start(bf16[1,256,1408]{2,1,0:T(8,128)(2,1)} %param.8) | copy-start | bytes 2162692
  90.2 36.1 %all-to-all-start.3 = ((bf16[64,16,1024]{2,1,0:T(8,128)(2,1)}), bf16[64,16,1024]{2,1,0:T(8,128)(2,1)S(1)}, u32[]{:S(2)}, u32[]{:S(2)}) async-start(bf16[64,16,1024]{2,1,0:T(8,128)(2,1)} %pack_shares.1), calls=%async_computation.3 | async-start | bytes 4194304 | tf_op jit(solution)/shard_map/all_to_all | solution.py:393
  96.4 2.7 %copy-start = (bf16[1408,2112]{0,1:T(8,128)(2,1)S(1)}, bf16[1408,2112]{0,1:T(8,128)(2,1)}, u32[]{:S(2)}) copy-start(bf16[1408,2112]{0,1:T(8,128)(2,1)} %param.12) | copy-start | bytes 17842180
  99.1 1.6 %copy-start.1 = (bf16[1408,704]{0,1:T(8,128)(2,1)S(1)}, bf16[1408,704]{0,1:T(8,128)(2,1)}, u32[]{:S(2)}) copy-start(bf16[1408,704]{0,1:T(8,128)(2,1)} %param.13) | copy-start | bytes 5947396
  100.7 1.2 copy-start.6
  101.9 1.2 copy-start.7

commit v6 on v5

--- a/solution.py
+++ b/solution.py
@@ -113,8 +113,11 @@
     tokens = stream.shape[0]
     if temporal:
         allowed = same_patch(tokens)
+    ahead = dot_nt(head(projected, 0, 0), head(projected, 1, 0))
     for h in range(HEADS):
-        scores = dot_nt(head(projected, 0, h), head(projected, 1, h)) * HEAD**-0.5
+        scores = ahead * HEAD**-0.5
+        if h + 1 < HEADS:
+            ahead = dot_nt(head(projected, 0, h + 1), head(projected, 1, h + 1))
         if temporal:
             scores = jnp.where(allowed, scores, -jnp.inf)
         weights = jnp.exp(scores - jnp.max(scores, axis=-1, keepdims=True))

time: 128 us -> 127 us (level)
  Pallas kernels: 49 us -> 47.7 us
    pallas_call x10, Pallas kernels: 49 us -> 47.7 us  [call(): pl.pallas_call(kernel, out_shape=outs, in_specs=spaces[:len(args)], out_s...]
  transfers between devices with their start and end apart: 14 -> 14, of which waited for: 9 -> 9; matrix products, arithmetic and copies ran while one was open for 1% -> 1% of each run, Pallas kernels for 27% -> 26%
where the time goes in v6:
time: 127 us
  Pallas kernels  47.7 us (38%)
  waiting for transfers between devices  38 us (30%)
  starting transfers between devices  31.4 us (25%)
  local copies, waits for them, and re-layouts  8.64 us (7%)
    pallas_call x10, Pallas kernels, call(): pl.pallas_call(kernel, out_shape=outs, in_specs=spaces[:len(args)], out_s...  47.7 us
    all_to_all x3, waiting for transfers between devices, exchange(): lax.all_to_all(cut, axes, split_axis=0, concat_axis=0, tiled=True)  16.2 us
    all_to_all x3, starting transfers between devices, exchange(): lax.all_to_all(cut, axes, split_axis=0, concat_axis=0, tiled=True)  15.7 us
    all_to_all x1, waiting for transfers between devices, body(): lax.all_to_all(packed, ('z', 'space'), split_axis=0, concat_axis=0, tiled...  12.9 us
    ppermute x10, starting transfers between devices, shift(): lax.ppermute(array, axis, [(i, (i + by) % devices) for i in range(devices)])  9.45 us
    ppermute x10, waiting for transfers between devices, shift(): lax.ppermute(array, axis, [(i, (i + by) % devices) for i in range(devices)])  8.9 us
    unnamed x20, local copies, waits for them, and re-layouts  7.58 us
    all_to_all x1, starting transfers between devices, body(): lax.all_to_all(packed, ('z', 'space'), split_axis=0, concat_axis=0, tiled...  6.25 us
  transfers between devices with their start and end apart: 14, of which 9 were waited for; matrix products, arithmetic and copies ran while one was open for 1% of the time, Pallas kernels for 26%

profile of v6, /device:TPU:0, one launch (start us, length us, event | category | flops | bytes accessed | tf_op | source)
XLA Modules:
  0.0 126.6 jit_solution(9994029131149214230)
XLA Ops:
  0.6 3.2 %aim_rows.1 = (bf16[144,1408]{1,0:T(8,128)(2,1)}, bf16[224,1408]{1,0:T(8,128)(2,1)}, bf16[224,1408]{1,0:T(8,128)(2,1)}) custom-call(s32[1,1,8]{2,1,0:T(1,128)} %counts_ref.1, s32[1,1,8,64]{3,2,1,0:T(8,128)} %targets_in.1, bf16[4,128,1408]{2,1,0:T(8,128)(2,1)} %bitcast.28), custom_call_target="tpu_custom_call" | custom-call | flops 1000000 | bytes 5000 | tf_op jit(solution)/shard_map/aim_rows/pallas_call | solution.py:36
  3.8 2.1 %collective-permute-start = (bf16[224,1408]{1,0:T(8,128)(2,1)}, bf16[224,1408]{1,0:T(8,128)(2,1)S(1)}, u32[]{:S(2)}, u32[]{:S(2)}) collective-permute-start(bf16[224,1408]{1,0:T(8,128)(2,1)} %get-tuple-element.26), channel_id=1, source_target_pairs={{0,32},{32,64},{64,96},{96,0},{1,33},{33,65},{65,97},{97,1},{2,34}... | collective-permute-start | bytes 1892360 | tf_op jit(solution)/shard_map/ppermute | solution.py:344
  5.9 2.2 %collective-permute-start.1 = (bf16[224,1408]{1,0:T(8,128)(2,1)}, bf16[224,1408]{1,0:T(8,128)(2,1)S(1)}, u32[]{:S(2)}, u32[]{:S(2)}) collective-permute-start(bf16[224,1408]{1,0:T(8,128)(2,1)} %get-tuple-element.27), channel_id=1, source_target_pairs={{0,96},{32,0},{64,32},{96,64},{1,97},{33,1},{65,33},{97,65},{2,98}... | collective-permute-start | bytes 1892360 | tf_op jit(solution)/shard_map/ppermute | solution.py:344
  8.1 8.6 %space_forward.1 = (bf16[256,2112]{1,0:T(8,128)(2,1)}, bf16[8,256,256]{2,1,0:T(8,128)(2,1)}, bf16[256,2112]{1,0:T(8,128)(2,1)}) custom-call(bf16[256,1408]{1,0:T(8,128)(2,1)} %bitcast.23, bf16[2112,1408]{1,0:T(8,128)(2,1)} %bitcast.15, bf16[704,1408]{1,0:T(8,128)(2,1)} %bitcast.17), custom_call_target="tpu_custom_call" | custom-call | flops 2200000000 | bytes 11000000 | tf_op jit(solution)/shard_map/space_forward/pallas_call | solution.py:36
  16.7 7.6 %all-to-all-start.1 = ((bf16[32,8,2112]{2,1,0:T(8,128)(2,1)}), bf16[32,8,2112]{2,1,0:T(8,128)(2,1)}, u32[]{:S(2)}, u32[]{:S(2)}) async-start(bf16[32,8,2112]{2,1,0:T(8,128)(2,1)} %bitcast.29), calls=%async_computation.1 | async-start | bytes 2228224 | tf_op jit(solution)/shard_map/all_to_all | solution.py:339
  24.4 3.3 %collective-permute-start.3 = (bf16[80,1408]{1,0:T(8,128)(2,1)S(1)}, bf16[80,1408]{1,0:T(8,128)(2,1)S(1)}, u32[]{:S(2)}, u32[]{:S(2)}) collective-permute-start(bf16[80,1408]{1,0:T(8,128)(2,1)S(1)} %slice.13), channel_id=1, source_target_pairs={{0,96},{32,0},{64,32},{96,64},{1,97},{33,1},{65,33},{97,65},{2,98}... | collective-permute-start | bytes 675848 | tf_op jit(solution)/shard_map/ppermute | solution.py:344
  27.8 5.4 %collective-permute-done.2.far0_ref = bf16[80,1408]{1,0:T(8,128)(2,1)S(1)} collective-permute-done((bf16[80,1408]{1,0:T(8,128)(2,1)S(1)}, bf16[80,1408]{1,0:T(8,128)(2,1)S(1)}, u32[]{:S(2)}, u32[]{:S(2)}) %collective-permute-start.2) | collective-permute-done | bytes 225312 | tf_op jit(solution)/shard_map/ppermute | solution.py:344
  33.2 2.2 %scatter_rows.1 = (bf16[256,1408]{1,0:T(8,128)(2,1)S(1)}, bf16[128,1408]{1,0:T(8,128)(2,1)S(1)}, bf16[128,1408]{1,0:T(8,128)(2,1)S(1)}) custom-call(s32[2]{0:T(128)S(1)} %pad_add_fusion.place_ref.refs_0_, bf16[144,1408]{1,0:T(8,128)(2,1)S(1)} %copy-done.8, bf16[224,1408]{1,0:T(8,128)(2,1)S(1)} %collective-permute-done.next_ref, ...), custom_call_target="tpu_custom_call" | custom-call | flops 1000000 | bytes 5000 | tf_op jit(solution)/shard_map/scatter_rows/pallas_call | solution.py:36
  36.0 1.2 collective-permute-done.4.refs_0_
  37.2 0.5 collective-permute-done.5.refs_1_
  37.7 0.9 join_rows.1
  38.6 3.8 %all-to-all-done.1 = bf16[32,8,2112]{2,1,0:T(8,128)(2,1)} async-done(((bf16[32,8,2112]{2,1,0:T(8,128)(2,1)}), bf16[32,8,2112]{2,1,0:T(8,128)(2,1)}, u32[]{:S(2)}, u32[]{:S(2)}) %all-to-all-start.1) | async-done | bytes 1081376 | tf_op jit(solution)/shard_map/all_to_all | solution.py:339
  42.4 4.1 %all-to-all-start = ((bf16[32,8,1408]{2,1,0:T(8,128)(2,1)}), bf16[32,8,1408]{2,1,0:T(8,128)(2,1)S(1)}, u32[]{:S(2)}, u32[]{:S(2)}) async-start(bf16[32,8,1408]{2,1,0:T(8,128)(2,1)} %bitcast.6), calls=%async_computation | async-start | bytes 1441792 | tf_op jit(solution)/shard_map/all_to_all | solution.py:339
  46.5 7.5 %time_forward.1 = (bf16[256,2112]{1,0:T(8,128)(2,1)}, bf16[8,256,256]{2,1,0:T(8,128)(2,1)}, bf16[256,704]{1,0:T(8,128)(2,1)}) custom-call(bf16[256,2112]{1,0:T(8,128)(2,1)} %bitcast.9.refs_0_.stream_in, bf16[2112,1408]{1,0:T(8,128)(2,1)} %bitcast.25), custom_call_target="tpu_custom_call" | custom-call | flops 2200000000 | bytes 11000000 | tf_op jit(solution)/shard_map/time_forward/pallas_call | solution.py:36
  54.0 6.3 %all-to-all-done = bf16[32,8,1408]{2,1,0:T(8,128)(2,1)S(1)} async-done(((bf16[32,8,1408]{2,1,0:T(8,128)(2,1)}), bf16[32,8,1408]{2,1,0:T(8,128)(2,1)S(1)}, u32[]{:S(2)}, u32[]{:S(2)}) %all-to-all-start) | async-done | bytes 720928 | tf_op jit(solution)/shard_map/all_to_all | solution.py:339
  60.3 0.9 copy-done.3
  61.2 10.3 %time_backward.1.refs_2_ = bf16[256,1408]{1,0:T(8,128)(2,1)} custom-call(bf16[256,1408]{1,0:T(8,128)(2,1)} %bitcast.20, bf16[256,2112]{1,0:T(8,128)(2,1)} %bitcast.9.refs_0_.stream_in, bf16[256,2112]{1,0:T(8,128)(2,1)} %get-tuple-element.31.projected_in, bf16[8,256,256]{2,1,0:T(8,128)(2,1)} %get-tuple-element.32.probs_in, bf16[2112,1408]{1,0:T(8,128)(2,1)} %bitcast.26, ...), custom_call_target="tpu_custom_call" | custom-call | flops 2600000000 | bytes 13000000 | tf_op jit(solution)/shard_map/time_backward/pallas_call | solution.py:36
  71.5 4.0 %all-to-all-start.2 = ((bf16[32,8,1408]{2,1,0:T(8,128)(2,1)}), bf16[32,8,1408]{2,1,0:T(8,128)(2,1)S(1)}, u32[]{:S(2)}, u32[]{:S(2)}) async-start(bf16[32,8,1408]{2,1,0:T(8,128)(2,1)} %bitcast.19), calls=%async_computation.2 | async-start | bytes 1441792 | tf_op jit(solution)/shard_map/all_to_all | solution.py:339
  75.6 1.0 slice.14.refs_5_
  77.3 1.1 split_features.1
  79.0 1.2 collective-permute-done.6.refs_2_
  80.1 0.6 collective-permute-done.8.refs_6_
  80.7 2.7 %pack_shares.1 = bf16[64,16,1024]{2,1,0:T(8,128)(2,1)} custom-call(bf16[256,704]{1,0:T(8,128)(2,1)S(1)} %get-tuple-element.35.refs_0_, bf16[256,704]{1,0:T(8,128)(2,1)S(1)} %copy-done.9, bf16[256,704]{1,0:T(8,128)(2,1)S(1)} %collective-permute-done.6.refs_2_, bf16[256,704]{1,0:T(8,128)(2,1)S(1)} %collective-permute-done.7.refs_3_, ...), custom_call_target="tpu_custom_call" | custom-call | flops 1000000 | bytes 5000 | tf_op jit(solution)/shard_map/pack_shares/pallas_call | solution.py:36
  83.4 6.2 %all-to-all-done.2 = bf16[32,8,1408]{2,1,0:T(8,128)(2,1)S(1)} async-done(((bf16[32,8,1408]{2,1,0:T(8,128)(2,1)}), bf16[32,8,1408]{2,1,0:T(8,128)(2,1)S(1)}, u32[]{:S(2)}, u32[]{:S(2)}) %all-to-all-start.2) | async-done | bytes 720928 | tf_op jit(solution)/shard_map/all_to_all | solution.py:339
  89.6 6.3 %all-to-all-start.3 = ((bf16[64,16,1024]{2,1,0:T(8,128)(2,1)}), bf16[64,16,1024]{2,1,0:T(8,128)(2,1)S(1)}, u32[]{:S(2)}, u32[]{:S(2)}) async-start(bf16[64,16,1024]{2,1,0:T(8,128)(2,1)} %pack_shares.1), calls=%async_computation.3 | async-start | bytes 4194304 | tf_op jit(solution)/shard_map/all_to_all | solution.py:396
  95.9 2.7 %copy-done = bf16[1408,2112]{0,1:T(8,128)(2,1)S(1)} copy-done((bf16[1408,2112]{0,1:T(8,128)(2,1)S(1)}, bf16[1408,2112]{0,1:T(8,128)(2,1)}, u32[]{:S(2)}) %copy-start) | copy-done | bytes 5947416
  98.5 1.5 %copy-done.1 = bf16[1408,704]{0,1:T(8,128)(2,1)S(1)} copy-done((bf16[1408,704]{0,1:T(8,128)(2,1)S(1)}, bf16[1408,704]{0,1:T(8,128)(2,1)}, u32[]{:S(2)}) %copy-start.1) | copy-done | bytes 1982488
  100.1 1.2 copy-done.6
  101.3 1.2 copy-done.7
  102.6 10.2 %space_backward.1 = bf16[256,1408]{1,0:T(8,128)(2,1)} custom-call(bf16[256,1408]{1,0:T(8,128)(2,1)S(1)} %bitcast.22, bf16[256,1408]{1,0:T(8,128)(2,1)S(1)} %bitcast.24, bf16[256,2112]{1,0:T(8,128)(2,1)S(1)} %copy-done.6, bf16[8,256,256]{2,1,0:T(8,128)(2,1)S(1)} %copy-done.7, bf16[2112,1408]{1,0:T(8,128)(2,1)S(1)} %bitcast.16, bf16[704,1408]{1,0:T(8,128)(2,1)S(1)} %bitcast.18), custom_call_target="tpu_custom_call" | custom-call | flops 2600000000 | bytes 13000000 | tf_op jit(solution)/shard_map/space_backward/pallas_call | solution.py:36
  112.8 12.9 %all-to-all-done.3.parts_ref = bf16[64,16,1024]{2,1,0:T(8,128)(2,1)S(1)} async-done(((bf16[64,16,1024]{2,1,0:T(8,128)(2,1)}), bf16[64,16,1024]{2,1,0:T(8,128)(2,1)S(1)}, u32[]{:S(2)}, u32[]{:S(2)}) %all-to-all-start.3) | async-done | bytes 2097184 | tf_op jit(solution)/shard_map/all_to_all | solution.py:396
  125.7 1.0 sum_shares.1
  (30 shorter events, 2.1 us)
Async XLA Ops:
  3.8 20.4 %collective-permute-start = (bf16[224,1408]{1,0:T(8,128)(2,1)}, bf16[224,1408]{1,0:T(8,128)(2,1)S(1)}, u32[]{:S(2)}, u32[]{:S(2)}) collective-permute-start(bf16[224,1408]{1,0:T(8,128)(2,1)} %get-tuple-element.26), channel_id=1, source_target_pairs={{0,32},{32,64},{64,96},{96,0},{1,33},{33,65},{65,97},{97,1},{2,34}... | collective-permute-start | bytes 1892360 | tf_op jit(solution)/shard_map/ppermute | solution.py:344
  5.9 18.5 %collective-permute-start.1 = (bf16[224,1408]{1,0:T(8,128)(2,1)}, bf16[224,1408]{1,0:T(8,128)(2,1)S(1)}, u32[]{:S(2)}, u32[]{:S(2)}) collective-permute-start(bf16[224,1408]{1,0:T(8,128)(2,1)} %get-tuple-element.27), channel_id=1, source_target_pairs={{0,96},{32,0},{64,32},{96,64},{1,97},{33,1},{65,33},{97,65},{2,98}... | collective-permute-start | bytes 1892360 | tf_op jit(solution)/shard_map/ppermute | solution.py:344
  16.7 16.6 %copy-start.8 = (bf16[144,1408]{1,0:T(8,128)(2,1)S(1)}, bf16[144,1408]{1,0:T(8,128)(2,1)}, u32[]{:S(2)}) copy-start(bf16[144,1408]{1,0:T(8,128)(2,1)} %get-tuple-element.25.keep_ref) | copy-start | bytes 1216516
  16.7 25.7 %all-to-all-start.1 = ((bf16[32,8,2112]{2,1,0:T(8,128)(2,1)}), bf16[32,8,2112]{2,1,0:T(8,128)(2,1)}, u32[]{:S(2)}, u32[]{:S(2)}) async-start(bf16[32,8,2112]{2,1,0:T(8,128)(2,1)} %bitcast.29), calls=%async_computation.1 | async-start | bytes 2228224 | tf_op jit(solution)/shard_map/all_to_all | solution.py:339
  24.3 8.9 %collective-permute-start.2 = (bf16[80,1408]{1,0:T(8,128)(2,1)S(1)}, bf16[80,1408]{1,0:T(8,128)(2,1)S(1)}, u32[]{:S(2)}, u32[]{:S(2)}) collective-permute-start(bf16[80,1408]{1,0:T(8,128)(2,1)S(1)} %slice.12), channel_id=1, source_target_pairs={{0,32},{32,64},{64,96},{96,0},{1,33},{33,65},{65,97},{97,1},{2,34}... | collective-permute-start | bytes 675848 | tf_op jit(solution)/shard_map/ppermute | solution.py:344
  24.4 8.8 %collective-permute-start.3 = (bf16[80,1408]{1,0:T(8,128)(2,1)S(1)}, bf16[80,1408]{1,0:T(8,128)(2,1)S(1)}, u32[]{:S(2)}, u32[]{:S(2)}) collective-permute-start(bf16[80,1408]{1,0:T(8,128)(2,1)S(1)} %slice.13), channel_id=1, source_target_pairs={{0,96},{32,0},{64,32},{96,64},{1,97},{33,1},{65,33},{97,65},{2,98}... | collective-permute-start | bytes 675848 | tf_op jit(solution)/shard_map/ppermute | solution.py:344
  35.4 1.8 %collective-permute-start.4 = (bf16[128,1408]{1,0:T(8,128)(2,1)S(1)}, bf16[128,1408]{1,0:T(8,128)(2,1)S(1)}, u32[]{:S(2)}, u32[]{:S(2)}) collective-permute-start(bf16[128,1408]{1,0:T(8,128)(2,1)S(1)} %get-tuple-element.29), channel_id=1, source_target_pairs={{0,16},{16,0},{1,17},{17,1},{2,18},{18,2},{3,19},{19,3},{4,20},{20... | collective-permute-start | bytes 1081352 | tf_op jit(solution)/shard_map/ppermute | solution.py:344
  35.5 2.2 %collective-permute-start.5 = (bf16[128,1408]{1,0:T(8,128)(2,1)S(1)}, bf16[128,1408]{1,0:T(8,128)(2,1)S(1)}, u32[]{:S(2)}, u32[]{:S(2)}) collective-permute-start(bf16[128,1408]{1,0:T(8,128)(2,1)S(1)} %get-tuple-element.30), channel_id=1, source_target_pairs={{0,16},{16,0},{1,17},{17,1},{2,18},{18,2},{3,19},{19,3},{4,20},{20... | collective-permute-start | bytes 1081352 | tf_op jit(solution)/shard_map/ppermute | solution.py:344
  42.4 17.9 %all-to-all-start = ((bf16[32,8,1408]{2,1,0:T(8,128)(2,1)}), bf16[32,8,1408]{2,1,0:T(8,128)(2,1)S(1)}, u32[]{:S(2)}, u32[]{:S(2)}) async-start(bf16[32,8,1408]{2,1,0:T(8,128)(2,1)} %bitcast.6), calls=%async_computation | async-start | bytes 1441792 | tf_op jit(solution)/shard_map/all_to_all | solution.py:339
  60.3 0.9 copy-start.3
  71.5 5.1 %copy-start.9 = (bf16[256,704]{1,0:T(8,128)(2,1)S(1)}, bf16[256,704]{1,0:T(8,128)(2,1)}, u32[]{:S(2)}) copy-start(bf16[256,704]{1,0:T(8,128)(2,1)} %get-tuple-element.36.refs_1_) | copy-start | bytes 1081348
  71.5 5.8 %copy-start.2 = (bf16[256,1408]{1,0:T(8,128)(2,1)S(1)}, bf16[256,1408]{1,0:T(8,128)(2,1)}, u32[]{:S(2)}) copy-start(bf16[256,1408]{1,0:T(8,128)(2,1)} %time_backward.1.refs_2_) | copy-start | bytes 2162692
  71.5 5.8 %copy-start.4 = (bf16[32,8,1408]{2,1,0:T(8,128)(2,1)S(1)}, bf16[32,8,1408]{2,1,0:T(8,128)(2,1)}, u32[]{:S(2)}) copy-start(bf16[32,8,1408]{2,1,0:T(8,128)(2,1)} %copy-done.3) | copy-start | bytes 2162692
  71.5 18.1 %all-to-all-start.2 = ((bf16[32,8,1408]{2,1,0:T(8,128)(2,1)}), bf16[32,8,1408]{2,1,0:T(8,128)(2,1)S(1)}, u32[]{:S(2)}, u32[]{:S(2)}) async-start(bf16[32,8,1408]{2,1,0:T(8,128)(2,1)} %bitcast.19), calls=%async_computation.2 | async-start | bytes 1441792 | tf_op jit(solution)/shard_map/all_to_all | solution.py:339
  76.6 2.3 %collective-permute-start.7 = (bf16[256,704]{1,0:T(8,128)(2,1)S(1)}, bf16[256,704]{1,0:T(8,128)(2,1)S(1)}, u32[]{:S(2)}, u32[]{:S(2)}) collective-permute-start(bf16[256,704]{1,0:T(8,128)(2,1)S(1)} %copy-done.9), channel_id=1, source_target_pairs={{0,16},{16,0},{1,17},{17,1},{2,18},{18,2},{3,19},{19,3},{4,20},{20... | collective-permute-start | bytes 1081352 | tf_op jit(solution)/shard_map/ppermute | solution.py:344
  76.9 2.0 %collective-permute-start.9 = (bf16[256,704]{1,0:T(8,128)(2,1)S(1)}, bf16[256,704]{1,0:T(8,128)(2,1)S(1)}, u32[]{:S(2)}, u32[]{:S(2)}) collective-permute-start(bf16[256,704]{1,0:T(8,128)(2,1)S(1)} %slice.14.refs_5_), channel_id=1, source_target_pairs={{0,16},{16,0},{1,17},{17,1},{2,18},{18,2},{3,19},{19,3},{4,20},{20... | collective-permute-start | bytes 1081352 | tf_op jit(solution)/shard_map/ppermute | solution.py:344
  78.3 1.8 %collective-permute-start.6 = (bf16[256,704]{1,0:T(8,128)(2,1)S(1)}, bf16[256,704]{1,0:T(8,128)(2,1)S(1)}, u32[]{:S(2)}, u32[]{:S(2)}) collective-permute-start(bf16[256,704]{1,0:T(8,128)(2,1)S(1)} %get-tuple-element.37), channel_id=1, source_target_pairs={{0,16},{16,0},{1,17},{17,1},{2,18},{18,2},{3,19},{19,3},{4,20},{20... | collective-permute-start | bytes 1081352 | tf_op jit(solution)/shard_map/ppermute | solution.py:344
  78.7 2.0 %collective-permute-start.8 = (bf16[256,704]{1,0:T(8,128)(2,1)S(1)}, bf16[256,704]{1,0:T(8,128)(2,1)S(1)}, u32[]{:S(2)}, u32[]{:S(2)}) collective-permute-start(bf16[256,704]{1,0:T(8,128)(2,1)S(1)} %get-tuple-element.39), channel_id=1, source_target_pairs={{0,16},{16,0},{1,17},{17,1},{2,18},{18,2},{3,19},{19,3},{4,20},{20... | collective-permute-start | bytes 1081352 | tf_op jit(solution)/shard_map/ppermute | solution.py:344
  89.6 6.3 %copy-start.5 = (bf16[1,256,1408]{2,1,0:T(8,128)(2,1)S(1)}, bf16[1,256,1408]{2,1,0:T(8,128)(2,1)}, u32[]{:S(2)}) copy-start(bf16[1,256,1408]{2,1,0:T(8,128)(2,1)} %param.8) | copy-start | bytes 2162692
  89.6 36.1 %all-to-all-start.3 = ((bf16[64,16,1024]{2,1,0:T(8,128)(2,1)}), bf16[64,16,1024]{2,1,0:T(8,128)(2,1)S(1)}, u32[]{:S(2)}, u32[]{:S(2)}) async-start(bf16[64,16,1024]{2,1,0:T(8,128)(2,1)} %pack_shares.1), calls=%async_computation.3 | async-start | bytes 4194304 | tf_op jit(solution)/shard_map/all_to_all | solution.py:396
  95.8 2.7 %copy-start = (bf16[1408,2112]{0,1:T(8,128)(2,1)S(1)}, bf16[1408,2112]{0,1:T(8,128)(2,1)}, u32[]{:S(2)}) copy-start(bf16[1408,2112]{0,1:T(8,128)(2,1)} %param.12) | copy-start | bytes 17842180
  98.5 1.6 %copy-start.1 = (bf16[1408,704]{0,1:T(8,128)(2,1)S(1)}, bf16[1408,704]{0,1:T(8,128)(2,1)}, u32[]{:S(2)}) copy-start(bf16[1408,704]{0,1:T(8,128)(2,1)} %param.13) | copy-start | bytes 5947396
  100.1 1.2 copy-start.6
  101.3 1.2 copy-start.7

commit v7 on v6

--- a/solution.py
+++ b/solution.py
@@ -215,31 +215,48 @@
     return call(backward_kernel, bf16(*grad.shape), args, name, "a" * 7, scratch, 2.6e9, room)
 
 
-def aim_kernel(counts_ref, targets_in, rows_in, keep_ref, next_ref, last_ref, targets, sems):
+def put_targets(counts_ref, targets, ref, to, at):
+    line = lax.broadcasted_iota(jnp.int32, (16, 64), 0)
+    slot = lax.broadcasted_iota(jnp.int32, (16, 64), 1)
+    aims = jnp.full((16, 64), -1, jnp.int32)
+    for core in range(2):
+        valid = (line == core) & (slot < counts_ref[0, 0, 2 * to + core])
+        aims = jnp.where(valid, targets[0, 0, pl.ds(2 * to + core, 1), :], aims)
+    ref[at : at + 16, :] = jnp.zeros((16, ref.shape[1]), jnp.bfloat16)
+    ref[at : at + 16, :64] = aims.astype(jnp.float32).astype(jnp.bfloat16)
+
+
+def aim_kernel(counts_ref, targets_in, rows_in, next_ref, last_ref, targets, sems):
     chips = rows_in.shape[0]
     own = lax.axis_index("z")
     far = (own + 2) % chips
-    near = ((keep_ref, own), (next_ref, (own + 1) % chips), (last_ref, (own + chips - 1) % chips))
+    near = ((next_ref, (own + 1) % chips), (last_ref, (own + chips - 1) % chips))
     loads = [pltpu.make_async_copy(targets_in, targets, sems.at[0])]
     for i, (ref, to) in enumerate(near):
         loads.append(pltpu.make_async_copy(rows_in.at[to], ref.at[pl.ds(0, 128)], sems.at[1 + i]))
-    for i, ref in enumerate((next_ref, last_ref)):
         source = rows_in.at[far, pl.ds(64 * i, 64)]
-        loads.append(pltpu.make_async_copy(source, ref.at[pl.ds(144, 64)], sems.at[4 + i]))
+        loads.append(pltpu.make_async_copy(source, ref.at[pl.ds(144, 64)], sems.at[3 + i]))
     for load in loads:
         load.start()
-    line = lax.broadcasted_iota(jnp.int32, (16, 64), 0)
-    slot = lax.broadcasted_iota(jnp.int32, (16, 64), 1)
     loads[0].wait()
-    for ref, to, at in [(ref, to, 128) for ref, to in near] + [(next_ref, far, 208), (last_ref, far, 208)]:
-        aims = jnp.full((16, 64), -1, jnp.int32)
-        for core in range(2):
-            valid = (line == core) & (slot < counts_ref[0, 0, 2 * to + core])
-            aims = jnp.where(valid, targets[0, 0, pl.ds(2 * to + core, 1), :], aims)
-        ref[at : at + 16, :] = jnp.zeros((16, ref.shape[1]), jnp.bfloat16)
-        ref[at : at + 16, :64] = aims.astype(jnp.float32).astype(jnp.bfloat16)
+    for ref, to in near:
+        put_targets(counts_ref, targets, ref, to, 128)
+        put_targets(counts_ref, targets, ref, far, 208)
     for load in loads[1:]:
         load.wait()
+
+
+def keep_kernel(counts_ref, targets_in, rows_in, keep_ref, targets, sems):
+    own = lax.axis_index("z")
+    loads = [
+        pltpu.make_async_copy(targets_in, targets, sems.at[0]),
+        pltpu.make_async_copy(rows_in.at[own], keep_ref.at[pl.ds(0, 128)], sems.at[1]),
+    ]
+    for load in loads:
+        load.start()
+    loads[0].wait()
+    put_targets(counts_ref, targets, keep_ref, own, 128)
+    loads[1].wait()
 
 
 def scatter_kernel(place_ref, keep_ref, next_ref, last_ref, far0_ref, far1_ref, mine_ref, *other_refs):
@@ -358,8 +375,8 @@
 
     args = [counts, targets, grad_rows.reshape(chips, 128, width)]
     scratch = [pltpu.VMEM(targets.shape, jnp.int32), pltpu.SemaphoreType.DMA((6,))]
-    outs = [bf16(144, width), bf16(224, width), bf16(224, width)]
-    keep, to_next, to_last = call(aim_kernel, outs, args, "aim_rows", "saavvv", scratch, room=60)
+    outs = [bf16(224, width), bf16(224, width)]
+    to_next, to_last = call(aim_kernel, outs, args, "aim_rows", "saavv", scratch, room=60)
     from_last, from_next = shift(to_next, "z", 1), shift(to_last, "z", chips - 1)
     far = [shift(from_last[144:], "z", 1), shift(from_next[144:], "z", chips - 1)]
 
@@ -367,6 +384,8 @@
     hidden = exchange(space_saved[2], CLIP)
 
     place = after(place, space_saved[2])
+    keep_args = [after(counts, space_saved[2])] + args[1:]
+    keep = call(keep_kernel, bf16(144, width), keep_args, "keep_rows", "saav", scratch, room=60)
     args = [place, keep, from_last, from_next, *far]
     cuts = 2
     outs = [bf16(tokens, width)] + [bf16(tokens // cuts, width)] * cuts

time: 127 us -> 128 us (level)
  waiting for transfers between devices: 38 us -> 34.5 us
  Pallas kernels: 47.7 us -> 50 us
    ppermute x10, waiting for transfers between devices: 8.9 us -> 6.5 us  [shift(): lax.ppermute(array, axis, [(i, (i + by) % devices) for i in range(devices)])]
    pallas_call x10 -> x11, Pallas kernels: 47.7 us -> 50 us  [call(): pl.pallas_call(kernel, out_shape=outs, in_specs=spaces[:len(args)], out_s...]
    unnamed x20 -> x22, local copies, waits for them, and re-layouts: 7.58 us -> 8.58 us
  transfers between devices with their start and end apart: 14 -> 14, of which waited for: 9 -> 9; matrix products, arithmetic and copies ran while one was open for 1% -> 1% of each run, Pallas kernels for 26% -> 28%
where the time goes in v7:
time: 128 us; the launch traced here: 127 us
  Pallas kernels  50 us (39%)
  waiting for transfers between devices  34.5 us (27%)
  starting transfers between devices  32.2 us (25%)
  local copies, waits for them, and re-layouts  9.64 us (8%)
    pallas_call x11, Pallas kernels, call(): pl.pallas_call(kernel, out_shape=outs, in_specs=spaces[:len(args)], out_s...  50 us
    all_to_all x3, starting transfers between devices, exchange(): lax.all_to_all(cut, axes, split_axis=0, concat_axis=0, tiled=True)  16.1 us
    all_to_all x3, waiting for transfers between devices, exchange(): lax.all_to_all(cut, axes, split_axis=0, concat_axis=0, tiled=True)  15.1 us
    all_to_all x1, waiting for transfers between devices, body(): lax.all_to_all(packed, ('z', 'space'), split_axis=0, concat_axis=0, tiled...  12.9 us
    ppermute x10, starting transfers between devices, shift(): lax.ppermute(array, axis, [(i, (i + by) % devices) for i in range(devices)])  9.45 us
    unnamed x22, local copies, waits for them, and re-layouts  8.58 us
    all_to_all x1, starting transfers between devices, body(): lax.all_to_all(packed, ('z', 'space'), split_axis=0, concat_axis=0, tiled...  6.67 us
    ppermute x10, waiting for transfers between devices, shift(): lax.ppermute(array, axis, [(i, (i + by) % devices) for i in range(devices)])  6.5 us
  transfers between devices with their start and end apart: 14, of which 9 were waited for; matrix products, arithmetic and copies ran while one was open for 1% of the time, Pallas kernels for 28%

profile of v7, /device:TPU:0, one launch (start us, length us, event | category | flops | bytes accessed | tf_op | source)
XLA Modules:
  0.0 127.3 jit_solution(16134226374077105132)
XLA Ops:
  0.6 3.0 %aim_rows.1 = (bf16[224,1408]{1,0:T(8,128)(2,1)}, bf16[224,1408]{1,0:T(8,128)(2,1)}) custom-call(s32[1,1,8]{2,1,0:T(1,128)} %counts_ref.2, s32[1,1,8,64]{3,2,1,0:T(8,128)} %targets_in.3, bf16[4,128,1408]{2,1,0:T(8,128)(2,1)} %bitcast.30), custom_call_target="tpu_custom_call" | custom-call | flops 1000000 | bytes 5000 | tf_op jit(solution)/shard_map/aim_rows/pallas_call | solution.py:36
  3.6 2.1 %collective-permute-start = (bf16[224,1408]{1,0:T(8,128)(2,1)}, bf16[224,1408]{1,0:T(8,128)(2,1)S(1)}, u32[]{:S(2)}, u32[]{:S(2)}) collective-permute-start(bf16[224,1408]{1,0:T(8,128)(2,1)} %get-tuple-element.26), channel_id=1, source_target_pairs={{0,32},{32,64},{64,96},{96,0},{1,33},{33,65},{65,97},{97,1},{2,34}... | collective-permute-start | bytes 1892360 | tf_op jit(solution)/shard_map/ppermute | solution.py:361
  5.7 2.2 %collective-permute-start.1 = (bf16[224,1408]{1,0:T(8,128)(2,1)}, bf16[224,1408]{1,0:T(8,128)(2,1)S(1)}, u32[]{:S(2)}, u32[]{:S(2)}) collective-permute-start(bf16[224,1408]{1,0:T(8,128)(2,1)} %get-tuple-element.27), channel_id=1, source_target_pairs={{0,96},{32,0},{64,32},{96,64},{1,97},{33,1},{65,33},{97,65},{2,98}... | collective-permute-start | bytes 1892360 | tf_op jit(solution)/shard_map/ppermute | solution.py:361
  7.9 8.6 %space_forward.1 = (bf16[256,2112]{1,0:T(8,128)(2,1)}, bf16[8,256,256]{2,1,0:T(8,128)(2,1)}, bf16[256,2112]{1,0:T(8,128)(2,1)}) custom-call(bf16[256,1408]{1,0:T(8,128)(2,1)} %bitcast.23, bf16[2112,1408]{1,0:T(8,128)(2,1)} %bitcast.15, bf16[704,1408]{1,0:T(8,128)(2,1)} %bitcast.17), custom_call_target="tpu_custom_call" | custom-call | flops 2200000000 | bytes 11000000 | tf_op jit(solution)/shard_map/space_forward/pallas_call | solution.py:36
  16.5 7.3 %all-to-all-start.1 = ((bf16[32,8,2112]{2,1,0:T(8,128)(2,1)}), bf16[32,8,2112]{2,1,0:T(8,128)(2,1)S(1)}, u32[]{:S(2)}, u32[]{:S(2)}) async-start(bf16[32,8,2112]{2,1,0:T(8,128)(2,1)} %bitcast.33), calls=%async_computation.1 | async-start | bytes 2228224 | tf_op jit(solution)/shard_map/all_to_all | solution.py:356
  24.0 3.3 %collective-permute-start.3 = (bf16[80,1408]{1,0:T(8,128)(2,1)S(1)}, bf16[80,1408]{1,0:T(8,128)(2,1)S(1)}, u32[]{:S(2)}, u32[]{:S(2)}) collective-permute-start(bf16[80,1408]{1,0:T(8,128)(2,1)S(1)} %slice.13), channel_id=1, source_target_pairs={{0,96},{32,0},{64,32},{96,64},{1,97},{33,1},{65,33},{97,65},{2,98}... | collective-permute-start | bytes 675848 | tf_op jit(solution)/shard_map/ppermute | solution.py:361
  27.3 2.5 %keep_rows.1.keep_ref = bf16[144,1408]{1,0:T(8,128)(2,1)} custom-call(s32[1,1,8]{2,1,0:T(1,128)} %counts_ref.2, s32[1,1,8,64]{3,2,1,0:T(8,128)} %targets_in.3, bf16[4,128,1408]{2,1,0:T(8,128)(2,1)} %bitcast.31), custom_call_target="tpu_custom_call" | custom-call | flops 1000000 | bytes 5000 | tf_op jit(solution)/shard_map/keep_rows/pallas_call | solution.py:36
  29.8 3.0 %collective-permute-done.2.far0_ref = bf16[80,1408]{1,0:T(8,128)(2,1)S(1)} collective-permute-done((bf16[80,1408]{1,0:T(8,128)(2,1)S(1)}, bf16[80,1408]{1,0:T(8,128)(2,1)S(1)}, u32[]{:S(2)}, u32[]{:S(2)}) %collective-permute-start.2) | collective-permute-done | bytes 225312 | tf_op jit(solution)/shard_map/ppermute | solution.py:361
  32.9 1.0 copy-done.6
  33.9 2.2 %scatter_rows.1 = (bf16[256,1408]{1,0:T(8,128)(2,1)S(1)}, bf16[128,1408]{1,0:T(8,128)(2,1)S(1)}, bf16[128,1408]{1,0:T(8,128)(2,1)S(1)}) custom-call(s32[2]{0:T(128)S(1)} %pad_add_fusion.place_ref.refs_0_, bf16[144,1408]{1,0:T(8,128)(2,1)S(1)} %copy-done.6, bf16[224,1408]{1,0:T(8,128)(2,1)S(1)} %collective-permute-done.next_ref, ...), custom_call_target="tpu_custom_call" | custom-call | flops 1000000 | bytes 5000 | tf_op jit(solution)/shard_map/scatter_rows/pallas_call | solution.py:36
  36.6 1.2 collective-permute-done.4.refs_0_
  38.3 0.9 join_rows.1
  39.3 2.7 %all-to-all-done.1 = bf16[32,8,2112]{2,1,0:T(8,128)(2,1)S(1)} async-done(((bf16[32,8,2112]{2,1,0:T(8,128)(2,1)}), bf16[32,8,2112]{2,1,0:T(8,128)(2,1)S(1)}, u32[]{:S(2)}, u32[]{:S(2)}) %all-to-all-start.1) | async-done | bytes 1081376 | tf_op jit(solution)/shard_map/all_to_all | solution.py:356
  42.0 4.7 %all-to-all-start = ((bf16[32,8,1408]{2,1,0:T(8,128)(2,1)}), bf16[32,8,1408]{2,1,0:T(8,128)(2,1)S(1)}, u32[]{:S(2)}, u32[]{:S(2)}) async-start(bf16[32,8,1408]{2,1,0:T(8,128)(2,1)} %bitcast.6), calls=%async_computation | async-start | bytes 1441792 | tf_op jit(solution)/shard_map/all_to_all | solution.py:356
  46.7 7.5 %time_forward.1 = (bf16[256,2112]{1,0:T(8,128)(2,1)}, bf16[8,256,256]{2,1,0:T(8,128)(2,1)}, bf16[256,704]{1,0:T(8,128)(2,1)}) custom-call(bf16[256,2112]{1,0:T(8,128)(2,1)} %bitcast.25, bf16[2112,1408]{1,0:T(8,128)(2,1)} %bitcast.28), custom_call_target="tpu_custom_call" | custom-call | flops 2200000000 | bytes 11000000 | tf_op jit(solution)/shard_map/time_forward/pallas_call | solution.py:36
  54.3 6.3 %all-to-all-done = bf16[32,8,1408]{2,1,0:T(8,128)(2,1)S(1)} async-done(((bf16[32,8,1408]{2,1,0:T(8,128)(2,1)}), bf16[32,8,1408]{2,1,0:T(8,128)(2,1)S(1)}, u32[]{:S(2)}, u32[]{:S(2)}) %all-to-all-start) | async-done | bytes 720928 | tf_op jit(solution)/shard_map/all_to_all | solution.py:356
  60.5 0.9 copy-done.3
  61.4 10.3 %time_backward.1.refs_2_ = bf16[256,1408]{1,0:T(8,128)(2,1)} custom-call(bf16[256,1408]{1,0:T(8,128)(2,1)} %bitcast.20, bf16[256,2112]{1,0:T(8,128)(2,1)} %bitcast.26, bf16[256,2112]{1,0:T(8,128)(2,1)} %get-tuple-element.31.projected_in, bf16[8,256,256]{2,1,0:T(8,128)(2,1)} %get-tuple-element.32.probs_in, bf16[2112,1408]{1,0:T(8,128)(2,1)} %bitcast.29, ...), custom_call_target="tpu_custom_call" | custom-call | flops 2600000000 | bytes 13000000 | tf_op jit(solution)/shard_map/time_backward/pallas_call | solution.py:36
  71.7 4.0 %all-to-all-start.2 = ((bf16[32,8,1408]{2,1,0:T(8,128)(2,1)}), bf16[32,8,1408]{2,1,0:T(8,128)(2,1)S(1)}, u32[]{:S(2)}, u32[]{:S(2)}) async-start(bf16[32,8,1408]{2,1,0:T(8,128)(2,1)} %bitcast.19), calls=%async_computation.2 | async-start | bytes 1441792 | tf_op jit(solution)/shard_map/all_to_all | solution.py:356
  75.8 1.0 slice.14.refs_5_
  77.5 1.1 split_features.1
  79.2 1.2 collective-permute-done.6.refs_2_
  80.9 2.7 %pack_shares.1 = bf16[64,16,1024]{2,1,0:T(8,128)(2,1)} custom-call(bf16[256,704]{1,0:T(8,128)(2,1)S(1)} %get-tuple-element.35.refs_0_, bf16[256,704]{1,0:T(8,128)(2,1)S(1)} %copy-done.9, bf16[256,704]{1,0:T(8,128)(2,1)S(1)} %collective-permute-done.6.refs_2_, bf16[256,704]{1,0:T(8,128)(2,1)S(1)} %collective-permute-done.7.refs_3_, ...), custom_call_target="tpu_custom_call" | custom-call | flops 1000000 | bytes 5000 | tf_op jit(solution)/shard_map/pack_shares/pallas_call | solution.py:36
  83.6 6.2 %all-to-all-done.2 = bf16[32,8,1408]{2,1,0:T(8,128)(2,1)S(1)} async-done(((bf16[32,8,1408]{2,1,0:T(8,128)(2,1)}), bf16[32,8,1408]{2,1,0:T(8,128)(2,1)S(1)}, u32[]{:S(2)}, u32[]{:S(2)}) %all-to-all-start.2) | async-done | bytes 720928 | tf_op jit(solution)/shard_map/all_to_all | solution.py:356
  89.8 6.7 %all-to-all-start.3 = ((bf16[64,16,1024]{2,1,0:T(8,128)(2,1)}), bf16[64,16,1024]{2,1,0:T(8,128)(2,1)S(1)}, u32[]{:S(2)}, u32[]{:S(2)}) async-start(bf16[64,16,1024]{2,1,0:T(8,128)(2,1)} %pack_shares.1), calls=%async_computation.3 | async-start | bytes 4194304 | tf_op jit(solution)/shard_map/all_to_all | solution.py:415
  96.5 2.7 %copy-done = bf16[1408,2112]{0,1:T(8,128)(2,1)S(1)} copy-done((bf16[1408,2112]{0,1:T(8,128)(2,1)S(1)}, bf16[1408,2112]{0,1:T(8,128)(2,1)}, u32[]{:S(2)}) %copy-start) | copy-done | bytes 5947416
  99.2 1.5 %copy-done.1 = bf16[1408,704]{0,1:T(8,128)(2,1)S(1)} copy-done((bf16[1408,704]{0,1:T(8,128)(2,1)S(1)}, bf16[1408,704]{0,1:T(8,128)(2,1)}, u32[]{:S(2)}) %copy-start.1) | copy-done | bytes 1982488
  100.7 1.2 copy-done.7
  102.0 1.2 copy-done.8
  103.2 10.2 %space_backward.1 = bf16[256,1408]{1,0:T(8,128)(2,1)} custom-call(bf16[256,1408]{1,0:T(8,128)(2,1)S(1)} %bitcast.22, bf16[256,1408]{1,0:T(8,128)(2,1)S(1)} %bitcast.24, bf16[256,2112]{1,0:T(8,128)(2,1)S(1)} %copy-done.7, bf16[8,256,256]{2,1,0:T(8,128)(2,1)S(1)} %copy-done.8, bf16[2112,1408]{1,0:T(8,128)(2,1)S(1)} %bitcast.16, bf16[704,1408]{1,0:T(8,128)(2,1)S(1)} %bitcast.18), custom_call_target="tpu_custom_call" | custom-call | flops 2600000000 | bytes 13000000 | tf_op jit(solution)/shard_map/space_backward/pallas_call | solution.py:36
  113.4 12.9 %all-to-all-done.3.parts_ref = bf16[64,16,1024]{2,1,0:T(8,128)(2,1)S(1)} async-done(((bf16[64,16,1024]{2,1,0:T(8,128)(2,1)}), bf16[64,16,1024]{2,1,0:T(8,128)(2,1)S(1)}, u32[]{:S(2)}, u32[]{:S(2)}) %all-to-all-start.3) | async-done | bytes 2097184 | tf_op jit(solution)/shard_map/all_to_all | solution.py:415
  126.3 0.9 sum_shares.1
  (33 shorter events, 3.2 us)
Async XLA Ops:
  3.6 20.2 %collective-permute-start = (bf16[224,1408]{1,0:T(8,128)(2,1)}, bf16[224,1408]{1,0:T(8,128)(2,1)S(1)}, u32[]{:S(2)}, u32[]{:S(2)}) collective-permute-start(bf16[224,1408]{1,0:T(8,128)(2,1)} %get-tuple-element.26), channel_id=1, source_target_pairs={{0,32},{32,64},{64,96},{96,0},{1,33},{33,65},{65,97},{97,1},{2,34}... | collective-permute-start | bytes 1892360 | tf_op jit(solution)/shard_map/ppermute | solution.py:361
  5.7 18.2 %collective-permute-start.1 = (bf16[224,1408]{1,0:T(8,128)(2,1)}, bf16[224,1408]{1,0:T(8,128)(2,1)S(1)}, u32[]{:S(2)}, u32[]{:S(2)}) collective-permute-start(bf16[224,1408]{1,0:T(8,128)(2,1)} %get-tuple-element.27), channel_id=1, source_target_pairs={{0,96},{32,0},{64,32},{96,64},{1,97},{33,1},{65,33},{97,65},{2,98}... | collective-permute-start | bytes 1892360 | tf_op jit(solution)/shard_map/ppermute | solution.py:361
  16.5 25.5 %all-to-all-start.1 = ((bf16[32,8,2112]{2,1,0:T(8,128)(2,1)}), bf16[32,8,2112]{2,1,0:T(8,128)(2,1)S(1)}, u32[]{:S(2)}, u32[]{:S(2)}) async-start(bf16[32,8,2112]{2,1,0:T(8,128)(2,1)} %bitcast.33), calls=%async_computation.1 | async-start | bytes 2228224 | tf_op jit(solution)/shard_map/all_to_all | solution.py:356
  23.9 9.0 %collective-permute-start.2 = (bf16[80,1408]{1,0:T(8,128)(2,1)S(1)}, bf16[80,1408]{1,0:T(8,128)(2,1)S(1)}, u32[]{:S(2)}, u32[]{:S(2)}) collective-permute-start(bf16[80,1408]{1,0:T(8,128)(2,1)S(1)} %slice.12), channel_id=1, source_target_pairs={{0,32},{32,64},{64,96},{96,0},{1,33},{33,65},{65,97},{97,1},{2,34}... | collective-permute-start | bytes 675848 | tf_op jit(solution)/shard_map/ppermute | solution.py:361
  24.0 8.9 %collective-permute-start.3 = (bf16[80,1408]{1,0:T(8,128)(2,1)S(1)}, bf16[80,1408]{1,0:T(8,128)(2,1)S(1)}, u32[]{:S(2)}, u32[]{:S(2)}) collective-permute-start(bf16[80,1408]{1,0:T(8,128)(2,1)S(1)} %slice.13), channel_id=1, source_target_pairs={{0,96},{32,0},{64,32},{96,64},{1,97},{33,1},{65,33},{97,65},{2,98}... | collective-permute-start | bytes 675848 | tf_op jit(solution)/shard_map/ppermute | solution.py:361
  32.8 1.0 copy-start.6
  36.0 1.8 %collective-permute-start.4 = (bf16[128,1408]{1,0:T(8,128)(2,1)S(1)}, bf16[128,1408]{1,0:T(8,128)(2,1)S(1)}, u32[]{:S(2)}, u32[]{:S(2)}) collective-permute-start(bf16[128,1408]{1,0:T(8,128)(2,1)S(1)} %get-tuple-element.29), channel_id=1, source_target_pairs={{0,16},{16,0},{1,17},{17,1},{2,18},{18,2},{3,19},{19,3},{4,20},{20... | collective-permute-start | bytes 1081352 | tf_op jit(solution)/shard_map/ppermute | solution.py:361
  36.1 2.2 %collective-permute-start.5 = (bf16[128,1408]{1,0:T(8,128)(2,1)S(1)}, bf16[128,1408]{1,0:T(8,128)(2,1)S(1)}, u32[]{:S(2)}, u32[]{:S(2)}) collective-permute-start(bf16[128,1408]{1,0:T(8,128)(2,1)S(1)} %get-tuple-element.30), channel_id=1, source_target_pairs={{0,16},{16,0},{1,17},{17,1},{2,18},{18,2},{3,19},{19,3},{4,20},{20... | collective-permute-start | bytes 1081352 | tf_op jit(solution)/shard_map/ppermute | solution.py:361
  42.0 4.7 %copy-start.10 = (bf16[32,8,2112]{2,1,0:T(8,128)(2,1)}, bf16[32,8,2112]{2,1,0:T(8,128)(2,1)S(1)}, u32[]{:S(2)}) copy-start(bf16[32,8,2112]{2,1,0:T(8,128)(2,1)S(1)} %all-to-all-done.1) | copy-start | bytes 3244036
  42.0 18.6 %all-to-all-start = ((bf16[32,8,1408]{2,1,0:T(8,128)(2,1)}), bf16[32,8,1408]{2,1,0:T(8,128)(2,1)S(1)}, u32[]{:S(2)}, u32[]{:S(2)}) async-start(bf16[32,8,1408]{2,1,0:T(8,128)(2,1)} %bitcast.6), calls=%async_computation | async-start | bytes 1441792 | tf_op jit(solution)/shard_map/all_to_all | solution.py:356
  60.5 0.9 copy-start.3
  71.7 5.1 %copy-start.9 = (bf16[256,704]{1,0:T(8,128)(2,1)S(1)}, bf16[256,704]{1,0:T(8,128)(2,1)}, u32[]{:S(2)}) copy-start(bf16[256,704]{1,0:T(8,128)(2,1)} %get-tuple-element.36.refs_1_) | copy-start | bytes 1081348
  71.7 5.8 %copy-start.2 = (bf16[256,1408]{1,0:T(8,128)(2,1)S(1)}, bf16[256,1408]{1,0:T(8,128)(2,1)}, u32[]{:S(2)}) copy-start(bf16[256,1408]{1,0:T(8,128)(2,1)} %time_backward.1.refs_2_) | copy-start | bytes 2162692
  71.7 5.8 %copy-start.4 = (bf16[32,8,1408]{2,1,0:T(8,128)(2,1)S(1)}, bf16[32,8,1408]{2,1,0:T(8,128)(2,1)}, u32[]{:S(2)}) copy-start(bf16[32,8,1408]{2,1,0:T(8,128)(2,1)} %copy-done.3) | copy-start | bytes 2162692
  71.7 18.1 %all-to-all-start.2 = ((bf16[32,8,1408]{2,1,0:T(8,128)(2,1)}), bf16[32,8,1408]{2,1,0:T(8,128)(2,1)S(1)}, u32[]{:S(2)}, u32[]{:S(2)}) async-start(bf16[32,8,1408]{2,1,0:T(8,128)(2,1)} %bitcast.19), calls=%async_computation.2 | async-start | bytes 1441792 | tf_op jit(solution)/shard_map/all_to_all | solution.py:356
  76.8 2.3 %collective-permute-start.7 = (bf16[256,704]{1,0:T(8,128)(2,1)S(1)}, bf16[256,704]{1,0:T(8,128)(2,1)S(1)}, u32[]{:S(2)}, u32[]{:S(2)}) collective-permute-start(bf16[256,704]{1,0:T(8,128)(2,1)S(1)} %copy-done.9), channel_id=1, source_target_pairs={{0,16},{16,0},{1,17},{17,1},{2,18},{18,2},{3,19},{19,3},{4,20},{20... | collective-permute-start | bytes 1081352 | tf_op jit(solution)/shard_map/ppermute | solution.py:361
  77.2 2.0 %collective-permute-start.9 = (bf16[256,704]{1,0:T(8,128)(2,1)S(1)}, bf16[256,704]{1,0:T(8,128)(2,1)S(1)}, u32[]{:S(2)}, u32[]{:S(2)}) collective-permute-start(bf16[256,704]{1,0:T(8,128)(2,1)S(1)} %slice.14.refs_5_), channel_id=1, source_target_pairs={{0,16},{16,0},{1,17},{17,1},{2,18},{18,2},{3,19},{19,3},{4,20},{20... | collective-permute-start | bytes 1081352 | tf_op jit(solution)/shard_map/ppermute | solution.py:361
  78.6 1.8 %collective-permute-start.6 = (bf16[256,704]{1,0:T(8,128)(2,1)S(1)}, bf16[256,704]{1,0:T(8,128)(2,1)S(1)}, u32[]{:S(2)}, u32[]{:S(2)}) collective-permute-start(bf16[256,704]{1,0:T(8,128)(2,1)S(1)} %get-tuple-element.37), channel_id=1, source_target_pairs={{0,16},{16,0},{1,17},{17,1},{2,18},{18,2},{3,19},{19,3},{4,20},{20... | collective-permute-start | bytes 1081352 | tf_op jit(solution)/shard_map/ppermute | solution.py:361
  78.9 2.0 %collective-permute-start.8 = (bf16[256,704]{1,0:T(8,128)(2,1)S(1)}, bf16[256,704]{1,0:T(8,128)(2,1)S(1)}, u32[]{:S(2)}, u32[]{:S(2)}) collective-permute-start(bf16[256,704]{1,0:T(8,128)(2,1)S(1)} %get-tuple-element.39), channel_id=1, source_target_pairs={{0,16},{16,0},{1,17},{17,1},{2,18},{18,2},{3,19},{19,3},{4,20},{20... | collective-permute-start | bytes 1081352 | tf_op jit(solution)/shard_map/ppermute | solution.py:361
  89.8 6.7 %copy-start.5 = (bf16[1,256,1408]{2,1,0:T(8,128)(2,1)S(1)}, bf16[1,256,1408]{2,1,0:T(8,128)(2,1)}, u32[]{:S(2)}) copy-start(bf16[1,256,1408]{2,1,0:T(8,128)(2,1)} %param.8) | copy-start | bytes 2162692
  89.8 36.5 %all-to-all-start.3 = ((bf16[64,16,1024]{2,1,0:T(8,128)(2,1)}), bf16[64,16,1024]{2,1,0:T(8,128)(2,1)S(1)}, u32[]{:S(2)}, u32[]{:S(2)}) async-start(bf16[64,16,1024]{2,1,0:T(8,128)(2,1)} %pack_shares.1), calls=%async_computation.3 | async-start | bytes 4194304 | tf_op jit(solution)/shard_map/all_to_all | solution.py:415
  96.5 2.7 %copy-start = (bf16[1408,2112]{0,1:T(8,128)(2,1)S(1)}, bf16[1408,2112]{0,1:T(8,128)(2,1)}, u32[]{:S(2)}) copy-start(bf16[1408,2112]{0,1:T(8,128)(2,1)} %param.12) | copy-start | bytes 17842180
  99.2 1.6 %copy-start.1 = (bf16[1408,704]{0,1:T(8,128)(2,1)S(1)}, bf16[1408,704]{0,1:T(8,128)(2,1)}, u32[]{:S(2)}) copy-start(bf16[1408,704]{0,1:T(8,128)(2,1)} %param.13) | copy-start | bytes 5947396
  100.7 1.2 copy-start.7
  102.0 1.2 copy-start.8

commit v8 on v6

--- a/solution.py
+++ b/solution.py
@@ -81,13 +81,14 @@
 
 def forward_kernel(temporal, *refs):
     if temporal:
-        stream_in, attend_in, projected_out, probs_out, mixed_out = refs[:5]
-        stream, attend, projected, probs, mixed, sems = refs[5:]
+        stream_in, attend_in, saved_out, mixed_out = refs[:4]
+        stream, attend, saved, mixed, sems = refs[4:]
     else:
-        stream_in, attend_in, output_in, projected_out, probs_out, result_out = refs[:6]
-        stream, attend, projected, probs, output, result, sems = refs[6:]
+        stream_in, attend_in, output_in, saved_out, result_out = refs[:5]
+        stream, attend, saved, output, result, sems = refs[5:]
         mixed = result.at[:, pl.ds(stream.shape[1], WIDE)]
-    width = stream.shape[1]
+    width, tokens = stream.shape[1], stream.shape[0]
+    projected = saved.at[:, pl.ds(HEADS * tokens, 3 * WIDE)]
 
     def copy(source, target, at):
         return pltpu.make_async_copy(source, target, sems.at[at])
@@ -108,9 +109,6 @@
     for part, (a, n) in zip(parts, ATTEND_CUTS):
         part.wait()
         projected[:, a : a + n] = dot_nt(normed, attend[a : a + n, :]).astype(jnp.bfloat16)
-    stores = [copy(projected, projected_out, 5)]
-    stores[0].start()
-    tokens = stream.shape[0]
     if temporal:
         allowed = same_patch(tokens)
     ahead = dot_nt(head(projected, 0, 0), head(projected, 1, 0))
@@ -122,12 +120,12 @@
             scores = jnp.where(allowed, scores, -jnp.inf)
         weights = jnp.exp(scores - jnp.max(scores, axis=-1, keepdims=True))
         chances = (weights / jnp.sum(weights, axis=-1, keepdims=True)).astype(jnp.bfloat16)
-        probs[h] = chances
+        saved[:, h * tokens : (h + 1) * tokens] = chances
         mixed[:, h * HEAD : (h + 1) * HEAD] = dot_nn(chances, head(projected, 2, h)).astype(
             jnp.bfloat16
         )
-    stores.append(copy(probs, probs_out, 7))
-    stores[1].start()
+    stores = [copy(saved, saved_out, 5)]
+    stores[0].start()
     if temporal:
         stores.append(copy(mixed, mixed_out, 6))
     else:
@@ -135,7 +133,7 @@
         branch = dot_nn(mixed[...], output[...])
         result[:, :width] = (stream[...].astype(jnp.float32) + branch).astype(jnp.bfloat16)
         stores.append(copy(result, result_out, 6))
-    stores[2].start()
+    stores[1].start()
     for store in stores:
         store.wait()
 
@@ -144,13 +142,13 @@
     temporal = output is None
     tokens, width = stream.shape[0], attend.shape[0]
     last = (tokens, WIDE) if temporal else (tokens, width + WIDE)
-    shapes = [(tokens, 3 * WIDE), (HEADS, tokens, tokens), last]
+    shapes = [(tokens, HEADS * tokens + 3 * WIDE), last]
     outs = [bf16(*shape) for shape in shapes]
     scratch = [held(tokens, width), held(3 * WIDE, width)] + [held(*shape) for shape in shapes]
     args = [stream, attend.T]
     if not temporal:
         args.append(output.T)
-        scratch.insert(4, held(WIDE, width))
+        scratch.insert(3, held(WIDE, width))
     scratch.append(pltpu.SemaphoreType.DMA((16,)))
     name = "time_forward" if temporal else "space_forward"
     spaces = "a" * (len(args) + len(outs))
@@ -158,8 +156,8 @@
 
 
 def backward_kernel(
-    grad_in, stream_in, projected_in, probs_in, attend_in, output_in, result_out,
-    grad, stream, projected, probs, attend, output, result, dproj, sems,
+    grad_in, stream_in, saved_in, attend_in, output_in, result_out,
+    grad, stream, saved, attend, output, result, dproj, sems,
 ):
     bf = jnp.bfloat16
 
@@ -167,18 +165,18 @@
         return pltpu.make_async_copy(source, target, sems.at[at])
 
     load_grad, load_output = copy(grad_in, grad, 0), copy(output_in, output, 1)
-    load_projected = copy(projected_in, projected, 2)
-    load_probs = copy(probs_in, probs, 7)
+    load_saved = copy(saved_in, saved, 2)
+    tokens = grad.shape[0]
+    projected = saved.at[:, pl.ds(HEADS * tokens, 3 * WIDE)]
     load_attend, load_stream = copy(attend_in, attend, 3), copy(stream_in.at[:, pl.ds(0, stream.shape[1])], stream, 4)
-    for load in (load_grad, load_output, load_projected, load_probs, load_attend, load_stream):
+    for load in (load_grad, load_output, load_saved, load_attend, load_stream):
         load.start()
     load_grad.wait()
     load_output.wait()
     dmixed = dot_nt(grad[...], output[...]).astype(bf)
-    load_projected.wait()
-    load_probs.wait()
+    load_saved.wait()
     for h in range(HEADS):
-        chances = probs[h]
+        chances = saved[:, h * tokens : (h + 1) * tokens]
         dm = dmixed[:, h * HEAD : (h + 1) * HEAD]
         dprobs = dot_nt(dm, head(projected, 2, h)).astype(bf).astype(jnp.float32)
         wide = chances.astype(jnp.float32)
@@ -208,11 +206,12 @@
     store.wait()
 
 
-def backward(grad, stream, projected, probs, attend, output, name, room):
-    args = [grad, stream, projected, probs, attend.T, output.T]
-    scratch = [held(*arg.shape) for arg in [grad, grad] + args[2:] + [grad, projected]]
+def backward(grad, stream, saved, attend, output, name, room):
+    args = [grad, stream, saved, attend.T, output.T]
+    scratch = [held(*arg.shape) for arg in [grad, grad] + args[2:] + [grad]]
+    scratch.append(held(grad.shape[0], 3 * WIDE))
     scratch.append(pltpu.SemaphoreType.DMA((16,)))
-    return call(backward_kernel, bf16(*grad.shape), args, name, "a" * 7, scratch, 2.6e9, room)
+    return call(backward_kernel, bf16(*grad.shape), args, name, "a" * 6, scratch, 2.6e9, room)
 
 
 def aim_kernel(counts_ref, targets_in, rows_in, keep_ref, next_ref, last_ref, targets, sems):
@@ -364,9 +363,9 @@
     far = [shift(from_last[144:], "z", 1), shift(from_next[144:], "z", chips - 1)]
 
     space_saved = forward(stream, attend_space, output_space)
-    hidden = exchange(space_saved[2], CLIP)
-
-    place = after(place, space_saved[2])
+    hidden = exchange(space_saved[1], CLIP)
+
+    place = after(place, space_saved[1])
     args = [place, keep, from_last, from_next, *far]
     cuts = 2
     outs = [bf16(tokens, width)] + [bf16(tokens // cuts, width)] * cuts
@@ -375,10 +374,10 @@
     grad_out = call(join_kernel, bf16(tokens, width), args, "join_rows", "v" * (cuts + 2))
     grad = exchange(grad_out, CLIP)
     time_saved = forward(hidden, attend_time)
-    time_mixed, space_mixed = time_saved[2], hidden[:, width:]
+    time_mixed, space_mixed = time_saved[1], hidden[:, width:]
     time_mixed_got, space_mixed_got = shift(time_mixed, "core", 1), shift(space_mixed, "core", 1)
     grad_hidden = backward(
-        grad, hidden, time_saved[0], time_saved[1], attend_time, output_time, "time_backward", 60
+        grad, hidden, time_saved[0], attend_time, output_time, "time_backward", 60
     )
     half = bf16(tokens, width // 2)
     time_mine, time_other, space_mine, space_other = call(
@@ -397,7 +396,7 @@
     share = jax.ShapeDtypeStruct((SHARE, WIDE), jnp.float32)
     space_grad, time_grad = call(unpack_kernel, [share, share], [packed], "sum_shares", "vvv")
     token_grad = backward(
-        grad_hidden, stream, space_saved[0], space_saved[1], attend_space, output_space, "space_backward", 40
+        grad_hidden, stream, space_saved[0], attend_space, output_space, "space_backward", 40
     )
     return (token_grad[None], space_grad, time_grad)
 

time: 127 us -> 127 us (level)
    unnamed x20 -> x18, local copies, waits for them, and re-layouts: 7.58 us -> 6.72 us
  transfers between devices with their start and end apart: 14 -> 14, of which waited for: 9 -> 9; matrix products, arithmetic and copies ran while one was open for 1% -> 1% of each run, Pallas kernels for 26% -> 27%
where the time goes in v8:
time: 127 us
  Pallas kernels  48 us (38%)
  waiting for transfers between devices  38.5 us (30%)
  starting transfers between devices  31.4 us (25%)
  local copies, waits for them, and re-layouts  7.78 us (6%)
    pallas_call x10, Pallas kernels, call(): pl.pallas_call(kernel, out_shape=outs, in_specs=spaces[:len(args)], out_s...  48 us
    all_to_all x3, waiting for transfers between devices, exchange(): lax.all_to_all(cut, axes, split_axis=0, concat_axis=0, tiled=True)  15.9 us
    all_to_all x3, starting transfers between devices, exchange(): lax.all_to_all(cut, axes, split_axis=0, concat_axis=0, tiled=True)  15.7 us
    all_to_all x1, waiting for transfers between devices, body(): lax.all_to_all(packed, ('z', 'space'), split_axis=0, concat_axis=0, tiled...  13.7 us
    ppermute x10, starting transfers between devices, shift(): lax.ppermute(array, axis, [(i, (i + by) % devices) for i in range(devices)])  9.45 us
    ppermute x10, waiting for transfers between devices, shift(): lax.ppermute(array, axis, [(i, (i + by) % devices) for i in range(devices)])  8.9 us
    unnamed x18, local copies, waits for them, and re-layouts  6.72 us
    all_to_all x1, starting transfers between devices, body(): lax.all_to_all(packed, ('z', 'space'), split_axis=0, concat_axis=0, tiled...  6.26 us
  transfers between devices with their start and end apart: 14, of which 9 were waited for; matrix products, arithmetic and copies ran while one was open for 1% of the time, Pallas kernels for 27%

profile of v8, /device:TPU:0, one launch (start us, length us, event | category | flops | bytes accessed | tf_op | source)
XLA Modules:
  0.0 126.7 jit_solution(18143818025159910764)
XLA Ops:
  0.6 3.2 %aim_rows.1 = (bf16[144,1408]{1,0:T(8,128)(2,1)}, bf16[224,1408]{1,0:T(8,128)(2,1)}, bf16[224,1408]{1,0:T(8,128)(2,1)}) custom-call(s32[1,1,8]{2,1,0:T(1,128)} %counts_ref.1, s32[1,1,8,64]{3,2,1,0:T(8,128)} %targets_in.1, bf16[4,128,1408]{2,1,0:T(8,128)(2,1)} %bitcast.28), custom_call_target="tpu_custom_call" | custom-call | flops 1000000 | bytes 5000 | tf_op jit(solution)/shard_map/aim_rows/pallas_call | solution.py:36
  3.8 2.1 %collective-permute-start = (bf16[224,1408]{1,0:T(8,128)(2,1)}, bf16[224,1408]{1,0:T(8,128)(2,1)S(1)}, u32[]{:S(2)}, u32[]{:S(2)}) collective-permute-start(bf16[224,1408]{1,0:T(8,128)(2,1)} %get-tuple-element.24), channel_id=1, source_target_pairs={{0,32},{32,64},{64,96},{96,0},{1,33},{33,65},{65,97},{97,1},{2,34}... | collective-permute-start | bytes 1892360 | tf_op jit(solution)/shard_map/ppermute | solution.py:343
  5.9 2.2 %collective-permute-start.1 = (bf16[224,1408]{1,0:T(8,128)(2,1)}, bf16[224,1408]{1,0:T(8,128)(2,1)S(1)}, u32[]{:S(2)}, u32[]{:S(2)}) collective-permute-start(bf16[224,1408]{1,0:T(8,128)(2,1)} %get-tuple-element.25), channel_id=1, source_target_pairs={{0,96},{32,0},{64,32},{96,64},{1,97},{33,1},{65,33},{97,65},{2,98}... | collective-permute-start | bytes 1892360 | tf_op jit(solution)/shard_map/ppermute | solution.py:343
  8.1 8.6 %space_forward.1 = (bf16[256,4160]{1,0:T(8,128)(2,1)}, bf16[256,2112]{1,0:T(8,128)(2,1)}) custom-call(bf16[256,1408]{1,0:T(8,128)(2,1)} %bitcast.23, bf16[2112,1408]{1,0:T(8,128)(2,1)} %bitcast.15, bf16[704,1408]{1,0:T(8,128)(2,1)} %bitcast.17), custom_call_target="tpu_custom_call" | custom-call | flops 2200000000 | bytes 11000000 | tf_op jit(solution)/shard_map/space_forward/pallas_call | solution.py:36
  16.7 7.6 %all-to-all-start.1 = ((bf16[32,8,2112]{2,1,0:T(8,128)(2,1)}), bf16[32,8,2112]{2,1,0:T(8,128)(2,1)}, u32[]{:S(2)}, u32[]{:S(2)}) async-start(bf16[32,8,2112]{2,1,0:T(8,128)(2,1)} %bitcast.29), calls=%async_computation.1 | async-start | bytes 2228224 | tf_op jit(solution)/shard_map/all_to_all | solution.py:338
  24.4 3.3 %collective-permute-start.3 = (bf16[80,1408]{1,0:T(8,128)(2,1)S(1)}, bf16[80,1408]{1,0:T(8,128)(2,1)S(1)}, u32[]{:S(2)}, u32[]{:S(2)}) collective-permute-start(bf16[80,1408]{1,0:T(8,128)(2,1)S(1)} %slice.13), channel_id=1, source_target_pairs={{0,96},{32,0},{64,32},{96,64},{1,97},{33,1},{65,33},{97,65},{2,98}... | collective-permute-start | bytes 675848 | tf_op jit(solution)/shard_map/ppermute | solution.py:343
  27.8 5.4 %collective-permute-done.2.far0_ref = bf16[80,1408]{1,0:T(8,128)(2,1)S(1)} collective-permute-done((bf16[80,1408]{1,0:T(8,128)(2,1)S(1)}, bf16[80,1408]{1,0:T(8,128)(2,1)S(1)}, u32[]{:S(2)}, u32[]{:S(2)}) %collective-permute-start.2) | collective-permute-done | bytes 225312 | tf_op jit(solution)/shard_map/ppermute | solution.py:343
  33.2 2.2 %scatter_rows.1 = (bf16[256,1408]{1,0:T(8,128)(2,1)S(1)}, bf16[128,1408]{1,0:T(8,128)(2,1)S(1)}, bf16[128,1408]{1,0:T(8,128)(2,1)S(1)}) custom-call(s32[2]{0:T(128)S(1)} %pad_add_fusion.place_ref.refs_0_, bf16[144,1408]{1,0:T(8,128)(2,1)S(1)} %copy-done.7, bf16[224,1408]{1,0:T(8,128)(2,1)S(1)} %collective-permute-done.next_ref, ...), custom_call_target="tpu_custom_call" | custom-call | flops 1000000 | bytes 5000 | tf_op jit(solution)/shard_map/scatter_rows/pallas_call | solution.py:36
  35.5 0.5 collective-permute-start.5
  36.0 1.2 collective-permute-done.4.refs_0_
  37.2 0.5 collective-permute-done.5.refs_1_
  37.7 0.9 join_rows.1
  38.6 3.8 %all-to-all-done.1 = bf16[32,8,2112]{2,1,0:T(8,128)(2,1)} async-done(((bf16[32,8,2112]{2,1,0:T(8,128)(2,1)}), bf16[32,8,2112]{2,1,0:T(8,128)(2,1)}, u32[]{:S(2)}, u32[]{:S(2)}) %all-to-all-start.1) | async-done | bytes 1081376 | tf_op jit(solution)/shard_map/all_to_all | solution.py:338
  42.4 4.1 %all-to-all-start = ((bf16[32,8,1408]{2,1,0:T(8,128)(2,1)}), bf16[32,8,1408]{2,1,0:T(8,128)(2,1)S(1)}, u32[]{:S(2)}, u32[]{:S(2)}) async-start(bf16[32,8,1408]{2,1,0:T(8,128)(2,1)} %bitcast.6), calls=%async_computation | async-start | bytes 1441792 | tf_op jit(solution)/shard_map/all_to_all | solution.py:338
  46.5 7.9 %time_forward.1 = (bf16[256,4160]{1,0:T(8,128)(2,1)}, bf16[256,704]{1,0:T(8,128)(2,1)}) custom-call(bf16[256,2112]{1,0:T(8,128)(2,1)} %bitcast.9.refs_0_.stream_in, bf16[2112,1408]{1,0:T(8,128)(2,1)} %bitcast.25), custom_call_target="tpu_custom_call" | custom-call | flops 2200000000 | bytes 11000000 | tf_op jit(solution)/shard_map/time_forward/pallas_call | solution.py:36
  54.4 5.9 %all-to-all-done = bf16[32,8,1408]{2,1,0:T(8,128)(2,1)S(1)} async-done(((bf16[32,8,1408]{2,1,0:T(8,128)(2,1)}), bf16[32,8,1408]{2,1,0:T(8,128)(2,1)S(1)}, u32[]{:S(2)}, u32[]{:S(2)}) %all-to-all-start) | async-done | bytes 720928 | tf_op jit(solution)/shard_map/all_to_all | solution.py:338
  60.3 0.9 copy-done.3
  61.2 10.3 %time_backward.1.refs_2_ = bf16[256,1408]{1,0:T(8,128)(2,1)} custom-call(bf16[256,1408]{1,0:T(8,128)(2,1)} %bitcast.20, bf16[256,2112]{1,0:T(8,128)(2,1)} %bitcast.9.refs_0_.stream_in, bf16[256,4160]{1,0:T(8,128)(2,1)} %get-tuple-element.29.saved_in, bf16[2112,1408]{1,0:T(8,128)(2,1)} %bitcast.26, bf16[704,1408]{1,0:T(8,128)(2,1)} %bitcast.27), custom_call_target="tpu_custom_call" | custom-call | flops 2600000000 | bytes 13000000 | tf_op jit(solution)/shard_map/time_backward/pallas_call | solution.py:36
  71.5 4.0 %all-to-all-start.2 = ((bf16[32,8,1408]{2,1,0:T(8,128)(2,1)}), bf16[32,8,1408]{2,1,0:T(8,128)(2,1)S(1)}, u32[]{:S(2)}, u32[]{:S(2)}) async-start(bf16[32,8,1408]{2,1,0:T(8,128)(2,1)} %bitcast.19), calls=%async_computation.2 | async-start | bytes 1441792 | tf_op jit(solution)/shard_map/all_to_all | solution.py:338
  75.6 1.0 slice.14.refs_5_
  77.3 1.1 split_features.1
  79.0 1.2 collective-permute-done.6.refs_2_
  80.1 0.6 collective-permute-done.8.refs_6_
  80.7 2.7 %pack_shares.1 = bf16[64,16,1024]{2,1,0:T(8,128)(2,1)} custom-call(bf16[256,704]{1,0:T(8,128)(2,1)S(1)} %get-tuple-element.31.refs_0_, bf16[256,704]{1,0:T(8,128)(2,1)S(1)} %copy-done.8, bf16[256,704]{1,0:T(8,128)(2,1)S(1)} %collective-permute-done.6.refs_2_, bf16[256,704]{1,0:T(8,128)(2,1)S(1)} %collective-permute-done.7.refs_3_, ...), custom_call_target="tpu_custom_call" | custom-call | flops 1000000 | bytes 5000 | tf_op jit(solution)/shard_map/pack_shares/pallas_call | solution.py:36
  83.4 6.2 %all-to-all-done.2 = bf16[32,8,1408]{2,1,0:T(8,128)(2,1)S(1)} async-done(((bf16[32,8,1408]{2,1,0:T(8,128)(2,1)}), bf16[32,8,1408]{2,1,0:T(8,128)(2,1)S(1)}, u32[]{:S(2)}, u32[]{:S(2)}) %all-to-all-start.2) | async-done | bytes 720928 | tf_op jit(solution)/shard_map/all_to_all | solution.py:338
  89.6 6.3 %all-to-all-start.3 = ((bf16[64,16,1024]{2,1,0:T(8,128)(2,1)}), bf16[64,16,1024]{2,1,0:T(8,128)(2,1)S(1)}, u32[]{:S(2)}, u32[]{:S(2)}) async-start(bf16[64,16,1024]{2,1,0:T(8,128)(2,1)} %pack_shares.1), calls=%async_computation.3 | async-start | bytes 4194304 | tf_op jit(solution)/shard_map/all_to_all | solution.py:395
  95.9 2.7 %copy-done = bf16[1408,2112]{0,1:T(8,128)(2,1)S(1)} copy-done((bf16[1408,2112]{0,1:T(8,128)(2,1)S(1)}, bf16[1408,2112]{0,1:T(8,128)(2,1)}, u32[]{:S(2)}) %copy-start) | copy-done | bytes 5947416
  98.6 1.5 %copy-done.1 = bf16[1408,704]{0,1:T(8,128)(2,1)S(1)} copy-done((bf16[1408,704]{0,1:T(8,128)(2,1)S(1)}, bf16[1408,704]{0,1:T(8,128)(2,1)}, u32[]{:S(2)}) %copy-start.1) | copy-done | bytes 1982488
  100.1 1.6 %copy-done.6 = bf16[256,4160]{1,0:T(8,128)(2,1)S(1)} copy-done((bf16[256,4160]{1,0:T(8,128)(2,1)S(1)}, bf16[256,4160]{1,0:T(8,128)(2,1)}, u32[]{:S(2)}) %copy-start.6) | copy-done | bytes 2129944
  101.7 10.2 %space_backward.1 = bf16[256,1408]{1,0:T(8,128)(2,1)} custom-call(bf16[256,1408]{1,0:T(8,128)(2,1)S(1)} %bitcast.22, bf16[256,1408]{1,0:T(8,128)(2,1)S(1)} %bitcast.24, bf16[256,4160]{1,0:T(8,128)(2,1)S(1)} %copy-done.6, bf16[2112,1408]{1,0:T(8,128)(2,1)S(1)} %bitcast.16, bf16[704,1408]{1,0:T(8,128)(2,1)S(1)} %bitcast.18), custom_call_target="tpu_custom_call" | custom-call | flops 2600000000 | bytes 13000000 | tf_op jit(solution)/shard_map/space_backward/pallas_call | solution.py:36
  112.0 13.7 %all-to-all-done.3.parts_ref = bf16[64,16,1024]{2,1,0:T(8,128)(2,1)S(1)} async-done(((bf16[64,16,1024]{2,1,0:T(8,128)(2,1)}), bf16[64,16,1024]{2,1,0:T(8,128)(2,1)S(1)}, u32[]{:S(2)}, u32[]{:S(2)}) %all-to-all-start.3) | async-done | bytes 2097184 | tf_op jit(solution)/shard_map/all_to_all | solution.py:395
  125.7 1.0 sum_shares.1
  (28 shorter events, 1.6 us)
Async XLA Ops:
  3.8 20.4 %collective-permute-start = (bf16[224,1408]{1,0:T(8,128)(2,1)}, bf16[224,1408]{1,0:T(8,128)(2,1)S(1)}, u32[]{:S(2)}, u32[]{:S(2)}) collective-permute-start(bf16[224,1408]{1,0:T(8,128)(2,1)} %get-tuple-element.24), channel_id=1, source_target_pairs={{0,32},{32,64},{64,96},{96,0},{1,33},{33,65},{65,97},{97,1},{2,34}... | collective-permute-start | bytes 1892360 | tf_op jit(solution)/shard_map/ppermute | solution.py:343
  5.9 18.5 %collective-permute-start.1 = (bf16[224,1408]{1,0:T(8,128)(2,1)}, bf16[224,1408]{1,0:T(8,128)(2,1)S(1)}, u32[]{:S(2)}, u32[]{:S(2)}) collective-permute-start(bf16[224,1408]{1,0:T(8,128)(2,1)} %get-tuple-element.25), channel_id=1, source_target_pairs={{0,96},{32,0},{64,32},{96,64},{1,97},{33,1},{65,33},{97,65},{2,98}... | collective-permute-start | bytes 1892360 | tf_op jit(solution)/shard_map/ppermute | solution.py:343
  16.7 16.6 %copy-start.7 = (bf16[144,1408]{1,0:T(8,128)(2,1)S(1)}, bf16[144,1408]{1,0:T(8,128)(2,1)}, u32[]{:S(2)}) copy-start(bf16[144,1408]{1,0:T(8,128)(2,1)} %get-tuple-element.23.keep_ref) | copy-start | bytes 1216516
  16.7 25.7 %all-to-all-start.1 = ((bf16[32,8,2112]{2,1,0:T(8,128)(2,1)}), bf16[32,8,2112]{2,1,0:T(8,128)(2,1)}, u32[]{:S(2)}, u32[]{:S(2)}) async-start(bf16[32,8,2112]{2,1,0:T(8,128)(2,1)} %bitcast.29), calls=%async_computation.1 | async-start | bytes 2228224 | tf_op jit(solution)/shard_map/all_to_all | solution.py:338
  24.3 8.9 %collective-permute-start.2 = (bf16[80,1408]{1,0:T(8,128)(2,1)S(1)}, bf16[80,1408]{1,0:T(8,128)(2,1)S(1)}, u32[]{:S(2)}, u32[]{:S(2)}) collective-permute-start(bf16[80,1408]{1,0:T(8,128)(2,1)S(1)} %slice.12), channel_id=1, source_target_pairs={{0,32},{32,64},{64,96},{96,0},{1,33},{33,65},{65,97},{97,1},{2,34}... | collective-permute-start | bytes 675848 | tf_op jit(solution)/shard_map/ppermute | solution.py:343
  24.4 8.8 %collective-permute-start.3 = (bf16[80,1408]{1,0:T(8,128)(2,1)S(1)}, bf16[80,1408]{1,0:T(8,128)(2,1)S(1)}, u32[]{:S(2)}, u32[]{:S(2)}) collective-permute-start(bf16[80,1408]{1,0:T(8,128)(2,1)S(1)} %slice.13), channel_id=1, source_target_pairs={{0,96},{32,0},{64,32},{96,64},{1,97},{33,1},{65,33},{97,65},{2,98}... | collective-permute-start | bytes 675848 | tf_op jit(solution)/shard_map/ppermute | solution.py:343
  35.4 1.8 %collective-permute-start.4 = (bf16[128,1408]{1,0:T(8,128)(2,1)S(1)}, bf16[128,1408]{1,0:T(8,128)(2,1)S(1)}, u32[]{:S(2)}, u32[]{:S(2)}) collective-permute-start(bf16[128,1408]{1,0:T(8,128)(2,1)S(1)} %get-tuple-element.27), channel_id=1, source_target_pairs={{0,16},{16,0},{1,17},{17,1},{2,18},{18,2},{3,19},{19,3},{4,20},{20... | collective-permute-start | bytes 1081352 | tf_op jit(solution)/shard_map/ppermute | solution.py:343
  35.5 2.2 %collective-permute-start.5 = (bf16[128,1408]{1,0:T(8,128)(2,1)S(1)}, bf16[128,1408]{1,0:T(8,128)(2,1)S(1)}, u32[]{:S(2)}, u32[]{:S(2)}) collective-permute-start(bf16[128,1408]{1,0:T(8,128)(2,1)S(1)} %get-tuple-element.28), channel_id=1, source_target_pairs={{0,16},{16,0},{1,17},{17,1},{2,18},{18,2},{3,19},{19,3},{4,20},{20... | collective-permute-start | bytes 1081352 | tf_op jit(solution)/shard_map/ppermute | solution.py:343
  42.4 17.9 %all-to-all-start = ((bf16[32,8,1408]{2,1,0:T(8,128)(2,1)}), bf16[32,8,1408]{2,1,0:T(8,128)(2,1)S(1)}, u32[]{:S(2)}, u32[]{:S(2)}) async-start(bf16[32,8,1408]{2,1,0:T(8,128)(2,1)} %bitcast.6), calls=%async_computation | async-start | bytes 1441792 | tf_op jit(solution)/shard_map/all_to_all | solution.py:338
  60.3 0.9 copy-start.3
  71.5 5.1 %copy-start.8 = (bf16[256,704]{1,0:T(8,128)(2,1)S(1)}, bf16[256,704]{1,0:T(8,128)(2,1)}, u32[]{:S(2)}) copy-start(bf16[256,704]{1,0:T(8,128)(2,1)} %get-tuple-element.32.refs_1_) | copy-start | bytes 1081348
  71.5 5.8 %copy-start.2 = (bf16[256,1408]{1,0:T(8,128)(2,1)S(1)}, bf16[256,1408]{1,0:T(8,128)(2,1)}, u32[]{:S(2)}) copy-start(bf16[256,1408]{1,0:T(8,128)(2,1)} %time_backward.1.refs_2_) | copy-start | bytes 2162692
  71.5 5.8 %copy-start.4 = (bf16[32,8,1408]{2,1,0:T(8,128)(2,1)S(1)}, bf16[32,8,1408]{2,1,0:T(8,128)(2,1)}, u32[]{:S(2)}) copy-start(bf16[32,8,1408]{2,1,0:T(8,128)(2,1)} %copy-done.3) | copy-start | bytes 2162692
  71.5 18.1 %all-to-all-start.2 = ((bf16[32,8,1408]{2,1,0:T(8,128)(2,1)}), bf16[32,8,1408]{2,1,0:T(8,128)(2,1)S(1)}, u32[]{:S(2)}, u32[]{:S(2)}) async-start(bf16[32,8,1408]{2,1,0:T(8,128)(2,1)} %bitcast.19), calls=%async_computation.2 | async-start | bytes 1441792 | tf_op jit(solution)/shard_map/all_to_all | solution.py:338
  76.6 2.3 %collective-permute-start.7 = (bf16[256,704]{1,0:T(8,128)(2,1)S(1)}, bf16[256,704]{1,0:T(8,128)(2,1)S(1)}, u32[]{:S(2)}, u32[]{:S(2)}) collective-permute-start(bf16[256,704]{1,0:T(8,128)(2,1)S(1)} %copy-done.8), channel_id=1, source_target_pairs={{0,16},{16,0},{1,17},{17,1},{2,18},{18,2},{3,19},{19,3},{4,20},{20... | collective-permute-start | bytes 1081352 | tf_op jit(solution)/shard_map/ppermute | solution.py:343
  77.0 2.0 %collective-permute-start.9 = (bf16[256,704]{1,0:T(8,128)(2,1)S(1)}, bf16[256,704]{1,0:T(8,128)(2,1)S(1)}, u32[]{:S(2)}, u32[]{:S(2)}) collective-permute-start(bf16[256,704]{1,0:T(8,128)(2,1)S(1)} %slice.14.refs_5_), channel_id=1, source_target_pairs={{0,16},{16,0},{1,17},{17,1},{2,18},{18,2},{3,19},{19,3},{4,20},{20... | collective-permute-start | bytes 1081352 | tf_op jit(solution)/shard_map/ppermute | solution.py:343
  78.3 1.8 %collective-permute-start.6 = (bf16[256,704]{1,0:T(8,128)(2,1)S(1)}, bf16[256,704]{1,0:T(8,128)(2,1)S(1)}, u32[]{:S(2)}, u32[]{:S(2)}) collective-permute-start(bf16[256,704]{1,0:T(8,128)(2,1)S(1)} %get-tuple-element.33), channel_id=1, source_target_pairs={{0,16},{16,0},{1,17},{17,1},{2,18},{18,2},{3,19},{19,3},{4,20},{20... | collective-permute-start | bytes 1081352 | tf_op jit(solution)/shard_map/ppermute | solution.py:343
  78.7 2.0 %collective-permute-start.8 = (bf16[256,704]{1,0:T(8,128)(2,1)S(1)}, bf16[256,704]{1,0:T(8,128)(2,1)S(1)}, u32[]{:S(2)}, u32[]{:S(2)}) collective-permute-start(bf16[256,704]{1,0:T(8,128)(2,1)S(1)} %get-tuple-element.35), channel_id=1, source_target_pairs={{0,16},{16,0},{1,17},{17,1},{2,18},{18,2},{3,19},{19,3},{4,20},{20... | collective-permute-start | bytes 1081352 | tf_op jit(solution)/shard_map/ppermute | solution.py:343
  89.6 6.3 %copy-start.5 = (bf16[1,256,1408]{2,1,0:T(8,128)(2,1)S(1)}, bf16[1,256,1408]{2,1,0:T(8,128)(2,1)}, u32[]{:S(2)}) copy-start(bf16[1,256,1408]{2,1,0:T(8,128)(2,1)} %param.8) | copy-start | bytes 2162692
  89.6 36.1 %all-to-all-start.3 = ((bf16[64,16,1024]{2,1,0:T(8,128)(2,1)}), bf16[64,16,1024]{2,1,0:T(8,128)(2,1)S(1)}, u32[]{:S(2)}, u32[]{:S(2)}) async-start(bf16[64,16,1024]{2,1,0:T(8,128)(2,1)} %pack_shares.1), calls=%async_computation.3 | async-start | bytes 4194304 | tf_op jit(solution)/shard_map/all_to_all | solution.py:395
  95.9 2.7 %copy-start = (bf16[1408,2112]{0,1:T(8,128)(2,1)S(1)}, bf16[1408,2112]{0,1:T(8,128)(2,1)}, u32[]{:S(2)}) copy-start(bf16[1408,2112]{0,1:T(8,128)(2,1)} %param.12) | copy-start | bytes 17842180
  98.6 1.6 %copy-start.1 = (bf16[1408,704]{0,1:T(8,128)(2,1)S(1)}, bf16[1408,704]{0,1:T(8,128)(2,1)}, u32[]{:S(2)}) copy-start(bf16[1408,704]{0,1:T(8,128)(2,1)} %param.13) | copy-start | bytes 5947396
  100.1 1.6 %copy-start.6 = (bf16[256,4160]{1,0:T(8,128)(2,1)S(1)}, bf16[256,4160]{1,0:T(8,128)(2,1)}, u32[]{:S(2)}) copy-start(bf16[256,4160]{1,0:T(8,128)(2,1)} %get-tuple-element.30.saved_in) | copy-start | bytes 6389764
